TPU v7x, 32 devices: a whole 2x2x4 slice. The times are simulated.
32 devices in a mesh: batch: 4 (over y, x), tensor: 8 (over z, core).
Axes of the slice: x: 2, y: 2, z: 4, core: 2. Of those that a mesh axis runs over, the one named last changes fastest.
Arguments:
- tokens: bfloat16 [2048, 2048], P('batch', 'tensor'), may hold values from -6 to 6
- captions: bfloat16 [1024, 4096], P('batch', 'tensor'), may hold values from -6 to 6
- mask_counts: int32 [8], P('batch'), may hold values from 1 to 256, as said below
- mask_positions: int32 [8, 256], P('batch'), may hold values from 0 to 255, each once within a row
- cotangent: bfloat16 [2048, 2048], P('batch', 'tensor'), may hold values from -6 to 6
- mask_embed: bfloat16 [2048], P('tensor'), may hold values from -6 to 6
- position_embed: bfloat16 [256, 2048], P(None, 'tensor'), may hold values from -3 to 3
- norm_self: bfloat16 [2048], P('tensor'), may hold values from 0.099609375 to 1.8984375
- query_self: bfloat16 [2048, 2048], P(None, 'tensor'), may hold values from -0.125 to 0.125
- key_self: bfloat16 [2048, 2048], P(None, 'tensor'), may hold values from -0.125 to 0.125
- value_self: bfloat16 [2048, 2048], P(None, 'tensor'), may hold values from -0.125 to 0.125
- out_self: bfloat16 [2048, 2048], P('tensor'), may hold values from -1.25 to 1.25
- norm_cross: bfloat16 [2048], P('tensor'), may hold values from 0.099609375 to 1.8984375
- query_cross: bfloat16 [2048, 2048], P(None, 'tensor'), may hold values from -0.125 to 0.125
- key_text: bfloat16 [4096, 2048], P(None, 'tensor'), may hold values from -0.09375 to 0.09375
- value_text: bfloat16 [4096, 2048], P(None, 'tensor'), may hold values from -0.09375 to 0.09375
- out_cross: bfloat16 [2048, 2048], P('tensor'), may hold values from -0.875 to 0.875
- norm_feed: bfloat16 [2048], P('tensor'), may hold values from 0.099609375 to 1.8984375
- up_weight: bfloat16 [2048, 8192], P(None, 'tensor'), may hold values from -0.125 to 0.125
- down_weight: bfloat16 [8192, 2048], P('tensor'), may hold values from -0.0625 to 0.0625
Outputs:
- layer_out: bfloat16 [2048, 2048], P('batch', 'tensor')
- tokens_grad: bfloat16 [2048, 2048], P('batch', 'tensor')
- captions_grad: bfloat16 [1024, 4096], P('batch', 'tensor')
- mask_embed_grad: float32 [2048], P('tensor')
- position_embed_grad: float32 [256, 2048], P(None, 'tensor')
- norm_self_grad: float32 [2048], P('tensor')
- query_self_grad: float32 [2048, 2048], P(None, 'tensor')
- key_self_grad: float32 [2048, 2048], P(None, 'tensor')
- value_self_grad: float32 [2048, 2048], P(None, 'tensor')
- out_self_grad: float32 [2048, 2048], P('tensor')
- norm_cross_grad: float32 [2048], P('tensor')
- query_cross_grad: float32 [2048, 2048], P(None, 'tensor')
- key_text_grad: float32 [4096, 2048], P(None, 'tensor')
- value_text_grad: float32 [4096, 2048], P(None, 'tensor')
- out_cross_grad: float32 [2048, 2048], P('tensor')
- norm_feed_grad: float32 [2048], P('tensor')
- up_weight_grad: float32 [2048, 8192], P(None, 'tensor')
- down_weight_grad: float32 [8192, 2048], P('tensor')
Inputs may be any that keep to these rules, and one draw needn't show every extreme that they name: `mask_counts`: every draw has an image with all 256 tokens masked and one with a single masked token; counts are skewed towards few masked tokens. `mask_positions`: each row holds every position of the image once.
All inputs are finite; a program needn't handle non-finite values.
Results may differ from a plain program's by a relative error of at most 0.025.
Values may be sent and summed in bfloat16 or wider, within the bound.
No kernel may reach another device: no remote copies, remote signals or barrier semaphores. Data moves between devices by JAX's collectives and lax.ppermute only.
A program may use at most 192 MiB of HBM per device.

v0:
```python
import jax
import jax.numpy as jnp
from jax import lax
from jax.sharding import PartitionSpec as P

HEAD_DIM = 128
IMG_LEN = 256


EPS = 1e-06


def contract(left, right, left_dim, right_dim):
    return lax.dot_general(
        left, right, (((left_dim,), (right_dim,)), ((), ())), preferred_element_type=jnp.float32
    )


def mask_table(counts, positions):
    slot_ids = jnp.arange(positions.shape[1], dtype=jnp.int32)
    active = slot_ids[None, :] < counts[:, None]
    matched = (positions[:, :, None] == slot_ids[None, None, :]) & active[:, :, None]
    return jnp.any(matched, axis=1)


def gelu_tanh(values):
    return (
        0.5
        * values
        * (1.0 + jnp.tanh(0.7978845608028654 * (values + 0.044715 * values * values * values)))
    )


def split_heads(array, images):
    return array.reshape(images, array.shape[0] // images, array.shape[1] // HEAD_DIM, HEAD_DIM)


def norm_forward(stream, gain_vec):
    full_width = stream.shape[1] * lax.axis_size("tensor")
    row_sums, row_squares = lax.psum(
        (jnp.sum(stream, axis=1), jnp.sum(stream * stream, axis=1)), "tensor"
    )
    row_mean = row_sums / full_width
    inv_std = lax.rsqrt(row_squares / full_width - row_mean * row_mean + EPS)
    normal = (stream - row_mean[:, None]) * inv_std[:, None]
    normed = (normal * gain_vec.astype(jnp.float32)[None, :]).astype(jnp.bfloat16)
    gathered = lax.all_gather(normed, "tensor", axis=1, tiled=True)
    return (gathered, normal, inv_std)


def norm_backward(partial_grad, normal, inv_std, gain_vec):
    normed_grad = lax.psum_scatter(
        partial_grad.astype(jnp.bfloat16), "tensor", scatter_dimension=1, tiled=True
    ).astype(jnp.float32)
    full_width = normed_grad.shape[1] * lax.axis_size("tensor")
    scaled = normed_grad * gain_vec.astype(jnp.float32)[None, :]
    first_sum, second_sum = lax.psum(
        (jnp.sum(scaled, axis=1), jnp.sum(scaled * normal, axis=1)), "tensor"
    )
    stream_grad = inv_std[:, None] * (
        scaled - first_sum[:, None] / full_width - normal * (second_sum[:, None] / full_width)
    )
    gain_grad = jnp.sum(normed_grad * normal, axis=0)
    return (stream_grad, gain_grad)


def branch_seed(stream_grad):
    return lax.all_gather(stream_grad.astype(jnp.bfloat16), "tensor", axis=1, tiled=True)


def project_out(mixed_rows, out_weight):
    partial_out = contract(mixed_rows, out_weight, 1, 0)
    return lax.psum_scatter(partial_out, "tensor", scatter_dimension=1, tiled=True)


def attend_forward(query_rows, key_rows, value_rows, images):
    inv_root = float(HEAD_DIM) ** (-0.5)
    q_heads = split_heads(query_rows, images)
    k_heads = split_heads(key_rows, images)
    v_heads = split_heads(value_rows, images)
    scores = (
        jnp.einsum("bqhd,bkhd->bhqk", q_heads, k_heads, preferred_element_type=jnp.float32)
        * inv_root
    )
    row_max = jnp.max(scores, axis=-1, keepdims=True)
    exp_terms = jnp.exp(scores - row_max)
    attn_probs = exp_terms / jnp.sum(exp_terms, axis=-1, keepdims=True)
    probs_low = attn_probs.astype(jnp.bfloat16)
    mixed = jnp.einsum("bhqk,bkhd->bqhd", probs_low, v_heads, preferred_element_type=jnp.float32)
    return (mixed.astype(jnp.bfloat16).reshape(query_rows.shape), attn_probs, probs_low)


def attend_backward(mixed_grad, query_rows, key_rows, value_rows, attn_probs, probs_low, images):
    inv_root = float(HEAD_DIM) ** (-0.5)
    q_heads = split_heads(query_rows, images)
    k_heads = split_heads(key_rows, images)
    v_heads = split_heads(value_rows, images)
    g_heads = split_heads(mixed_grad, images)
    prob_grad = jnp.einsum("bqhd,bkhd->bhqk", g_heads, v_heads, preferred_element_type=jnp.float32)
    inner = jnp.sum(attn_probs * prob_grad, axis=-1, keepdims=True)
    score_grad = (attn_probs * (prob_grad - inner)).astype(jnp.bfloat16)
    query_grad = (
        jnp.einsum("bhqk,bkhd->bqhd", score_grad, k_heads, preferred_element_type=jnp.float32)
        * inv_root
    )
    key_grad = (
        jnp.einsum("bhqk,bqhd->bkhd", score_grad, q_heads, preferred_element_type=jnp.float32)
        * inv_root
    )
    value_grad = jnp.einsum(
        "bhqk,bqhd->bkhd", probs_low, g_heads, preferred_element_type=jnp.float32
    )
    return (
        query_grad.astype(jnp.bfloat16).reshape(query_rows.shape),
        key_grad.astype(jnp.bfloat16).reshape(key_rows.shape),
        value_grad.astype(jnp.bfloat16).reshape(value_rows.shape),
    )


def layer_forward(tokens, captions, masked, weights):
    (
        mask_embed,
        position_embed,
        norm_self,
        query_self,
        key_self,
        value_self,
        out_self,
        norm_cross,
        query_cross,
        key_text,
        value_text,
        out_cross,
        norm_feed,
        up_weight,
        down_weight,
    ) = weights
    images = masked.shape[0]
    columns = tokens.shape[1]
    token_rows = tokens.astype(jnp.float32).reshape(images, IMG_LEN, columns)
    base = jnp.where(masked[:, :, None], mask_embed.astype(jnp.float32)[None, None, :], token_rows)
    stream_zero = (base + position_embed.astype(jnp.float32)[None]).reshape(
        images * IMG_LEN, columns
    )
    gathered_self, normal_self, inv_self = norm_forward(stream_zero, norm_self)
    query_one = contract(gathered_self, query_self, 1, 0).astype(jnp.bfloat16)
    key_one = contract(gathered_self, key_self, 1, 0).astype(jnp.bfloat16)
    value_one = contract(gathered_self, value_self, 1, 0).astype(jnp.bfloat16)
    mixed_self, probs_self, low_self = attend_forward(query_one, key_one, value_one, images)
    stream_one = stream_zero + project_out(mixed_self, out_self)
    gathered_cross, normal_cross, inv_cross = norm_forward(stream_one, norm_cross)
    text_full = lax.all_gather(captions, "tensor", axis=1, tiled=True)
    query_two = contract(gathered_cross, query_cross, 1, 0).astype(jnp.bfloat16)
    key_two = contract(text_full, key_text, 1, 0).astype(jnp.bfloat16)
    value_two = contract(text_full, value_text, 1, 0).astype(jnp.bfloat16)
    mixed_cross, probs_cross, low_cross = attend_forward(query_two, key_two, value_two, images)
    stream_two = stream_one + project_out(mixed_cross, out_cross)
    gathered_feed, normal_feed, inv_feed = norm_forward(stream_two, norm_feed)
    hidden = contract(gathered_feed, up_weight, 1, 0)
    activation = gelu_tanh(hidden).astype(jnp.bfloat16)
    stream_out = stream_two + project_out(activation, down_weight)
    stored = {
        "gathered_self": gathered_self,
        "normal_self": normal_self,
        "inv_self": inv_self,
        "query_one": query_one,
        "key_one": key_one,
        "value_one": value_one,
        "mixed_self": mixed_self,
        "probs_self": probs_self,
        "low_self": low_self,
        "gathered_cross": gathered_cross,
        "normal_cross": normal_cross,
        "inv_cross": inv_cross,
        "text_full": text_full,
        "query_two": query_two,
        "key_two": key_two,
        "value_two": value_two,
        "mixed_cross": mixed_cross,
        "probs_cross": probs_cross,
        "low_cross": low_cross,
        "gathered_feed": gathered_feed,
        "normal_feed": normal_feed,
        "inv_feed": inv_feed,
        "hidden": hidden,
        "activation": activation,
    }
    return (stream_out, stored)


def body(
    tokens,
    captions,
    mask_counts,
    mask_positions,
    cotangent,
    mask_embed,
    position_embed,
    norm_self,
    query_self,
    key_self,
    value_self,
    out_self,
    norm_cross,
    query_cross,
    key_text,
    value_text,
    out_cross,
    norm_feed,
    up_weight,
    down_weight,
):
    masked = mask_table(mask_counts, mask_positions)
    weights = (
        mask_embed,
        position_embed,
        norm_self,
        query_self,
        key_self,
        value_self,
        out_self,
        norm_cross,
        query_cross,
        key_text,
        value_text,
        out_cross,
        norm_feed,
        up_weight,
        down_weight,
    )
    stream_out, ignored = layer_forward(tokens, captions, masked, weights)
    fresh = lax.optimization_barrier((tokens, captions, weights))
    ignored_out, stored = layer_forward(fresh[0], fresh[1], masked, fresh[2])
    layer_out = stream_out.astype(jnp.bfloat16)
    images = masked.shape[0]
    columns = tokens.shape[1]
    mask_rows = masked.reshape(images * IMG_LEN, 1).astype(jnp.float32)
    grad_three = cotangent.astype(jnp.float32) * mask_rows
    seed_feed = branch_seed(grad_three)
    act_grad = contract(seed_feed, down_weight, 1, 1)
    down_grad = contract(stored["activation"], seed_feed, 0, 0)
    ignored_value, gelu_pull = jax.vjp(gelu_tanh, stored["hidden"])
    hidden_grad = gelu_pull(act_grad)[0].astype(jnp.bfloat16)
    up_grad = contract(stored["gathered_feed"], hidden_grad, 0, 0)
    feed_back, feed_gain = norm_backward(
        contract(hidden_grad, up_weight, 1, 1), stored["normal_feed"], stored["inv_feed"], norm_feed
    )
    grad_two = grad_three + feed_back
    seed_cross = branch_seed(grad_two)
    mixed_grad = contract(seed_cross, out_cross, 1, 1).astype(jnp.bfloat16)
    out_cross_grad = contract(stored["mixed_cross"], seed_cross, 0, 0)
    query_grad, key_grad, value_grad = attend_backward(
        mixed_grad,
        stored["query_two"],
        stored["key_two"],
        stored["value_two"],
        stored["probs_cross"],
        stored["low_cross"],
        images,
    )
    query_cross_grad = contract(stored["gathered_cross"], query_grad, 0, 0)
    key_text_grad = contract(stored["text_full"], key_grad, 0, 0)
    value_text_grad = contract(stored["text_full"], value_grad, 0, 0)
    text_partial = contract(key_grad, key_text, 1, 1) + contract(value_grad, value_text, 1, 1)
    captions_grad = lax.psum_scatter(
        text_partial.astype(jnp.bfloat16), "tensor", scatter_dimension=1, tiled=True
    )
    cross_back, cross_gain = norm_backward(
        contract(query_grad, query_cross, 1, 1),
        stored["normal_cross"],
        stored["inv_cross"],
        norm_cross,
    )
    grad_one = grad_two + cross_back
    seed_self = branch_seed(grad_one)
    mixed_grad = contract(seed_self, out_self, 1, 1).astype(jnp.bfloat16)
    out_self_grad = contract(stored["mixed_self"], seed_self, 0, 0)
    query_grad, key_grad, value_grad = attend_backward(
        mixed_grad,
        stored["query_one"],
        stored["key_one"],
        stored["value_one"],
        stored["probs_self"],
        stored["low_self"],
        images,
    )
    query_self_grad = contract(stored["gathered_self"], query_grad, 0, 0)
    key_self_grad = contract(stored["gathered_self"], key_grad, 0, 0)
    value_self_grad = contract(stored["gathered_self"], value_grad, 0, 0)
    self_partial = (
        contract(query_grad, query_self, 1, 1)
        + contract(key_grad, key_self, 1, 1)
        + contract(value_grad, value_self, 1, 1)
    )
    self_back, self_gain = norm_backward(
        self_partial, stored["normal_self"], stored["inv_self"], norm_self
    )
    grad_zero = grad_one + self_back
    grad_image = grad_zero.reshape(images, IMG_LEN, columns)
    mask_three = masked[:, :, None]
    tokens_grad = (
        jnp.where(mask_three, 0.0, grad_image)
        .reshape(images * IMG_LEN, columns)
        .astype(jnp.bfloat16)
    )
    embed_grad = jnp.sum(jnp.where(mask_three, grad_image, 0.0), axis=(0, 1))
    position_grad = jnp.sum(grad_image, axis=0)
    summed = (
        lax.psum(embed_grad.astype(jnp.bfloat16), "batch").astype(jnp.float32),
        lax.psum(position_grad.astype(jnp.bfloat16), "batch").astype(jnp.float32),
        lax.psum(self_gain.astype(jnp.bfloat16), "batch").astype(jnp.float32),
        lax.psum(query_self_grad.astype(jnp.bfloat16), "batch").astype(jnp.float32),
        lax.psum(key_self_grad.astype(jnp.bfloat16), "batch").astype(jnp.float32),
        lax.psum(value_self_grad.astype(jnp.bfloat16), "batch").astype(jnp.float32),
        lax.psum(out_self_grad.astype(jnp.bfloat16), "batch").astype(jnp.float32),
        lax.psum(cross_gain.astype(jnp.bfloat16), "batch").astype(jnp.float32),
        lax.psum(query_cross_grad.astype(jnp.bfloat16), "batch").astype(jnp.float32),
        lax.psum(key_text_grad.astype(jnp.bfloat16), "batch").astype(jnp.float32),
        lax.psum(value_text_grad.astype(jnp.bfloat16), "batch").astype(jnp.float32),
        lax.psum(out_cross_grad.astype(jnp.bfloat16), "batch").astype(jnp.float32),
        lax.psum(feed_gain.astype(jnp.bfloat16), "batch").astype(jnp.float32),
        lax.psum(up_grad.astype(jnp.bfloat16), "batch").astype(jnp.float32),
        lax.psum(down_grad.astype(jnp.bfloat16), "batch").astype(jnp.float32),
    )
    return (
        layer_out,
        tokens_grad,
        captions_grad,
        summed[0],
        summed[1],
        summed[2],
        summed[3],
        summed[4],
        summed[5],
        summed[6],
        summed[7],
        summed[8],
        summed[9],
        summed[10],
        summed[11],
        summed[12],
        summed[13],
        summed[14],
    )


def solution(mesh):
    return jax.shard_map(
        body,
        mesh=mesh,
        in_specs=(
            P("batch", "tensor"),
            P("batch", "tensor"),
            P("batch"),
            P("batch", None),
            P("batch", "tensor"),
            P("tensor"),
            P(None, "tensor"),
            P("tensor"),
            P(None, "tensor"),
            P(None, "tensor"),
            P(None, "tensor"),
            P("tensor", None),
            P("tensor"),
            P(None, "tensor"),
            P(None, "tensor"),
            P(None, "tensor"),
            P("tensor", None),
            P("tensor"),
            P(None, "tensor"),
            P("tensor", None),
        ),
        out_specs=(
            P("batch", "tensor"),
            P("batch", "tensor"),
            P("batch", "tensor"),
            P("tensor"),
            P(None, "tensor"),
            P("tensor"),
            P(None, "tensor"),
            P(None, "tensor"),
            P(None, "tensor"),
            P("tensor", None),
            P("tensor"),
            P(None, "tensor"),
            P(None, "tensor"),
            P(None, "tensor"),
            P("tensor", None),
            P("tensor"),
            P(None, "tensor"),
            P("tensor", None),
        ),
        check_vma=False,
    )
```

profile of v0, /device:TPU:0, one launch (start us, length us, event | category | flops | bytes accessed | tf_op | source)
XLA Modules:
  0.0 1311.7 jit_solution(503371704325715918)
XLA Ops:
  12.6 18.1 %all-reduce.7 = (f32[512]{0:T(512)S(1)}, f32[512]{0:T(512)S(1)}) all-reduce(f32[512]{0:T(512)S(1)} %get-tuple-element.57, f32[512]{0:T(512)S(1)} %get-tuple-element.56), channel_id=1, replica_groups=mesh['batch'=4,'tensor'=8] {'tensor'}, use_global_device_ids=true, to_apply=%region_23.24 | all-reduce | flops 1024 | bytes 8192 | tf_op jit(solution)/shard_map/psum | solution.py:40
  32.7 29.2 %all-gather.20.cloned.1.call-done = bf16[512,2048]{1,0:T(8,128)(2,1)} async-done(((bf16[512,256]{1,0:T(8,128)(2,1)}), bf16[512,2048]{1,0:T(8,128)(2,1)}) %all-gather.20.cloned.1.call-update) | async-done | bytes 2097168 | tf_op jit(solution)/shard_map/all_gather | solution.py:47
  77.6 48.4 %reduce-scatter.16.cloned.1.call-done = f32[512,256]{1,0:T(8,128)} async-done(((f32[512,2048]{1,0:T(8,128)}), f32[512,256]{1,0:T(8,128)}) %reduce-scatter.16.cloned.1.call-update) | async-done | bytes 524304 | tf_op jit(solution)/shard_map/reduce_scatter | solution.py:73
  127.4 14.0 %all-reduce.6 = (f32[512]{0:T(512)S(1)}, f32[512]{0:T(512)S(1)}) all-reduce(f32[512]{0:T(512)S(1)} %get-tuple-element.63, f32[512]{0:T(512)S(1)} %get-tuple-element.62), channel_id=1, replica_groups=mesh['batch'=4,'tensor'=8] {'tensor'}, use_global_device_ids=true, to_apply=%region_30.31 | all-reduce | flops 1024 | bytes 8192 | tf_op jit(solution)/shard_map/psum | solution.py:40
  142.4 12.6 all-gather.22.cloned.1.call-done
  161.2 26.2 %all-gather.24.cloned.1.call-done = bf16[512,2048]{1,0:T(8,128)(2,1)} async-done(((bf16[512,256]{1,0:T(8,128)(2,1)}), bf16[512,2048]{1,0:T(8,128)(2,1)}) %all-gather.24.cloned.1.call-update) | async-done | bytes 2097168 | tf_op jit(solution)/shard_map/all_gather | solution.py:47
  204.1 46.2 %reduce-scatter.18.cloned.1.call-done = f32[512,256]{1,0:T(8,128)} async-done(((f32[512,2048]{1,0:T(8,128)}), f32[512,256]{1,0:T(8,128)}) %reduce-scatter.18.cloned.1.call-update) | async-done | bytes 524304 | tf_op jit(solution)/shard_map/reduce_scatter | solution.py:73
  252.7 14.7 %all-reduce.5 = (f32[512]{0:T(512)}, f32[512]{0:T(512)}) all-reduce(f32[512]{0:T(512)} %get-tuple-element.61, f32[512]{0:T(512)} %get-tuple-element.60), channel_id=1, replica_groups=mesh['batch'=4,'tensor'=8] {'tensor'}, use_global_device_ids=true, to_apply=%region_37.38 | all-reduce | flops 1024 | bytes 8192 | tf_op jit(solution)/shard_map/psum | solution.py:40
  271.3 11.6 all-gather.28.cloned.1.call-done
  282.8 6.5 fusion.190
  289.3 25.3 %all-gather.26.cloned.1.call-done = bf16[512,2048]{1,0:T(8,128)(2,1)} async-done(((bf16[512,256]{1,0:T(8,128)(2,1)}), bf16[512,2048]{1,0:T(8,128)(2,1)}) %all-gather.26.cloned.1.call-update) | async-done | bytes 2097168 | tf_op jit(solution)/shard_map/all_gather | solution.py:47
  327.7 33.8 %reduce-scatter.20.cloned.1.call-done = bf16[512,256]{1,0:T(8,128)(2,1)} async-done(((bf16[512,2048]{1,0:T(8,128)(2,1)}), bf16[512,256]{1,0:T(8,128)(2,1)}) %reduce-scatter.20.cloned.1.call-update) | async-done | bytes 262160 | tf_op jit(solution)/shard_map/reduce_scatter | solution.py:52
  363.5 15.4 %all-reduce.4 = (f32[512]{0:T(512)}, f32[512]{0:T(512)}) all-reduce(f32[512]{0:T(512)} %get-tuple-element.53, f32[512]{0:T(512)} %get-tuple-element.69), channel_id=1, replica_groups=mesh['batch'=4,'tensor'=8] {'tensor'}, use_global_device_ids=true, to_apply=%region_42.43 | all-reduce | flops 1024 | bytes 8192 | tf_op jit(solution)/shard_map/psum | solution.py:57
  382.1 29.0 %all-gather.30.cloned.1.call-done = bf16[512,2048]{1,0:T(8,128)(2,1)} async-done(((bf16[512,256]{1,0:T(8,128)(2,1)}), bf16[512,2048]{1,0:T(8,128)(2,1)}) %all-gather.30.cloned.1.call-update) | async-done | bytes 2097168 | tf_op jit(solution)/shard_map/all_gather | solution.py:68
  423.8 35.0 %reduce-scatter.22.cloned.1.call-done = bf16[512,256]{1,0:T(8,128)(2,1)} async-done(((bf16[512,2048]{1,0:T(8,128)(2,1)}), bf16[512,256]{1,0:T(8,128)(2,1)}) %reduce-scatter.22.cloned.1.call-update) | async-done | bytes 262160 | tf_op jit(solution)/shard_map/reduce_scatter | solution.py:52
  460.6 14.7 %all-reduce.3 = (f32[512]{0:T(512)S(1)}, f32[512]{0:T(512)S(1)}) all-reduce(f32[512]{0:T(512)S(1)} %get-tuple-element.55, f32[512]{0:T(512)S(1)} %get-tuple-element.68), channel_id=1, replica_groups=mesh['batch'=4,'tensor'=8] {'tensor'}, use_global_device_ids=true, to_apply=%region_48.49 | all-reduce | flops 1024 | bytes 8192 | tf_op jit(solution)/shard_map/psum | solution.py:57
  478.0 28.7 %all-gather.32.cloned.1.call-done = bf16[512,2048]{1,0:T(8,128)(2,1)} async-done(((bf16[512,256]{1,0:T(8,128)(2,1)}), bf16[512,2048]{1,0:T(8,128)(2,1)}) %all-gather.32.cloned.1.call-update) | async-done | bytes 2097168 | tf_op jit(solution)/shard_map/all_gather | solution.py:68
  527.8 34.1 %reduce-scatter.24.cloned.1.call-done = bf16[512,256]{1,0:T(8,128)(2,1)} async-done(((bf16[512,2048]{1,0:T(8,128)(2,1)}), bf16[512,256]{1,0:T(8,128)(2,1)}) %reduce-scatter.24.cloned.1.call-update) | async-done | bytes 262160 | tf_op jit(solution)/shard_map/reduce_scatter | solution.py:52
  564.2 14.6 %all-reduce.2 = (f32[512]{0:T(512)S(1)}, f32[512]{0:T(512)S(1)}) all-reduce(f32[512]{0:T(512)S(1)} %get-tuple-element.71, f32[512]{0:T(512)S(1)} %get-tuple-element.72), channel_id=1, replica_groups=mesh['batch'=4,'tensor'=8] {'tensor'}, use_global_device_ids=true, to_apply=%region_4.5 | all-reduce | flops 1024 | bytes 8192 | tf_op jit(solution)/shard_map/psum | solution.py:40
  579.9 29.1 %all-gather.12.cloned.1.call-done = bf16[512,2048]{1,0:T(8,128)(2,1)} async-done(((bf16[512,256]{1,0:T(8,128)(2,1)}), bf16[512,2048]{1,0:T(8,128)(2,1)}) %all-gather.12.cloned.1.call-update) | async-done | bytes 2097168 | tf_op jit(solution)/shard_map/all_gather | solution.py:47
  627.1 48.6 %reduce-scatter.10.cloned.1.call-done = f32[512,256]{1,0:T(8,128)} async-done(((f32[512,2048]{1,0:T(8,128)}), f32[512,256]{1,0:T(8,128)}) %reduce-scatter.10.cloned.1.call-update) | async-done | bytes 524304 | tf_op jit(solution)/shard_map/reduce_scatter | solution.py:73
  677.0 14.0 %all-reduce.1 = (f32[512]{0:T(512)S(1)}, f32[512]{0:T(512)S(1)}) all-reduce(f32[512]{0:T(512)S(1)} %get-tuple-element.67, f32[512]{0:T(512)S(1)} %get-tuple-element.66), channel_id=1, replica_groups=mesh['batch'=4,'tensor'=8] {'tensor'}, use_global_device_ids=true, to_apply=%region_11.12 | all-reduce | flops 1024 | bytes 8192 | tf_op jit(solution)/shard_map/psum | solution.py:40
  692.2 12.2 all-gather.14.cloned.1.call-done
  710.5 26.4 %all-gather.16.cloned.1.call-done = bf16[512,2048]{1,0:T(8,128)(2,1)} async-done(((bf16[512,256]{1,0:T(8,128)(2,1)}), bf16[512,2048]{1,0:T(8,128)(2,1)}) %all-gather.16.cloned.1.call-update) | async-done | bytes 2097168 | tf_op jit(solution)/shard_map/all_gather | solution.py:47
  750.6 49.2 %reduce-scatter.12.cloned.1.call-done = f32[512,256]{1,0:T(8,128)} async-done(((f32[512,2048]{1,0:T(8,128)}), f32[512,256]{1,0:T(8,128)}) %reduce-scatter.12.cloned.1.call-update) | async-done | bytes 524304 | tf_op jit(solution)/shard_map/reduce_scatter | solution.py:73
  801.7 14.5 %all-reduce = (f32[512]{0:T(512)S(1)}, f32[512]{0:T(512)S(1)}, f32[512]{0:T(512)}, f32[512]{0:T(512)}) all-reduce(f32[512]{0:T(512)S(1)} %get-tuple-element.65, f32[512]{0:T(512)S(1)} %get-tuple-element.64, f32[512]{0:T(512)S(1)} %copy-done.57, f32[512]{0:T(512)S(1)} %copy-done.58), channel_id=1, replica_groups=mesh['batch'=4,'tensor'=8] {'tensor'}, use_global_device_ids=true, to_apply=%region_18.19 | all-reduce | flops 2048 | bytes 16384 | tf_op jit(solution)/shard_map/psum | solution.py:40
  818.3 29.1 %all-gather.18.cloned.1.call-done = bf16[512,2048]{1,0:T(8,128)(2,1)} async-done(((bf16[512,256]{1,0:T(8,128)(2,1)}), bf16[512,2048]{1,0:T(8,128)(2,1)}) %all-gather.18.cloned.1.call-update) | async-done | bytes 2097168 | tf_op jit(solution)/shard_map/all_gather | solution.py:47
  847.4 11.0 fusion.38
  858.8 7.0 convolution_convert_fusion.2
  898.1 9.6 all-reduce.8
  912.5 353.0 %all-reduce.12.cloned.1.call-done = (bf16[256,256]{1,0:T(8,128)(2,1)}, bf16[2048,256]{1,0:T(8,128)(2,1)}, bf16[2048,256]{1,0:T(8,128)(2,1)}, bf16[2048,256]{1,0:...) async-done(((bf16[256,256]{1,0:T(8,128)(2,1)}, ...) | async-done | bytes 19005456 | tf_op jit(solution)/shard_map/psum | solution.py:310
  1293.4 11.0 reduce-scatter.26.cloned.1.call-done
  (345 shorter events, 223.1 us)
Async XLA Ops:
  7.2 147.9 %copy-start = (bf16[4096,256]{1,0:T(8,128)(2,1)S(1)}, bf16[4096,256]{1,0:T(8,128)(2,1)}, u32[]{:S(2)}) copy-start(bf16[4096,256]{1,0:T(8,128)(2,1)} %param.34) | copy-start | bytes 6291460
  7.2 54.6 %all-gather.20.cloned.1.call-start = ((), (), s32[]{:S(2)}) async-start(), calls=%async_computation.16 | async-start | bytes 2359296 | tf_op jit(solution)/shard_map/all_gather | solution.py:47
  8.0 118.0 %copy-start.51 = (f32[256]{0:T(256)}, f32[256]{0:T(256)S(1)}, u32[]{:S(2)}) copy-start(f32[256]{0:T(256)S(1)} %convert_element_type.348) | copy-start | bytes 3076
  32.6 93.4 %reduce-scatter.16.cloned.1.call-start = ((), (), s32[]{:S(2)}) async-start(), calls=%async_computation.17 | async-start | bytes 4718592 | tf_op jit(solution)/shard_map/reduce_scatter | solution.py:73
  76.8 49.2 %copy-start.2 = (bf16[512,256]{1,0:T(8,128)(2,1)S(1)}, bf16[512,256]{1,0:T(8,128)(2,1)}, u32[]{:S(2)}) copy-start(bf16[512,256]{1,0:T(8,128)(2,1)} %param.20) | copy-start | bytes 786436
  76.8 78.2 %all-gather.22.cloned.1.call-start = ((), (), s32[]{:S(2)}) async-start(), calls=%async_computation.18 | async-start | bytes 2359296 | tf_op jit(solution)/shard_map/all_gather | solution.py:152
  77.6 109.9 %all-gather.24.cloned.1.call-start = ((), (), s32[]{:S(2)}) async-start(), calls=%async_computation.19 | async-start | bytes 2359296 | tf_op jit(solution)/shard_map/all_gather | solution.py:47
  142.4 107.9 %reduce-scatter.18.cloned.1.call-start = ((), (), s32[]{:S(2)}) async-start(), calls=%async_computation.20 | async-start | bytes 4718592 | tf_op jit(solution)/shard_map/reduce_scatter | solution.py:73
  157.5 261.0 %copy-start.42 = (bf16[2,128,2,128]{1,3,2,0:T(8,128)(2,1)}, bf16[2,128,2,128]{1,3,2,0:T(8,128)(2,1)S(1)}, u32[]{:S(2)}) copy-start(bf16[2,128,2,128]{1,3,2,0:T(8,128)(2,1)S(1)} %copy.134) | copy-start | bytes 393220
  201.0 81.8 %all-gather.28.cloned.1.call-start = ((), (), s32[]{:S(2)}) async-start(), calls=%async_computation.22 | async-start | bytes 2359296 | tf_op jit(solution)/shard_map/all_gather | solution.py:68
  202.8 111.9 %all-gather.26.cloned.1.call-start = ((), (), s32[]{:S(2)}) async-start(), calls=%async_computation.21 | async-start | bytes 2359296 | tf_op jit(solution)/shard_map/all_gather | solution.py:47
  270.7 90.8 %reduce-scatter.20.cloned.1.call-start = ((), (), s32[]{:S(2)}) async-start(), calls=%async_computation.23 | async-start | bytes 2359296 | tf_op jit(solution)/shard_map/reduce_scatter | solution.py:52
  326.4 84.7 %all-gather.30.cloned.1.call-start = ((), (), s32[]{:S(2)}) async-start(), calls=%async_computation.24 | async-start | bytes 2359296 | tf_op jit(solution)/shard_map/all_gather | solution.py:68
  382.0 76.8 %reduce-scatter.22.cloned.1.call-start = ((), (), s32[]{:S(2)}) async-start(), calls=%async_computation.25 | async-start | bytes 2359296 | tf_op jit(solution)/shard_map/reduce_scatter | solution.py:52
  420.3 38.5 %copy-start.48 = (f32[512]{0:T(512)S(1)}, f32[512]{0:T(512)}, u32[]{:S(2)}) copy-start(f32[512]{0:T(512)} %copy-done.47) | copy-start | bytes 6148
  423.8 83.0 %all-gather.32.cloned.1.call-start = ((), (), s32[]{:S(2)}) async-start(), calls=%async_computation.26 | async-start | bytes 2359296 | tf_op jit(solution)/shard_map/all_gather | solution.py:68
  477.7 34.2 %copy-start.30 = (bf16[2,256,2,128]{1,3,2,0:T(8,128)(2,1)S(1)}, bf16[2,256,2,128]{1,3,2,0:T(8,128)(2,1)}, u32[]{:S(2)}) copy-start(bf16[2,256,2,128]{1,3,2,0:T(8,128)(2,1)} %copy-done.29) | copy-start | bytes 786436
  477.8 84.2 %reduce-scatter.24.cloned.1.call-start = ((), (), s32[]{:S(2)}) async-start(), calls=%async_computation.27 | async-start | bytes 2359296 | tf_op jit(solution)/shard_map/reduce_scatter | solution.py:52
  526.9 35.1 %copy-start.52 = (f32[256]{0:T(256)S(1)}, f32[256]{0:T(256)}, u32[]{:S(2)}) copy-start(f32[256]{0:T(256)} %copy-done.51) | copy-start | bytes 3076
  526.9 82.1 %all-gather.12.cloned.1.call-start = ((), (), s32[]{:S(2)}) async-start(), calls=%async_computation.9 | async-start | bytes 2359296 | tf_op jit(solution)/shard_map/all_gather | solution.py:47
  527.8 83.8 %copy-start.55 = (f32[256]{0:T(256)}, f32[256]{0:T(256)S(1)}, u32[]{:S(2)}) copy-start(f32[256]{0:T(256)S(1)} %convert_element_type.326) | copy-start | bytes 3076
  579.9 95.8 %reduce-scatter.10.cloned.1.call-start = ((), (), s32[]{:S(2)}) async-start(), calls=%async_computation.10 | async-start | bytes 4718592 | tf_op jit(solution)/shard_map/reduce_scatter | solution.py:73
  626.4 78.1 %all-gather.14.cloned.1.call-start = ((), (), s32[]{:S(2)}) async-start(), calls=%async_computation.11 | async-start | bytes 2359296 | tf_op jit(solution)/shard_map/all_gather | solution.py:152
  627.0 109.9 %all-gather.16.cloned.1.call-start = ((), (), s32[]{:S(2)}) async-start(), calls=%async_computation.12 | async-start | bytes 2359296 | tf_op jit(solution)/shard_map/all_gather | solution.py:47
  692.0 107.8 %reduce-scatter.12.cloned.1.call-start = ((), (), s32[]{:S(2)}) async-start(), calls=%async_computation.13 | async-start | bytes 4718592 | tf_op jit(solution)/shard_map/reduce_scatter | solution.py:73
  750.5 51.2 %copy-start.57 = (f32[512]{0:T(512)S(1)}, f32[512]{0:T(512)}, u32[]{:S(2)}) copy-start(f32[512]{0:T(512)} %get-tuple-element.51) | copy-start | bytes 6148
  750.5 51.2 %copy-start.58 = (f32[512]{0:T(512)S(1)}, f32[512]{0:T(512)}, u32[]{:S(2)}) copy-start(f32[512]{0:T(512)} %get-tuple-element.70) | copy-start | bytes 6148
  750.5 65.7 %copy-start.54 = (f32[256]{0:T(256)S(1)}, f32[256]{0:T(256)}, u32[]{:S(2)}) copy-start(f32[256]{0:T(256)} %convert_element_type.342) | copy-start | bytes 3076
  750.6 96.8 %all-gather.18.cloned.1.call-start = ((), (), s32[]{:S(2)}) async-start(), calls=%async_computation.14 | async-start | bytes 2359296 | tf_op jit(solution)/shard_map/all_gather | solution.py:47
  818.2 92.5 %reduce-scatter.14.cloned.1.call-start = ((), (), s32[]{:S(2)}) async-start(), calls=%async_computation.15 | async-start | bytes 4718592 | tf_op jit(solution)/shard_map/reduce_scatter | solution.py:73
  858.4 407.2 %all-reduce.12.cloned.1.call-start = ((), (), s32[]{:S(2)}) async-start(), calls=%async_computation.29 | async-start | bytes 38010880 | tf_op jit(solution)/shard_map/psum | solution.py:310
  893.4 411.0 %reduce-scatter.26.cloned.1.call-start = ((), (), s32[]{:S(2)}) async-start(), calls=%async_computation.28 | async-start | bytes 2359296 | tf_op jit(solution)/shard_map/reduce_scatter | solution.py:265
  (67 other events, 261.6 us)
Sparse Core Ops, SparseCore 0:
  32.8 29.0 all-gather.19
  77.0 49.0 reduce-scatter.15
  127.7 27.3 all-gather.21
  157.1 30.3 all-gather.23
  201.1 49.0 reduce-scatter.17
  252.3 30.5 all-gather.27
  285.0 29.6 all-gather.25
  326.5 34.8 reduce-scatter.19
  382.2 28.9 all-gather.29
  423.9 34.8 reduce-scatter.21
  477.8 28.8 all-gather.31
  527.0 34.8 reduce-scatter.23
  580.0 28.9 all-gather.11
  626.6 49.0 reduce-scatter.9
  677.1 27.3 all-gather.13
  706.5 30.3 all-gather.15
  750.7 49.0 reduce-scatter.11
  818.4 28.9 all-gather.17
  858.6 49.0 reduce-scatter.13
  914.9 350.6 all-reduce.11
  1268.6 35.7 reduce-scatter.25
where the time goes:
time: 1320 us; the launch traced here: 1310 us
  waiting for transfers between devices  920 us (70%)
  matrix products  147 us (11%)
  blocking collectives  130 us (10%)
  other arithmetic  69.4 us (5%)
  local copies, waits for them, and re-layouts  27.1 us (2%)
  between operations  15.6 us (1%)
    psum x1, waiting for transfers between devices, body(): lax.psum(position_grad.astype(jnp.bfloat16), 'batch').astype(jnp.float32)  353 us
    reduce_scatter x5, waiting for transfers between devices, project_out(): lax.psum_scatter(partial_out, 'tensor', scatter_dimension=1, tiled=True)  192 us
    all_gather x6, waiting for transfers between devices, norm_forward(): gathered = lax.all_gather(normed, 'tensor', axis=1, tiled=True)  165 us
    dot_general x38, matrix products, contract(): lax.dot_general(left, right, (((left_dim,), (right_dim,)), ((), ())), pre...  122 us
    reduce_scatter x3, waiting for transfers between devices, norm_backward(): lax.psum_scatter(partial_grad.astype(jnp.bfloat16), 'tensor', scatter_dim...  103 us
    psum x6, blocking collectives, norm_forward(): lax.psum((jnp.sum(stream, axis=1), jnp.sum(stream * stream, axis=1)), 'te...  89.9 us
    all_gather x3, waiting for transfers between devices, branch_seed(): lax.all_gather(stream_grad.astype(jnp.bfloat16), 'tensor', axis=1, tiled=...  69.3 us
    psum x2, blocking collectives, norm_backward(): lax.psum((jnp.sum(scaled, axis=1), jnp.sum(scaled * normal, axis=1)), 'te...  30.1 us
  transfers between devices with their start and end apart: 21, of which 20 were waited for; matrix products, arithmetic and copies ran while one was open for 8% of the time, Pallas kernels for 0%

commit v1 on v0

v1 whole, which is shorter than its diff:
```python
import jax
import jax.numpy as jnp
from jax import lax
from jax.experimental import pallas as pl
from jax.experimental.pallas import tpu as pltpu
from jax.sharding import PartitionSpec as P

HEAD_DIM = 128
IMG_LEN = 256
EPS = 1e-06
F32 = jnp.float32
BF16 = jnp.bfloat16
INV_ROOT = float(HEAD_DIM) ** (-0.5)
PAD = 16
DIRECT = ()
COST = {"self_forward": 17, "text_project": 25, "cross_forward": 0, "seed_product": 12, "feed_both": 6, "out_product": 15, "cross_backward": 20, "self_backward": 27, "self_end": 5, "text_back": 8, "down_grads": 17, "up_grads": 14, "text_grads": 15, "self_grads": 40, "cross_parts": 7, "self_parts": 7, "cross_finish": 0, "self_finish": 5}
DONE_BY = {"T1": "scattered1", "KV": "scattered1", "T2": "scattered2", "X1": "partial2", "X2": "scattered2", "T3": "scattered2", "DA": "scattered2", "Y1": "partial3", "X3": "mixed2", "Y2": "partial3", "F1": "scattered3", "OUT": "mixed2", "Y3": "scattered3", "F2": "mixed3", "A1": "partial4", "A2": "scattered4", "F3": "mixed3", "C0": "scattered4", "TB": "scattered4", "U1": "mixed4", "C1": "scattered4", "GD": "mixed4", "U2": "partial5", "D": "partial5", "GU": "partial5", "GT": "scattered5", "Q1": "scattered5", "Q2": "small", "S0": "scattered5", "S1": "scattered5", "S2": "small"}
AFTER = {"Y1": ("X2",), "A1": ("F2",), "U1": ("TB",), "D": ("C1", "U1",), "S1": ("Q2",), "GQ": ("S1",), "S2": ("GQ",), "GT": ("GU",)}


def contract(left, right, left_dim, right_dim):
    return lax.dot_general(
        left, right, (((left_dim,), (right_dim,)), ((), ())), preferred_element_type=F32
    )


def tie(*values):
    leaves, tree = jax.tree.flatten(values)
    arrays = iter(lax.optimization_barrier([v for v in leaves if not isinstance(v, int)]))
    return tree.unflatten([v if isinstance(v, int) else next(arrays) for v in leaves])


def gather_cols(array):
    return lax.all_gather(array, "tensor", axis=1, tiled=True)


def scatter_cols(array):
    return lax.psum_scatter(array, "tensor", scatter_dimension=1, tiled=True)


def square_batch():
    return lax.axis_size("batch") == 4


def hop(array, flip):
    pairs = [(i, i ^ flip) for i in range(lax.axis_size("batch"))]
    return lax.ppermute(array, "batch", pairs)


def swap_core(array):
    pairs = [(i, i ^ 1) for i in range(lax.axis_size("tensor"))]
    return lax.ppermute(array, "tensor", pairs)


def ring_others(array):
    size, own = lax.axis_size("batch"), lax.axis_index("batch")
    whole = lax.all_gather(array, "batch", axis=0, tiled=False)
    return [
        lax.dynamic_index_in_dim(whole, lax.rem(own + k, size), 0, keepdims=False)
        for k in range(1, size)
    ]


def direct(array):
    moved = [hop(array, k) for k in (1, 2, 3)] if square_batch() else ring_others(array)
    return [[(m, 0)] for m in moved]


class Spread:
    def __init__(self, array, shared):
        self.array, self.shared = array, shared

    def step_one(self):
        if not square_batch():
            return ring_others(self.array)
        return [hop(self.array, 1), hop(self.array, 2)]

    def step_two(self, held):
        rows = self.array.shape[0]
        if square_batch():
            cut = rows // 2
            along, across = held
            groups = [
                [(along, 0)],
                [(across, 0)],
                [(hop(along[:cut], 2), 0), (hop(across[cut:], 1), cut)],
            ]
        else:
            groups = [[(piece, 0)] for piece in held]
        return groups

    def swap(self, groups):
        if self.shared:
            rows = self.array.shape[0]
            groups = [g + [(swap_core(piece), rows + at) for piece, at in g] for g in groups]
        return groups


def direct_sum(array):
    if not square_batch():
        return lax.psum(array.astype(BF16), "batch").astype(F32)
    low = array.astype(BF16)
    moved = [hop(low, k) for k in (1, 2, 3)]
    return array + moved[0].astype(F32) + moved[1].astype(F32) + moved[2].astype(F32)


def params():
    return pltpu.CompilerParams(vmem_limit_bytes=56 << 20)


def cost(micros):
    return pl.CostEstimate(
        flops=1000, bytes_accessed=int(1e6 * micros) + 1000, transcendentals=0
    )


def struct(shape, dtype):
    return jax.ShapeDtypeStruct(shape, dtype)


def by_rows(rows, width, first=0):
    return pl.BlockSpec((rows, width), lambda i, *_: (first + i, 0))


def turned_rows(rows, width):
    blocks = IMG_LEN // rows
    return pl.BlockSpec((rows, width), lambda i, place: (image_turn(i, place, blocks), 0))


def fixed(shape, row=0, col=0):
    return pl.BlockSpec(shape, lambda i, *_: (row, col))


def call(name, kernel, place, grid, in_specs, out_specs, outs, args, scratch=(), aliases=None):
    return pl.pallas_call(
        kernel,
        grid_spec=pltpu.PrefetchScalarGridSpec(
            num_scalar_prefetch=1,
            grid=grid,
            in_specs=in_specs,
            out_specs=out_specs,
            scratch_shapes=list(scratch),
        ),
        out_shape=outs,
        input_output_aliases=aliases or {},
        compiler_params=params(),
        cost_estimate=cost(COST[name]),
        name=name,
    )(place, *args)


def core_of(place):
    return place[0] % 2


class Packed:
    def __init__(self, rows, text_rows):
        self.rows = rows
        self.pos = rows
        self.text = rows + IMG_LEN
        self.seed = self.text + text_rows
        self.vec = self.seed + rows
        self.total = self.vec + PAD


def pack_rows(at, counts, positions, tokens, captions, cotangent, position_embed, vectors):
    rows, columns = tokens.shape
    images = rows // IMG_LEN
    text_rows = captions.shape[0]
    text_blocks = captions.shape[1] // columns

    def kernel(counts, order, tok, cap, cot, pos, *rest):
        out, block, mask = rest[-3:]
        out[: at.pos, :] = tok[...]
        out[at.pos : at.text, :] = pos[...]
        for k in range(text_blocks):
            low = at.text + k * text_rows
            out[low : low + text_rows, :] = cap[:, k * columns : (k + 1) * columns]
        lines = [v[...].astype(F32).reshape(1, columns) for v in rest[:-3]]
        lines.append(jnp.zeros((PAD - len(lines), columns), F32))
        vec = jnp.concatenate(lines, axis=0).astype(BF16)
        out[at.vec :, :] = vec
        block[...] = vec
        place = lax.broadcasted_iota(jnp.int32, (IMG_LEN, IMG_LEN), 0)
        slot = lax.broadcasted_iota(jnp.int32, (IMG_LEN, IMG_LEN), 1)
        for i in range(images):
            hit = (order[i : i + 1, :] == place) & (slot < counts[i])
            column = jnp.max(hit.astype(F32), axis=1, keepdims=True)
            own = slice(i * IMG_LEN, (i + 1) * IMG_LEN)
            mask[own, :] = column
            out[at.seed + i * IMG_LEN : at.seed + (i + 1) * IMG_LEN, :] = jnp.where(
                column > 0.0, cot[own, :].astype(F32), 0.0
            ).astype(BF16)

    vmem = pl.BlockSpec(memory_space=pltpu.VMEM)
    outs = [
        struct((at.total, columns), BF16),
        struct((PAD, columns), BF16),
        struct((rows, 1), F32),
    ]
    args = (counts, positions, tokens, captions, cotangent, position_embed, *vectors)
    return pl.pallas_call(
        kernel,
        in_specs=[pl.BlockSpec(memory_space=pltpu.SMEM)] + [vmem] * (len(args) - 1),
        out_specs=[vmem] * 3,
        out_shape=outs,
        compiler_params=params(),
        cost_estimate=cost(2),
        name="pack_rows",
    )(*args)


def normalize(stream):
    width = stream.shape[1]
    mean = jnp.sum(stream, axis=1, keepdims=True) * (1.0 / width)
    var = jnp.sum(stream * stream, axis=1, keepdims=True) * (1.0 / width) - mean * mean
    inv_std = lax.rsqrt(var + EPS)
    return (stream - mean) * inv_std, mean, inv_std


def norm_back(grad, normed, inv_std, gain):
    width = grad.shape[1]
    normal = normed * (1.0 / gain)
    scaled = grad * gain
    first = jnp.sum(scaled, axis=1, keepdims=True) * (1.0 / width)
    second = jnp.sum(grad * normed, axis=1, keepdims=True) * (1.0 / width)
    back = inv_std * (scaled - first - normal * second)
    return back, jnp.sum(grad * normal, axis=0, keepdims=True)


def probabilities(query, key):
    scores = contract(query, key, 1, 1) * INV_ROOT
    terms = jnp.exp(scores - jnp.max(scores, axis=1, keepdims=True))
    return terms * (1.0 / jnp.sum(terms, axis=1, keepdims=True))


def head_slices(width):
    return [slice(at, at + HEAD_DIM) for at in range(0, width, HEAD_DIM)]


def attend(query, key, value):
    mixed = [
        contract(probabilities(query[:, h], key[:, h]).astype(BF16), value[:, h], 1, 0)
        for h in head_slices(query.shape[1])
    ]
    return jnp.concatenate(mixed, axis=1).astype(BF16)


def attend_back(grad, query, key, value):
    parts = []
    for h in head_slices(query.shape[1]):
        probs = probabilities(query[:, h], key[:, h])
        prob_grad = contract(grad[:, h], value[:, h], 1, 1)
        inner = jnp.sum(probs * prob_grad, axis=1, keepdims=True)
        score_grad = (probs * (prob_grad - inner)).astype(BF16)
        parts.append(
            (
                contract(score_grad, key[:, h], 1, 0) * INV_ROOT,
                contract(score_grad, query[:, h], 0, 0) * INV_ROOT,
                contract(probs.astype(BF16), grad[:, h], 0, 0),
            )
        )
    return [jnp.concatenate(group, axis=1).astype(BF16) for group in zip(*parts)]


def first_stream(mask, tok, pos, vec):
    base = jnp.where(mask[...] > 0.0, vec[0:1, :].astype(F32), tok[...].astype(F32))
    return base + pos[...].astype(F32)


def packed_specs(at, width):
    return [
        by_rows(IMG_LEN, 1),
        by_rows(IMG_LEN, width),
        fixed((IMG_LEN, width), at.pos // IMG_LEN),
        fixed((PAD, width), at.vec // PAD),
    ]


def self_forward(place, at, mask, packed, query_w, key_w, value_w, out_w):
    rows, width = mask.shape[0], packed.shape[1]
    columns = query_w.shape[1]

    def kernel(
        place, mask, tok, pos, vec, wq, wk, wv, wo, normed, query, key, value, mixed, part, stats
    ):
        normal, mean, inv_std = normalize(first_stream(mask, tok, pos, vec))
        stats[:, 0:1] = mean
        stats[:, 1:2] = inv_std
        low = (normal * vec[1:2, :].astype(F32)).astype(BF16)
        normed[...] = low
        q = contract(low, wq[...], 1, 0).astype(BF16)
        k = contract(low, wk[...], 1, 0).astype(BF16)
        v = contract(low, wv[...], 1, 0).astype(BF16)
        query[...], key[...], value[...] = q, k, v
        a = attend(q, k, v)
        mixed[...] = a
        part[...] = contract(a, wo[...], 1, 0).astype(BF16)

    outs = [struct((rows, width), BF16)] + [struct((rows, columns), BF16)] * 4
    outs += [struct((rows, width), BF16), struct((rows, 2), F32)]
    args = (mask, packed, packed, packed, query_w, key_w, value_w, out_w)
    return call(
        "self_forward",
        kernel,
        place,
        (rows // IMG_LEN,),
        packed_specs(at, width) + [fixed(w.shape) for w in (query_w, key_w, value_w, out_w)],
        [turned_rows(IMG_LEN, width)] + [by_rows(IMG_LEN, o.shape[1]) for o in outs[1:]],
        outs,
        args,
    )


def text_project(place, at, text, key_w, value_w):
    columns = key_w.shape[1]
    width = text.shape[1]
    shards = width // columns
    blocks = key_w.shape[0] // width
    text_rows = (at.seed - at.text) // blocks
    first = at.text // text_rows
    step = min(4, shards)

    def kernel(place, *refs):
        texts, (wk, wv, key, value, key_sum, value_sum) = refs[:blocks], refs[blocks:]

        @pl.when(pl.program_id(0) == 0)
        def _():
            key_sum[...] = jnp.zeros_like(key_sum)
            value_sum[...] = jnp.zeros_like(value_sum)

        for t in range(step):
            for k, text in enumerate(texts):
                piece = text[:, t * columns : (t + 1) * columns]
                key_sum[...] += contract(piece, wk[t, k], 1, 0)
                value_sum[...] += contract(piece, wv[t, k], 1, 0)

        @pl.when(pl.program_id(0) == pl.num_programs(0) - 1)
        def _():
            key[...] = key_sum[...].astype(BF16)
            value[...] = value_sum[...].astype(BF16)

    cut = (shards, blocks, columns, columns)
    outs = [struct((text_rows, columns), BF16)] * 2
    weight = pl.BlockSpec((step, *cut[1:]), lambda i, *_: (i, 0, 0, 0))
    args = (*[text] * blocks, key_w.reshape(cut), value_w.reshape(cut))
    return call(
        "text_project",
        kernel,
        place,
        (shards // step,),
        [
            pl.BlockSpec((text_rows, step * columns), lambda i, *_, k=k: (first + k, i))
            for k in range(blocks)
        ]
        + [weight] * 2,
        [fixed(o.shape) for o in outs],
        outs,
        args,
        scratch=[pltpu.VMEM((text_rows, columns), F32)] * 2,
    )


def cross_forward(place, at, mask, packed, added, query_w, key, value, out_w):
    rows, width = mask.shape[0], packed.shape[1]
    columns = query_w.shape[1]
    text_rows = key.shape[0] // (rows // IMG_LEN)

    def kernel(
        place, mask, tok, pos, vec, add, wq, k, v, wo, stream, normed, query, mixed, part, scale
    ):
        one = first_stream(mask, tok, pos, vec) + add[...].astype(F32)
        stream[...] = one
        normal, mean, inv_std = normalize(one)
        scale[...] = inv_std
        low = (normal * vec[2:3, :].astype(F32)).astype(BF16)
        normed[...] = low
        q = contract(low, wq[...], 1, 0).astype(BF16)
        query[...] = q
        a = attend(q, k[...], v[...])
        mixed[...] = a
        part[...] = contract(a, wo[...], 1, 0).astype(BF16)

    outs = [struct((rows, width), F32), struct((rows, width), BF16)]
    outs += [struct((rows, columns), BF16)] * 2 + [struct((rows, width), BF16)]
    outs += [struct((rows, 1), F32)]
    args = (mask, packed, packed, packed, added, query_w, key, value, out_w)
    return call(
        "cross_forward",
        kernel,
        place,
        (rows // IMG_LEN,),
        packed_specs(at, width)
        + [
            by_rows(IMG_LEN, width),
            fixed(query_w.shape),
            by_rows(text_rows, columns),
            by_rows(text_rows, columns),
            fixed(out_w.shape),
        ],
        [by_rows(IMG_LEN, o.shape[1]) for o in outs],
        outs,
        args,
    )


def seed_product(place, at, seed, down_w):
    rows, (hidden, width) = at.rows, down_w.shape

    def kernel(place, seed, down, out):
        out[...] = contract(seed[...], down[...], 1, 1)

    outs = [struct((rows, hidden), F32)]
    return call(
        "seed_product",
        kernel,
        place,
        (rows // IMG_LEN,),
        [by_rows(IMG_LEN, width, at.seed // IMG_LEN), fixed(down_w.shape)],
        [by_rows(IMG_LEN, hidden)],
        outs,
        (seed, down_w),
    )[0]


def gelu_parts(u):
    scale = 0.7978845608028654
    square = u * u
    bend = jnp.tanh(scale * (u + 0.044715 * square * u))
    half = 0.5 * (1.0 + bend)
    slope = half + 0.5 * u * (1.0 - bend * bend) * scale * (1.0 + 3.0 * 0.044715 * square)
    return u * half, slope


def image_turn(i, place, blocks):
    return (i // blocks + place[0] % 2) % 2 * blocks + i % blocks


def feed_both(place, at, stream, added, packed, act_grad, up_w):
    rows, width = stream.shape
    hidden, columns = up_w.shape[1], width // lax.axis_size("tensor")
    block = IMG_LEN

    def kernel(place, one, add, vec, dact, up, slim, scale, normed, act, grad, part, two):
        stream = one[...] + add[...].astype(F32)
        two[...] = stream
        slim[...] = two[:, pl.ds(pl.multiple_of(place[0] * columns, columns), columns)]
        normal, mean, inv_std = normalize(stream)
        scale[...] = inv_std
        low = (normal * vec[3:4, :].astype(F32)).astype(BF16)
        normed[...] = low
        value, slope = gelu_parts(contract(low, up[...], 1, 0))
        act[...] = value.astype(BF16)
        du = (dact[...] * slope).astype(BF16)
        grad[...] = du
        part[...] = contract(du, up[...], 1, 1).astype(BF16)

    outs = [
        struct((rows, columns), F32),
        struct((rows, 1), F32),
        struct((rows, width), BF16),
        struct((rows, hidden), BF16),
        struct((rows, hidden), BF16),
        struct((rows, width), BF16),
    ]
    args = (stream, added, packed, act_grad, up_w)
    return call(
        "feed_both",
        kernel,
        place,
        (rows // block,),
        [
            by_rows(block, width),
            by_rows(block, width),
            fixed((PAD, width), at.vec // PAD),
            by_rows(block, hidden),
            fixed(up_w.shape),
        ],
        [
            by_rows(block, columns),
            by_rows(block, 1),
            turned_rows(block, width),
            turned_rows(block, hidden),
            turned_rows(block, hidden),
            by_rows(block, width),
        ],
        outs,
        args,
        scratch=[pltpu.VMEM((block, width), F32)],
    )


def out_product(place, activation, down_w):
    rows, (hidden, width) = activation.shape[0], down_w.shape

    def kernel(place, act, down, out):
        out[...] = contract(act[...], down[...], 1, 0).astype(BF16)

    outs = [struct((2 * rows, width), BF16)]
    return call(
        "out_product",
        kernel,
        place,
        (rows // IMG_LEN,),
        [
            turned_rows(IMG_LEN, hidden),
            fixed(down_w.shape),
        ],
        [by_rows(IMG_LEN, width, rows // IMG_LEN)],
        outs,
        (activation, down_w),
    )[0]


def cross_backward(
    place, at, normed, scale, back, seed, packed, out_w, query, key, value, query_w, room
):
    rows, width = normed.shape
    columns = query.shape[1]
    text_rows = key.shape[0] // (rows // IMG_LEN)

    def kernel(place, three, inv, dn, g3, vec, wo, q, k, v, wq, room, grad, low, dq, dkv, part, gain):
        step, gain_step = norm_back(
            dn[...].astype(F32), three[...].astype(F32), inv[...], vec[3:4, :].astype(F32)
        )
        total = g3[...].astype(F32) + step
        grad[...] = total
        y = total.astype(BF16)
        low[...] = y

        @pl.when(pl.program_id(0) == 0)
        def _():
            gain[...] = jnp.zeros_like(gain)

        gain[...] += gain_step
        da = contract(y, wo[...], 1, 1).astype(BF16)
        query_grad, key_grad, value_grad = attend_back(da, q[...], k[...], v[...])
        dq[...] = query_grad
        dkv[:, :columns] = key_grad
        dkv[:, columns:] = value_grad
        part[...] = contract(query_grad, wq[...], 1, 1).astype(BF16)

    outs = [
        struct((rows, width), F32),
        struct((rows, width), BF16),
        struct((rows, columns), BF16),
        struct((key.shape[0], 2 * columns), BF16),
        struct(room.shape, BF16),
        struct((1, width), F32),
    ]
    args = (normed, scale, back, seed, packed, out_w, query, key, value, query_w, room)
    return call(
        "cross_backward",
        kernel,
        place,
        (rows // IMG_LEN,),
        [
            turned_rows(IMG_LEN, width),
            by_rows(IMG_LEN, 1),
            by_rows(IMG_LEN, width),
            by_rows(IMG_LEN, width, at.seed // IMG_LEN),
            fixed((PAD, width), at.vec // PAD),
            fixed(out_w.shape),
            by_rows(IMG_LEN, columns),
            by_rows(text_rows, columns),
            by_rows(text_rows, columns),
            fixed(query_w.shape),
            pl.BlockSpec(memory_space=pl.ANY),
        ],
        [
            by_rows(IMG_LEN, width),
            by_rows(IMG_LEN, width),
            by_rows(IMG_LEN, columns),
            by_rows(text_rows, 2 * columns),
            by_rows(IMG_LEN, width),
            fixed((1, width)),
        ],
        outs,
        args,
        aliases={len(args): 4},
    )


def text_back(place, pair, key_w, value_w, rows, width):
    columns = key_w.shape[1]
    shards = width // columns
    blocks = key_w.shape[0] // width
    text_rows = pair.shape[0]
    cut = (shards, blocks, columns, columns)

    def kernel(place, grads, wk, wv, out):
        for k in range(blocks):
            part = contract(grads[:, :columns], wk[0, k], 1, 1) + contract(
                grads[:, columns:], wv[0, k], 1, 1
            )
            out[k * text_rows : (k + 1) * text_rows, :] = part.astype(BF16)
        out[blocks * text_rows :, :] = jnp.zeros((rows - blocks * text_rows, columns), BF16)

    weight = pl.BlockSpec((1, *cut[1:]), lambda i, *_: (i, 0, 0, 0))
    outs = [struct((2 * rows, width), BF16)]
    return call(
        "text_back",
        kernel,
        place,
        (shards,),
        [fixed(pair.shape), weight, weight],
        [pl.BlockSpec((rows, columns), lambda i, *_: (1, i))],
        outs,
        (pair, key_w.reshape(cut), value_w.reshape(cut)),
    )[0]


def self_backward(
    place, at, start, normed, scale, back, packed, grad, out_w, query, key, value, weights, room
):
    rows, width = normed.shape
    columns = query.shape[1]
    parts = IMG_LEN // columns

    def kernel(
        place, one, two, inv, dn, vec, g2, wo, q, k, v, wq, wk, wv, room, mine, low, triple, part, gain, held, lines
    ):
        i = pl.program_id(0)
        step, gain_step = norm_back(
            dn[...].astype(F32), two[...].astype(F32), inv[...], vec[2:3, :].astype(F32)
        )
        total = g2[...] + step
        held[...] = total
        mine[...] = held[:, pl.ds(pl.multiple_of(place[0] * columns, columns), columns)]
        y = total.astype(BF16)
        low[...] = y

        @pl.when(i == 0)
        def _():
            gain[...] = jnp.zeros_like(gain)
            lines[...] = jnp.zeros_like(lines)

        gain[...] += gain_step
        da = contract(y, wo[...], 1, 1).astype(BF16)
        query_grad, key_grad, value_grad = attend_back(da, q[...], k[...], v[...])
        triple[:, :columns] = query_grad
        triple[:, columns : 2 * columns] = key_grad
        triple[:, 2 * columns :] = value_grad
        partial = (
            contract(query_grad, wq[...], 1, 1)
            + contract(key_grad, wk[...], 1, 1)
            + contract(value_grad, wv[...], 1, 1)
        )
        sent = partial.astype(BF16)
        part[pl.ds(pl.multiple_of(i * IMG_LEN, IMG_LEN), IMG_LEN), :] = sent
        first = contract(vec[...], sent, 1, 1)[1:2, :]
        weighted = (partial * one[...].astype(F32)).astype(BF16)
        second = contract(jnp.ones((PAD, width), BF16), weighted, 1, 1)[0:1, :]
        for stat, line in enumerate((first, second)):
            for k in range(parts):
                piece = line[:, k * columns : (k + 1) * columns]
                lines[pl.ds((2 * i + stat) * parts + k, 1), :] = jnp.concatenate(
                    [piece] * (width // columns), axis=1
                )

        @pl.when(i == pl.num_programs(0) - 1)
        def _():
            part[rows:, :] = lines[...].astype(BF16)

    outs = [
        struct((rows, columns), F32),
        struct((rows, width), BF16),
        struct((rows, 3 * columns), BF16),
        struct(room.shape, BF16),
        struct((1, width), F32),
    ]
    args = (start, normed, scale, back, packed, grad, out_w, query, key, value, *weights, room)
    return call(
        "self_backward",
        kernel,
        place,
        (rows // IMG_LEN,),
        [
            turned_rows(IMG_LEN, width),
            by_rows(IMG_LEN, width),
            by_rows(IMG_LEN, 1),
            by_rows(IMG_LEN, width),
            fixed((PAD, width), at.vec // PAD),
            by_rows(IMG_LEN, width),
            fixed(out_w.shape),
        ]
        + [by_rows(IMG_LEN, columns)] * 3
        + [fixed(w.shape) for w in weights]
        + [pl.BlockSpec(memory_space=pl.ANY)],
        [
            by_rows(IMG_LEN, columns),
            by_rows(IMG_LEN, width),
            turned_rows(IMG_LEN, 3 * columns),
            fixed((rows + PAD, width)),
            fixed((1, width)),
        ],
        outs,
        args,
        scratch=[pltpu.VMEM((IMG_LEN, width), F32), pltpu.VMEM((PAD, width), F32)],
        aliases={len(args): 3},
    )


def self_end(place, mask, tokens, position_embed, vectors, stats, back, grad, gains, width):
    rows, columns = tokens.shape
    images = rows // IMG_LEN
    parts = IMG_LEN // columns

    def kernel(place, mask, tok, pos, vec, stat, tot, dn, g1, cross, feed, out, small):
        i = pl.program_id(0)
        masked = mask[...] > 0.0
        stream = first_stream(mask, tok, pos, vec)
        normal = (stream - stat[:, 0:1]) * stat[:, 1:2]
        normed_grad = dn[...].astype(F32)
        scaled = normed_grad * vec[1:2, :].astype(F32)
        line = lax.broadcasted_iota(jnp.int32, (PAD, 128), 0)
        lane = lax.broadcasted_iota(jnp.int32, (PAD, 128), 1)
        turned = [
            contract(
                tot[...],
                ((line == (2 * i + lane) * parts + k) & (lane < 2)).astype(F32).astype(BF16),
                0,
                0,
            )
            for k in range(parts)
        ]
        sums = jnp.concatenate(turned, axis=0) * (1.0 / width)
        total = g1[...] + stat[:, 1:2] * (scaled - sums[:, 0:1] - normal * sums[:, 1:2])
        out[...] = jnp.where(masked, 0.0, total).astype(BF16)

        @pl.when(i == 0)
        def _():
            small[...] = jnp.zeros_like(small)
            small[IMG_LEN + 2 : IMG_LEN + 3, :] = cross[...]
            small[IMG_LEN + 3 : IMG_LEN + 4, :] = feed[...]

        small[:IMG_LEN, :] += total
        small[IMG_LEN : IMG_LEN + 1, :] += jnp.sum(
            jnp.where(masked, total, 0.0), axis=0, keepdims=True
        )
        small[IMG_LEN + 1 : IMG_LEN + 2, :] += jnp.sum(normed_grad * normal, axis=0, keepdims=True)

    outs = [struct((rows, columns), BF16), struct((IMG_LEN + PAD, columns), F32)]
    own = pl.BlockSpec((1, columns), lambda i, place: (0, place[0]))
    return call(
        "self_end",
        kernel,
        place,
        (images,),
        [
            by_rows(IMG_LEN, 1),
            by_rows(IMG_LEN, columns),
            fixed((IMG_LEN, columns)),
            fixed((PAD, columns)),
            by_rows(IMG_LEN, 2),
            fixed((PAD, columns), rows // PAD),
            by_rows(IMG_LEN, columns),
            by_rows(IMG_LEN, columns),
            own,
            own,
        ],
        [by_rows(IMG_LEN, columns), fixed((IMG_LEN + PAD, columns))],
        outs,
        (mask, tokens, position_embed, vectors, stats, back, back, grad, *gains),
    )


def grad_sum(name, place, left_groups, right_groups, splits, block, spans):
    lefts, rights, terms = [], [], []
    for left_group, right_group in zip(left_groups, right_groups):
        left_base, right_base = len(lefts), len(rights)
        lefts += [p if isinstance(p, tuple) else (p, p.shape[0], None) for p, at in left_group]
        rights += [p if isinstance(p, tuple) else (p, p.shape[0], None) for p, at in right_group]
        for i, (_, left_at) in enumerate(left_group):
            for j, (_, right_at) in enumerate(right_group):
                left_rows, right_rows = lefts[left_base + i][1], rights[right_base + j][1]
                low = max(left_at, right_at)
                high = min(left_at + left_rows, right_at + right_rows)
                if low < high:
                    terms.append(
                        (left_base + i, low - left_at, right_base + j, low - right_at, high - low)
                    )
    (left_turn, height), (right_turn, width) = spans
    block = min(block, height)
    left_turn = left_turn * (height // block)
    left_count, right_count = len(lefts), len(rights)

    def kernel(place, *refs):
        left_refs = refs[:left_count]
        right_refs = refs[left_count : left_count + right_count]
        outs = refs[left_count + right_count :]
        total = None
        for li, left_row, ri, right_row, rows in terms:
            part = contract(
                left_refs[li][left_row : left_row + rows, :],
                right_refs[ri][right_row : right_row + rows, :],
                0,
                0,
            )
            total = part if total is None else total + part
        at = 0
        for out in outs:
            out[...] = total[:, at : at + out.shape[1]]
            at += out.shape[1]

    def spec(rows, wide, col, turn):
        return pl.BlockSpec(
            (rows, wide), lambda i, place: (0 if turn is None else turn(place), col(i))
        )

    outs = [struct((height, n), F32) for n in splits]
    return call(
        name,
        kernel,
        place,
        (height // block,),
        [spec(rows, block, lambda i: left_turn + i, turn) for _, rows, turn in lefts]
        + [spec(rows, width, lambda i: right_turn, turn) for _, rows, turn in rights],
        [pl.BlockSpec((block, n), lambda i, *_: (i, 0)) for n in splits],
        outs,
        [a for a, _, _ in (*lefts, *rights)],
    )


def text_grads(place, at, text, pair, text_groups, pair_groups, blocks):
    width = text.shape[1]
    text_rows = pair.shape[0]
    columns = pair.shape[1] // 2
    shards = width // columns
    step = min(4, shards)
    core_split = square_batch()
    pieces, rights, terms = [], [pair], []
    for text_group, pair_group in zip(text_groups, pair_groups):
        rights.append(pair_group[0][0])
        for piece, row in text_group:
            pieces.append(piece)
            terms.append((row // text_rows, row % text_rows, len(rights) - 1))
    if not core_split:
        pieces, terms = [], []
        for k, text_group in enumerate(text_groups):
            for b in range(blocks):
                pieces.append(text_group[0][0][b * text_rows : (b + 1) * text_rows])
                terms.append((b, 0, k + 1))

    def which(s, place):
        return (s + place[0] % 2) % 2 if core_split else s

    def kernel(place, own, *refs):
        piece_refs = refs[: len(pieces)]
        right_refs = refs[len(pieces) : len(pieces) + len(rights)]
        key, value = refs[len(pieces) + len(rights) :]

        def run(s):
            total = contract(own[...], right_refs[0][...], 0, 0)
            for ref, (turn, row, k) in zip(piece_refs, terms):
                if turn == s:
                    total = total + contract(
                        ref[...], right_refs[k][row : row + ref.shape[0], :], 0, 0
                    )
            for t in range(step):
                rows = slice(t * columns, (t + 1) * columns)
                key[t, 0] = total[rows, :columns]
                value[t, 0] = total[rows, columns:]

        for s in range(blocks):
            pl.when(pl.program_id(0) == s)(lambda s=s: run(s))

    last = shards // step - 1

    def piece_spec(piece, turn):
        return pl.BlockSpec(
            (piece.shape[0], step * columns),
            lambda s, t, place: (0, jnp.where(s == turn, t, jnp.where(s > turn, last, 0))),
        )

    outs = [struct((shards, blocks, columns, columns), F32)] * 2
    out_spec = pl.BlockSpec(
        (step, 1, columns, columns), lambda s, t, place: (t, which(s, place), 0, 0)
    )
    key, value = call(
        "text_grads",
        kernel,
        place,
        (blocks, shards // step),
        [
            pl.BlockSpec(
                (text_rows, step * columns), lambda s, t, place: (at.text // text_rows + which(s, place), t)
            )
        ]
        + [piece_spec(p, term[0]) for p, term in zip(pieces, terms)]
        + [pl.BlockSpec(r.shape, lambda s, t, place: (0, 0)) for r in rights],
        [out_spec] * 2,
        outs,
        (text, *pieces, *rights),
    )
    return key.reshape(-1, columns), value.reshape(-1, columns)


class Plan:
    def __init__(self):
        self.makers, self.made = {}, {}

    def job(self, name, make):
        self.makers[name] = make

    def get(self, name):
        if name not in self.made:
            self.made[name] = self.makers[name]()
        return self.made[name]

    def behind(self, name, value):
        others = [self.get(n) for n in AFTER.get(name, ())]
        return tie(value, *others)[0] if others else value

    def tie(self, point, value):
        names = [n for n in self.makers if DONE_BY.get(n) == point]
        if not names:
            return value
        value, *done = tie(value, *[self.get(n) for n in names])
        self.made.update(zip(names, done))
        return value


class BatchSum:
    def __init__(self, name, place, products):
        self.name, self.place, self.products = name, place, products
        shapes = [
            (right.shape[1], left.shape[1]) if fold else (left.shape[1], right.shape[1])
            for left, right, fold in products
        ]
        if not square_batch():
            self.quarters = []
            return
        height, width = shapes[0]
        rows = height // 4

        def kernel(place, *refs):
            ins, outs, held = refs[: 2 * len(products)], refs[2 * len(products) : -1], refs[-1]
            for n, (_, _, fold) in enumerate(products):
                left, right = ins[2 * n], ins[2 * n + 1]
                if fold:
                    for at in range(0, width, height):
                        held[n, :, at : at + height] = contract(
                            left[:, at : at + height], right[...], 0, 0
                        ).astype(BF16)
                else:
                    held[n] = contract(left[...], right[...], 0, 0).astype(BF16)
                for k, out in enumerate(outs):
                    turn = pl.multiple_of((place[1] ^ k) * rows, rows)
                    out[n * rows : (n + 1) * rows, :] = held[n, pl.ds(turn, rows), :]

        args = [a for left, right, _ in products for a in (left, right)]
        outs = [struct((rows * len(products), width), BF16)] * 4
        self.quarters = call(
            name + "_parts",
            kernel,
            place,
            (1,),
            [fixed(a.shape) for a in args],
            [fixed(o.shape) for o in outs],
            outs,
            args,
            scratch=[pltpu.VMEM((len(products), height, width), BF16)],
        )
        self.height, self.width, self.rows = height, width, rows

    def step_one(self):
        if not square_batch():
            parts = [contract(left, right, 0, 0) for left, right, _ in self.products]
            return [lax.psum(p.astype(BF16), "batch") for p in parts]
        return [hop(self.sent[k - 1], k) for k in (1, 2, 3)]

    def step_two(self, held):
        if not square_batch():
            return held
        total = self.quarters[0].astype(F32)
        for moved in held:
            total = total + moved.astype(F32)
        low = total.astype(BF16)
        return [low] + [hop(low, k) for k in (1, 2, 3)]

    def finish(self, held):
        if not square_batch():
            return [h.astype(F32) for h in held]
        height, width, rows = self.height, self.width, self.rows
        folds = [fold for _, _, fold in self.products]

        def kernel(place, *refs):
            ins, outs = refs[:4], refs[4:]
            for n, (out, fold) in enumerate(zip(outs, folds)):
                for k, ref in enumerate(ins):
                    at = pl.multiple_of((place[1] ^ k) * rows, rows)
                    piece = ref[n * rows : (n + 1) * rows, :].astype(F32)
                    if fold:
                        for col in range(0, width, height):
                            out[pl.ds(col + at, rows), :] = piece[:, col : col + height]
                    else:
                        out[pl.ds(at, rows), :] = piece

        outs = [struct((width, height) if fold else (height, width), F32) for fold in folds]
        return call(
            self.name + "_finish",
            kernel,
            self.place,
            (1,),
            [fixed(a.shape) for a in held],
            [fixed(o.shape) for o in outs],
            outs,
            held,
        )


def body(
    tokens,
    captions,
    mask_counts,
    mask_positions,
    cotangent,
    mask_embed,
    position_embed,
    norm_self,
    query_self,
    key_self,
    value_self,
    out_self,
    norm_cross,
    query_cross,
    key_text,
    value_text,
    out_cross,
    norm_feed,
    up_weight,
    down_weight,
):
    rows, columns = tokens.shape
    width, hidden = query_self.shape[0], up_weight.shape[1]
    text_rows, text_blocks = captions.shape[0], captions.shape[1] // columns
    at = Packed(rows, text_rows * text_blocks)
    place = jnp.stack([lax.axis_index("tensor"), lax.axis_index("batch")]).astype(jnp.int32)
    core = place[0] % 2
    shared = square_batch()
    packed, vectors, mask = pack_rows(
        at,
        mask_counts,
        mask_positions,
        tokens,
        captions,
        cotangent,
        position_embed,
        (mask_embed, norm_self, norm_cross, norm_feed),
    )
    packed = gather_cols(packed)

    text_part, seed_part = packed[at.text : at.seed], packed[at.seed : at.vec]
    if shared:
        text_part = lax.dynamic_slice_in_dim(packed, at.text + core * text_rows, text_rows, 0)
        seed_part = lax.dynamic_slice_in_dim(packed, at.seed + core * IMG_LEN, IMG_LEN, 0)
    else:
        seed_part = jnp.concatenate(
            [
                lax.dynamic_slice_in_dim(seed_part, core * IMG_LEN, IMG_LEN, 0),
                lax.dynamic_slice_in_dim(seed_part, (1 - core) * IMG_LEN, IMG_LEN, 0),
            ],
            axis=0,
        )
    plan = Plan()

    def spread(name, source, shared):
        move = Spread(None, shared)

        def one():
            move.array = plan.behind(name + "1", source())
            return direct(move.array) if name in DIRECT else move.step_one()

        def two():
            held = plan.get(name + "1")
            return held if name in DIRECT else move.step_two(held)

        plan.job(name + "1", one)
        plan.job(name + "2", two)
        plan.job(name + "3", lambda: move.swap(plan.get(name + "2")))

    normed_self, query_one, key_one, value_one, mixed_self, partial, stats = self_forward(
        place, at, mask, packed, query_self, key_self, value_self, out_self
    )
    spread("T", lambda: text_part, shared)
    spread("X", lambda: normed_self[:IMG_LEN] if shared else normed_self, shared)
    spread("Y", lambda: seed_part, shared)
    plan.job("KV", lambda: text_project(place, at, packed, key_text, value_text))
    plan.job("DA", lambda: seed_product(place, at, packed, down_weight))
    scattered = plan.tie("scattered1", scatter_cols(partial))
    mixed_out = plan.tie("mixed1", gather_cols(scattered))
    key_two, value_two = plan.get("KV")

    stream_one, normed_cross, query_two, mixed_cross, partial, scale_cross = cross_forward(
        place, at, mask, packed, mixed_out, query_cross, key_two, value_two, out_cross
    )
    partial = plan.tie("partial2", partial)
    scattered = plan.tie("scattered2", scatter_cols(partial))
    mixed_out = plan.tie("mixed2", gather_cols(scattered))

    own_two, scale_feed, normed_feed, activation, hidden_grad, partial = feed_both(
        place, at, stream_one, mixed_out, packed, plan.get("DA"), up_weight
    )
    spread("F", lambda: normed_feed[:IMG_LEN] if shared else normed_feed, shared)
    spread("A", lambda: activation, False)
    spread("U", lambda: hidden_grad, False)
    plan.job("OUT", lambda: out_product(place, plan.behind("OUT", activation), down_weight))
    partial = plan.tie("partial3", partial)
    scattered = plan.tie("scattered3", scatter_cols(partial))
    feed_back = plan.tie("mixed3", gather_cols(scattered))

    grad_two, seed_cross, query_grad, pair, partial, feed_gain = cross_backward(
        place,
        at,
        normed_feed,
        scale_feed,
        feed_back,
        packed,
        packed,
        out_cross,
        query_two,
        key_two,
        value_two,
        query_cross,
        plan.get("OUT"),
    )
    own_seed = [
        ((packed, IMG_LEN, lambda p: at.seed // IMG_LEN + p[0] % 2), 0),
        ((packed, IMG_LEN, lambda p: at.seed // IMG_LEN + 1 - p[0] % 2), IMG_LEN),
    ]
    plan.job(
        "GD",
        lambda: grad_sum(
            "down_grads",
            place,
            [[(plan.behind("GD", activation), 0)], *plan.get("A2")],
            [own_seed, *plan.get("Y3")],
            (width,),
            256,
            ((0, hidden), (0, width)),
        ),
    )
    plan.job(
        "GU",
        lambda: grad_sum(
            "up_grads",
            place,
            [[(plan.behind("GU", normed_feed), 0)], *plan.get("F3")],
            [[(hidden_grad, 0)], *plan.get("U2")],
            (hidden,),
            512,
            ((0, width), (0, hidden)),
        ),
    )
    cross_sum = BatchSum(
        "cross", place, [(mixed_cross, seed_cross, False), (normed_cross, query_grad, True)]
    )

    def batch_sum(name, total):
        plan.job(name + "0", lambda: total.quarters)

        def one():
            total.sent = plan.behind(name + "1", plan.get(name + "0")[1:])
            return total.step_one()

        plan.job(name + "1", one)
        plan.job(name + "2", lambda: total.step_two(plan.behind(name + "2", plan.get(name + "1"))))

    batch_sum("C", cross_sum)
    plan.job(
        "TB",
        lambda: text_back(
            place, plan.behind("TB", pair), key_text, value_text, rows + PAD, width
        ),
    )
    plan.job("D", lambda: direct(plan.behind("D", pair)))
    plan.job(
        "GT",
        lambda: text_grads(
            place,
            at,
            packed,
            plan.behind("GT", pair),
            plan.get("T3"),
            plan.get("D"),
            text_blocks,
        ),
    )
    partial = plan.tie("partial4", partial)
    scattered = plan.tie("scattered4", scatter_cols(partial))
    out_slice = scattered[rows:]
    cross_back = plan.tie("mixed4", gather_cols(scattered[:rows]))

    own_one, seed_self, triple, partial, cross_gain = self_backward(
        place,
        at,
        normed_self,
        normed_cross,
        scale_cross,
        cross_back,
        packed,
        grad_two,
        out_self,
        query_one,
        key_one,
        value_one,
        (query_self, key_self, value_self),
        plan.get("TB"),
    )
    layer_out = (own_two + out_slice.astype(F32)).astype(BF16)
    self_sum = BatchSum("self", place, [(mixed_self, seed_self, False)])
    batch_sum("S", self_sum)
    spread("Q", lambda: triple, False)
    plan.job(
        "GQ",
        lambda: grad_sum(
            "self_grads",
            place,
            [[(plan.behind("GQ", normed_self), 0)], *plan.get("X3")],
            [[(triple, 0)], *plan.get("Q2")],
            (columns,) * 3,
            512,
            ((0, width), (0, 3 * columns)),
        ),
    )
    partial = plan.tie("partial5", partial)
    scattered = plan.tie("scattered5", scatter_cols(partial))
    low = rows + PAD
    captions_grad = jnp.concatenate(
        [
            scattered[low + k * text_rows : low + (k + 1) * text_rows]
            for k in range(text_blocks)
        ],
        axis=1,
    )
    tokens_grad, small = self_end(
        place,
        mask,
        tokens,
        position_embed,
        vectors,
        stats,
        scattered,
        own_one,
        (cross_gain, feed_gain),
        width,
    )
    small = plan.tie("small", small)
    small = direct_sum(small)
    (down_grad,) = plan.get("GD")
    (up_grad,) = plan.get("GU")
    key_text_grad, value_text_grad = plan.get("GT")
    query_self_grad, key_self_grad, value_self_grad = plan.get("GQ")
    out_cross_grad, query_cross_grad = cross_sum.finish(plan.get("C2"))
    (out_self_grad,) = self_sum.finish(plan.get("S2"))
    return (
        layer_out,
        tokens_grad,
        captions_grad,
        small[IMG_LEN],
        small[:IMG_LEN],
        small[IMG_LEN + 1],
        query_self_grad,
        key_self_grad,
        value_self_grad,
        out_self_grad,
        small[IMG_LEN + 2],
        query_cross_grad,
        key_text_grad,
        value_text_grad,
        out_cross_grad,
        small[IMG_LEN + 3],
        up_grad,
        down_grad,
    )


def solution(mesh):
    return jax.shard_map(
        body,
        mesh=mesh,
        in_specs=(
            P("batch", "tensor"),
            P("batch", "tensor"),
            P("batch"),
            P("batch", None),
            P("batch", "tensor"),
            P("tensor"),
            P(None, "tensor"),
            P("tensor"),
            P(None, "tensor"),
            P(None, "tensor"),
            P(None, "tensor"),
            P("tensor", None),
            P("tensor"),
            P(None, "tensor"),
            P(None, "tensor"),
            P(None, "tensor"),
            P("tensor", None),
            P("tensor"),
            P(None, "tensor"),
            P("tensor", None),
        ),
        out_specs=(
            P("batch", "tensor"),
            P("batch", "tensor"),
            P("batch", "tensor"),
            P("tensor"),
            P(None, "tensor"),
            P("tensor"),
            P(None, "tensor"),
            P(None, "tensor"),
            P(None, "tensor"),
            P("tensor", None),
            P("tensor"),
            P(None, "tensor"),
            P(None, "tensor"),
            P(None, "tensor"),
            P("tensor", None),
            P("tensor"),
            P(None, "tensor"),
            P("tensor", None),
        ),
        check_vma=False,
    )
```

time: 1320 us -> 563 us (0.43)
  waiting for transfers between devices: 920 us -> 274 us
  Pallas kernels: 0 us -> 172 us
  matrix products: 147 us -> 0 us
  blocking collectives: 130 us -> 0 us
  other arithmetic: 69.4 us -> 6.12 us
  starting transfers between devices: 2.32 us -> 61 us
    psum x1 -> x0, waiting for transfers between devices: 353 us -> none  [body(): lax.psum(position_grad.astype(jnp.bfloat16), 'batch').astype(jnp.float32)]
    reduce_scatter x9 -> x5, waiting for transfers between devices: 306 us -> 22.3 us  [scatter_cols(): return lax.psum_scatter(array, 'tensor', scatter_dimension=1, tiled=True)]
    pallas_call x0 -> x19, Pallas kernels: none -> 172 us  [the longest x18 170 us: call(): pl.pallas_call(kernel, grid_spec=pltpu.PrefetchScalarGridSpec(num_scalar_...]
    dot_general x52 -> x0, matrix products: 143 us -> none  [the longest x38 122 us: contract(): lax.dot_general(left, right, (((left_dim,), (right_dim,)), ((), ())), pre...]
    all_gather x11 -> x5, waiting for transfers between devices: 260 us -> 119 us  [gather_cols(): return lax.all_gather(array, 'tensor', axis=1, tiled=True)]
    ppermute x0 -> x62, waiting for transfers between devices: none -> 132 us  [the longest x46 128 us: hop(): return lax.ppermute(array, 'batch', pairs)]
    psum x9 -> x0, blocking collectives: 130 us -> none  [the longest x6 89.9 us: norm_forward(): lax.psum((jnp.sum(stream, axis=1), jnp.sum(stream * stream, axis=1)), 'te...]
    ppermute x0 -> x62, starting transfers between devices: none -> 60.2 us  [the longest x46 57.7 us: hop(): return lax.ppermute(array, 'batch', pairs)]
  transfers between devices with their start and end apart: 21 -> 72, of which waited for: 20 -> 28; matrix products, arithmetic and copies ran while one was open for 8% -> 3% of each run, Pallas kernels for 0% -> 29%
where the time goes in v1:
time: 563 us; the launch traced here: 555 us
  waiting for transfers between devices  274 us (49%)
  Pallas kernels  172 us (31%)
  starting transfers between devices  61 us (11%)
  local copies, waits for them, and re-layouts  27.3 us (5%)
  between operations  15.3 us (3%)
  other arithmetic  6.12 us (1%)
    pallas_call x18, Pallas kernels, call(): pl.pallas_call(kernel, grid_spec=pltpu.PrefetchScalarGridSpec(num_scalar_...  170 us
    ppermute x46, waiting for transfers between devices, hop(): return lax.ppermute(array, 'batch', pairs)  128 us
    all_gather x5, waiting for transfers between devices, gather_cols(): return lax.all_gather(array, 'tensor', axis=1, tiled=True)  119 us
    ppermute x46, starting transfers between devices, hop(): return lax.ppermute(array, 'batch', pairs)  57.7 us
    reduce_scatter x5, waiting for transfers between devices, scatter_cols(): return lax.psum_scatter(array, 'tensor', scatter_dimension=1, tiled=True)  22.3 us
    unnamed x108, local copies, waits for them, and re-layouts  12.5 us
  transfers between devices with their start and end apart: 72, of which 28 were waited for; matrix products, arithmetic and copies ran while one was open for 3% of the time, Pallas kernels for 29%

profile of v1, /device:TPU:0, one launch (start us, length us, event | category | flops | bytes accessed | tf_op | source)
XLA Modules:
  0.0 555.5 jit_solution(7990225822092521110)
XLA Ops:
  10.3 77.0 %all-gather.6.cloned.1.call-done.tok.pos.vec.refs_0_.refs_1_.seed.g3.refs_5_.refs_6_.own = bf16[1808,2048]{1,0:T(8,128)(2,1)} async-done(((bf16[1808,256]{1,0:T(8,128)(2,1)}), bf16[1808,2048]{1,0:T(8,128)(2,1)}) %all-gather.6.cloned.1.call-update) | async-done | bytes 7405584 | tf_op jit(solution)/shard_map/all_gather | solution.py:34
  87.3 10.6 %self_forward.1 = (bf16[512,2048]{1,0:T(8,128)(2,1)}, bf16[512,256]{1,0:T(8,128)(2,1)}, bf16[512,256]{1,0:T(8,128)(2,1)}, bf16[512,256]{1,0:T(8,128)(2,1)}, bf16...) custom-call(s32[2]{0:T(128)} %pad_add_fusion.place, f32[512,1]{1,0:T(8,128)} %get-tuple-element.169.mask, ...), custom_call_target="tpu_custom_call" | custom-call | flops 1000 | bytes 17001000 | tf_op jit(solution)/shard_map/self_forward/pallas_call | solution.py:135
  103.7 5.1 text_project.1
  108.8 17.3 %collective-permute-done.1.refs_2_ = bf16[256,2048]{1,0:T(8,128)(2,1)S(1)} collective-permute-done((bf16[256,2048]{1,0:T(8,128)(2,1)S(1)}, bf16[256,2048]{1,0:T(8,128)(2,1)S(1)}, u32[]{:S(2)}, u32[]{:S(2)}) %collective-permute-start.1) | collective-permute-done | bytes 1048608 | tf_op jit(solution)/shard_map/ppermute | solution.py:47
  127.4 4.5 reduce-scatter.6.cloned.1.call-done
  136.0 27.3 %all-gather.8.cloned.1.call-done.add = bf16[512,2048]{1,0:T(8,128)(2,1)} async-done(((bf16[512,256]{1,0:T(8,128)(2,1)}), bf16[512,2048]{1,0:T(8,128)(2,1)}) %all-gather.8.cloned.1.call-update) | async-done | bytes 2097168 | tf_op jit(solution)/shard_map/all_gather | solution.py:34
  163.2 9.9 %cross_forward.1 = (f32[512,2048]{1,0:T(8,128)}, bf16[512,2048]{1,0:T(8,128)(2,1)}, bf16[512,256]{1,0:T(8,128)(2,1)}, bf16[512,256]{1,0:T(8,128)(2,1)}, bf16[512,2048]{1,0:T(8,128)(2,1)}, /*index=5*/f32[512,1]{1,0:T(8,128)}) custom-call(s32[2]{0:T(128)} %pad_add_fusion.place, f32[512,1]{1,0:T(8,128)} %get-tuple-element.169.mask, ...), custom_call_target="tpu_custom_call" | custom-call | flops 1000 | bytes 1000 | tf_op jit(solution)/shard_map/cross_forward/pallas_call | solution.py:135
  177.7 9.7 %collective-permute-done.5.refs_5_ = bf16[128,2048]{1,0:T(8,128)(2,1)S(1)} collective-permute-done((bf16[128,2048]{1,0:T(8,128)(2,1)S(1)}, bf16[128,2048]{1,0:T(8,128)(2,1)S(1)}, u32[]{:S(2)}, u32[]{:S(2)}) %collective-permute-start.5) | collective-permute-done | bytes 524320 | tf_op jit(solution)/shard_map/ppermute | solution.py:47
  193.5 6.8 %seed_product.1.dact = f32[512,1024]{1,0:T(8,128)} custom-call(s32[2]{0:T(128)} %pad_add_fusion.place, bf16[1808,2048]{1,0:T(8,128)(2,1)} %all-gather.6.cloned.1.call-done.tok.pos.vec.refs_0_.refs_1_.seed.g3.refs_5_.refs_6_.own, bf16[1024,2048]{1,0:T(8,128)(2,1)} %down.3), custom_call_target="tpu_custom_call" | custom-call | flops 1000 | bytes 12001000 | tf_op jit(solution)/shard_map/seed_product/pallas_call | solution.py:135
  201.5 4.2 collective-permute-done.11.refs_6_
  211.8 20.1 %collective-permute-done.17.refs_9_ = bf16[256,2048]{1,0:T(8,128)(2,1)S(1)} collective-permute-done((bf16[256,2048]{1,0:T(8,128)(2,1)}, bf16[256,2048]{1,0:T(8,128)(2,1)S(1)}, u32[]{:S(2)}, u32[]{:S(2)}) %collective-permute-start.17) | collective-permute-done | bytes 1048608 | tf_op jit(solution)/shard_map/ppermute | solution.py:47
  239.2 13.0 %feed_both.1 = (f32[512,256]{1,0:T(8,128)}, f32[512,1]{1,0:T(8,128)}, bf16[512,2048]{1,0:T(8,128)(2,1)}, bf16[512,1024]{1,0:T(8,128)(2,1)}, bf16[512,1024]{1,0:T(8,128)(2,1)}, /*index=5*/bf16[512,2048]{1,0:T(8,128)(2,1)}) custom-call(s32[2]{0:T(128)} %pad_add_fusion.place, f32[512,2048]{1,0:T(8,128)} %get-tuple-element.177.one, ...), custom_call_target="tpu_custom_call" | custom-call | flops 1000 | bytes 6001000 | tf_op jit(solution)/shard_map/feed_both/pallas_call | solution.py:135
  261.0 18.3 %collective-permute-done.25.refs_3_ = bf16[256,2048]{1,0:T(8,128)(2,1)S(1)} collective-permute-done((bf16[256,2048]{1,0:T(8,128)(2,1)S(1)}, bf16[256,2048]{1,0:T(8,128)(2,1)S(1)}, u32[]{:S(2)}, u32[]{:S(2)}) %collective-permute-start.25) | collective-permute-done | bytes 1048608 | tf_op jit(solution)/shard_map/ppermute | solution.py:47
  280.3 6.8 %reduce-scatter.10.cloned.1.call-done = bf16[512,256]{1,0:T(8,128)(2,1)} async-done(((bf16[512,2048]{1,0:T(8,128)(2,1)}), bf16[512,256]{1,0:T(8,128)(2,1)}) %reduce-scatter.10.cloned.1.call-update) | async-done | bytes 262160 | tf_op jit(solution)/shard_map/reduce_scatter | solution.py:38
  290.4 8.0 %collective-permute-done.27.refs_6_ = bf16[128,2048]{1,0:T(8,128)(2,1)S(1)} collective-permute-done((bf16[128,2048]{1,0:T(8,128)(2,1)S(1)}, bf16[128,2048]{1,0:T(8,128)(2,1)S(1)}, u32[]{:S(2)}, u32[]{:S(2)}) %collective-permute-start.27) | collective-permute-done | bytes 524320 | tf_op jit(solution)/shard_map/ppermute | solution.py:47
  301.7 6.6 %out_product.1.room = bf16[1024,2048]{1,0:T(8,128)(2,1)} custom-call(s32[2]{0:T(128)} %pad_add_fusion.place, bf16[512,1024]{1,0:T(8,128)(2,1)} %get-tuple-element.207.act.refs_0_, bf16[1024,2048]{1,0:T(8,128)(2,1)} %down.3), custom_call_target="tpu_custom_call" | custom-call | flops 1000 | bytes 15001000 | tf_op jit(solution)/shard_map/out_product/pallas_call | solution.py:135
  310.1 8.2 %all-gather.12.cloned.1.call-done.dn = bf16[512,2048]{1,0:T(8,128)(2,1)} async-done(((bf16[512,256]{1,0:T(8,128)(2,1)}), bf16[512,2048]{1,0:T(8,128)(2,1)}) %all-gather.12.cloned.1.call-update) | async-done | bytes 2097168 | tf_op jit(solution)/shard_map/all_gather | solution.py:34
  318.3 11.8 %cross_backward.1 = (f32[512,2048]{1,0:T(8,128)}, bf16[512,2048]{1,0:T(8,128)(2,1)}, bf16[512,256]{1,0:T(8,128)(2,1)}, bf16[256,512]{1,0:T(8,128)(2,1)}, bf16[1024,2048]{1,0:T(8,128)(2,1)}, /*index=5*/f32[1,2048]{1,0:T(1,128)}) custom-call(s32[2]{0:T(128)} %pad_add_fusion.place, ...), custom_call_target="tpu_custom_call", output_to_operand_aliasing={{4}: (11, {})} | custom-call | flops 1000 | bytes 20001000 | tf_op jit(solution)/shard_map/cross_backward/pallas_call | solution.py:135
  335.1 5.6 %cross_parts.1 = (bf16[128,2048]{1,0:T(8,128)(2,1)}, bf16[128,2048]{1,0:T(8,128)(2,1)}, bf16[128,2048]{1,0:T(8,128)(2,1)}, bf16[128,2048]{1,0:T(8,128)(2,1)}) custom-call(s32[2]{0:T(128)} %pad_add_fusion.place, bf16[512,256]{1,0:T(8,128)(2,1)} %get-tuple-element.212.refs_0_, bf16[512,2048]{1,0:T(8,128)(2,1)} %get-tuple-element.213.refs_1_, ...), custom_call_target="tpu_custom_call" | custom-call | flops 1000 | bytes 7001000 | tf_op jit(solution)/shard_map/cross_parts/pallas_call | solution.py:135
  344.3 8.1 %text_back.1.room = bf16[1056,2048]{1,0:T(8,128)(2,1)} custom-call(s32[2]{0:T(128)} %pad_add_fusion.place, bf16[256,512]{1,0:T(8,128)(2,1)} %get-tuple-element.270.grads.refs_8_, bf16[8,2,256,256]{3,2,1,0:T(8,128)(2,1)} %bitcast.11, bf16[8,2,256,256]{3,2,1,0:T(8,128)(2,1)} %bitcast.13), custom_call_target="tpu_custom_call" | custom-call | flops 1000 | bytes 8001000 | tf_op jit(solution)/shard_map/text_back/pallas_call | solution.py:135
  352.4 6.1 %collective-permute-done.36 = bf16[128,2048]{1,0:T(8,128)(2,1)} collective-permute-done((bf16[128,2048]{1,0:T(8,128)(2,1)}, bf16[128,2048]{1,0:T(8,128)(2,1)}, u32[]{:S(2)}, u32[]{:S(2)}) %collective-permute-start.36) | collective-permute-done | bytes 524320 | tf_op jit(solution)/shard_map/ppermute | solution.py:47
  358.6 11.5 %collective-permute-done.37 = bf16[128,2048]{1,0:T(8,128)(2,1)} collective-permute-done((bf16[128,2048]{1,0:T(8,128)(2,1)}, bf16[128,2048]{1,0:T(8,128)(2,1)}, u32[]{:S(2)}, u32[]{:S(2)}) %collective-permute-start.37) | collective-permute-done | bytes 524320 | tf_op jit(solution)/shard_map/ppermute | solution.py:47
  370.0 9.4 %reduce-scatter.12.cloned.1.call-done = bf16[1024,256]{1,0:T(8,128)(2,1)} async-done(((bf16[1024,2048]{1,0:T(8,128)(2,1)}), bf16[1024,256]{1,0:T(8,128)(2,1)}) %reduce-scatter.12.cloned.1.call-update) | async-done | bytes 524304 | tf_op jit(solution)/shard_map/reduce_scatter | solution.py:38
  384.4 17.8 %down_grads.1 = f32[1024,2048]{1,0:T(8,128)} custom-call(s32[2]{0:T(128)} %pad_add_fusion.place, bf16[512,1024]{1,0:T(8,128)(2,1)} %get-tuple-element.207.act.refs_0_, bf16[512,1024]{1,0:T(8,128)(2,1)} %collective-permute-done.32.refs_1_, bf16[512,1024]{1,0:T(8,128)(2,1)} %collective-permute-done.33.refs_2_, ...), custom_call_target="tpu_custom_call" | custom-call | flops 1000 | bytes 17001000 | tf_op jit(solution)/shard_map/down_grads/pallas_call | solution.py:135
  405.4 5.2 all-gather.14.cloned.1.call-done.dn
  416.9 16.4 %self_backward.1 = (f32[512,256]{1,0:T(8,128)}, bf16[512,2048]{1,0:T(8,128)(2,1)}, bf16[512,768]{1,0:T(8,128)(2,1)}, bf16[1056,2048]{1,0:T(8,128)(2,1)}, f32[1,2048]{1,0:T(1,128)}) custom-call(s32[2]{0:T(128)} %pad_add_fusion.place, bf16[512,2048]{1,0:T(8,128)(2,1)} %get-tuple-element.295.one.refs_0_, ...), custom_call_target="tpu_custom_call", output_to_operand_aliasing={{3}: (14, {})} | custom-call | flops 1000 | bytes 27001000 | tf_op jit(solution)/shard_map/self_backward/pallas_call | solution.py:135
  434.9 16.8 %up_grads.1 = f32[2048,1024]{1,0:T(8,128)} custom-call(s32[2]{0:T(128)} %pad_add_fusion.place, bf16[512,2048]{1,0:T(8,128)(2,1)} %get-tuple-element.193.three.refs_0_, bf16[256,2048]{1,0:T(8,128)(2,1)} %copy-done.9, bf16[256,2048]{1,0:T(8,128)(2,1)} %copy-done.21, bf16[256,2048]{1,0:T(8,128)(2,1)} %copy-done.8, ...), custom_call_target="tpu_custom_call" | custom-call | flops 1000 | bytes 14001000 | tf_op jit(solution)/shard_map/up_grads/pallas_call | solution.py:135
  455.7 16.9 %collective-permute-done.47.refs_11_ = bf16[512,768]{1,0:T(8,128)(2,1)S(1)} collective-permute-done((bf16[512,768]{1,0:T(8,128)(2,1)S(1)}, bf16[512,768]{1,0:T(8,128)(2,1)S(1)}, u32[]{:S(2)}, u32[]{:S(2)}) %collective-permute-start.47) | collective-permute-done | bytes 786464 | tf_op jit(solution)/shard_map/ppermute | solution.py:47
  490.4 11.8 %text_grads.1 = (f32[8,2,256,256]{3,2,1,0:T(8,128)}, f32[8,2,256,256]{3,2,1,0:T(8,128)}) custom-call(s32[2]{0:T(128)} %pad_add_fusion.place, bf16[1808,2048]{1,0:T(8,128)(2,1)} %all-gather.6.cloned.1.call-done.tok.pos.vec.refs_0_.refs_1_.seed.g3.refs_5_.refs_6_.own, bf16[256,2048]{1,0:T(8,128)(2,1)} %collective-permute-done.refs_0_, ...), custom_call_target="tpu_custom_call" | custom-call | flops 1000 | bytes 15001000 | tf_op jit(solution)/shard_map/text_grads/pallas_call | solution.py:135
  502.9 5.2 collective-permute-done.51
  508.1 13.7 %self_grads.1 = (f32[2048,256]{1,0:T(8,128)}, f32[2048,256]{1,0:T(8,128)}, f32[2048,256]{1,0:T(8,128)}) custom-call(s32[2]{0:T(128)} %pad_add_fusion.place, bf16[512,2048]{1,0:T(8,128)(2,1)} %get-tuple-element.295.one.refs_0_, bf16[256,2048]{1,0:T(8,128)(2,1)} %copy-done.4, bf16[256,2048]{1,0:T(8,128)(2,1)} %copy-done.19, bf16[256,2048]{1,0:T(8,128)(2,1)} %copy-done.3, ...), custom_call_target="tpu_custom_call" | custom-call | flops 1000 | bytes 40001000 | tf_op jit(solution)/shard_map/self_grads/pallas_call | solution.py:135
  528.8 4.5 cross_finish.1
  (277 shorter events, 125.8 us)
Async XLA Ops:
  7.2 80.1 %all-gather.6.cloned.1.call-start = ((), (), s32[]{:S(2)}) async-start(), calls=%async_computation.5 | async-start | bytes 8331264 | tf_op jit(solution)/shard_map/all_gather | solution.py:34
  9.6 122.3 %reduce-scatter.6.cloned.1.call-start = ((), (), s32[]{:S(2)}) async-start(), calls=%async_computation.6 | async-start | bytes 2359296 | tf_op jit(solution)/shard_map/reduce_scatter | solution.py:38
  98.0 65.3 %all-gather.8.cloned.1.call-start = ((), (), s32[]{:S(2)}) async-start(), calls=%async_computation.7 | async-start | bytes 2359296 | tf_op jit(solution)/shard_map/all_gather | solution.py:34
  100.8 25.3 %collective-permute-start.1 = (bf16[256,2048]{1,0:T(8,128)(2,1)S(1)}, bf16[256,2048]{1,0:T(8,128)(2,1)S(1)}, u32[]{:S(2)}, u32[]{:S(2)}) collective-permute-start(bf16[256,2048]{1,0:T(8,128)(2,1)S(1)} %get-tuple-element.321), channel_id=1, source_target_pairs={{0,16},{8,24},{16,0},{24,8},{1,17},{9,25},{17,1},{25,9},{2,18},{10... | collective-permute-start | bytes 3145736 | tf_op jit(solution)/shard_map/ppermute | solution.py:47
  102.3 25.2 %collective-permute-start = (bf16[256,2048]{1,0:T(8,128)(2,1)S(1)}, bf16[256,2048]{1,0:T(8,128)(2,1)}, u32[]{:S(2)}, u32[]{:S(2)}) collective-permute-start(bf16[256,2048]{1,0:T(8,128)(2,1)S(1)} %get-tuple-element.321), channel_id=1, source_target_pairs={{0,8},{8,0},{16,24},{24,16},{1,9},{9,1},{17,25},{25,17},{2,10},{10... | collective-permute-start | bytes 3145736 | tf_op jit(solution)/shard_map/ppermute | solution.py:47
  132.0 76.2 %reduce-scatter.8.cloned.1.call-start = ((), (), s32[]{:S(2)}) async-start(), calls=%async_computation.8 | async-start | bytes 2359296 | tf_op jit(solution)/shard_map/reduce_scatter | solution.py:38
  133.1 40.1 %collective-permute-start.3 = (bf16[256,2048]{1,0:T(8,128)(2,1)}, bf16[256,2048]{1,0:T(8,128)(2,1)S(1)}, u32[]{:S(2)}, u32[]{:S(2)}) collective-permute-start(bf16[256,2048]{1,0:T(8,128)(2,1)} %slice.75), channel_id=1, source_target_pairs={{0,16},{8,24},{16,0},{24,8},{1,17},{9,25},{17,1},{25,9},{2,18},{10... | collective-permute-start | bytes 3145736 | tf_op jit(solution)/shard_map/ppermute | solution.py:47
  134.5 38.7 %collective-permute-start.2 = (bf16[256,2048]{1,0:T(8,128)(2,1)}, bf16[256,2048]{1,0:T(8,128)(2,1)S(1)}, u32[]{:S(2)}, u32[]{:S(2)}) collective-permute-start(bf16[256,2048]{1,0:T(8,128)(2,1)} %slice.75), channel_id=1, source_target_pairs={{0,8},{8,0},{16,24},{24,16},{1,9},{9,1},{17,25},{25,17},{2,10},{10... | collective-permute-start | bytes 3145736 | tf_op jit(solution)/shard_map/ppermute | solution.py:47
  173.2 66.0 %all-gather.10.cloned.1.call-start = ((), (), s32[]{:S(2)}) async-start(), calls=%async_computation.9 | async-start | bytes 2359296 | tf_op jit(solution)/shard_map/all_gather | solution.py:34
  208.2 79.0 %reduce-scatter.10.cloned.1.call-start = ((), (), s32[]{:S(2)}) async-start(), calls=%async_computation.10 | async-start | bytes 2359296 | tf_op jit(solution)/shard_map/reduce_scatter | solution.py:38
  211.2 24.7 %collective-permute-start.12 = (bf16[256,2048]{1,0:T(8,128)(2,1)S(1)}, bf16[256,2048]{1,0:T(8,128)(2,1)S(1)}, u32[]{:S(2)}, u32[]{:S(2)}) collective-permute-start(bf16[256,2048]{1,0:T(8,128)(2,1)S(1)} %collective-permute-done.2.refs_1_), channel_id=1, source_target_pairs={{0,1},{1,0},{2,3},{3,2},{4,5},{5,4},{6,7},{7,6},{8,9},{9,8},{10,11... | collective-permute-start | bytes 3145736 | tf_op jit(solution)/shard_map/ppermute | solution.py:52
  211.2 26.5 %collective-permute-start.13 = (bf16[256,2048]{1,0:T(8,128)(2,1)S(1)}, bf16[256,2048]{1,0:T(8,128)(2,1)}, u32[]{:S(2)}, u32[]{:S(2)}) collective-permute-start(bf16[256,2048]{1,0:T(8,128)(2,1)S(1)} %collective-permute-done.3.refs_3_), channel_id=1, source_target_pairs={{0,1},{1,0},{2,3},{3,2},{4,5},{5,4},{6,7},{7,6},{8,9},{9,8},{10,11... | collective-permute-start | bytes 3145736 | tf_op jit(solution)/shard_map/ppermute | solution.py:52
  252.3 66.0 %all-gather.12.cloned.1.call-start = ((), (), s32[]{:S(2)}) async-start(), calls=%async_computation.11 | async-start | bytes 2359296 | tf_op jit(solution)/shard_map/all_gather | solution.py:34
  253.9 25.4 %collective-permute-start.25 = (bf16[256,2048]{1,0:T(8,128)(2,1)S(1)}, bf16[256,2048]{1,0:T(8,128)(2,1)S(1)}, u32[]{:S(2)}, u32[]{:S(2)}) collective-permute-start(bf16[256,2048]{1,0:T(8,128)(2,1)S(1)} %slice.82), channel_id=1, source_target_pairs={{0,16},{8,24},{16,0},{24,8},{1,17},{9,25},{17,1},{25,9},{2,18},{10... | collective-permute-start | bytes 3145736 | tf_op jit(solution)/shard_map/ppermute | solution.py:47
  255.2 25.0 %collective-permute-start.24 = (bf16[256,2048]{1,0:T(8,128)(2,1)S(1)}, bf16[256,2048]{1,0:T(8,128)(2,1)S(1)}, u32[]{:S(2)}, u32[]{:S(2)}) collective-permute-start(bf16[256,2048]{1,0:T(8,128)(2,1)S(1)} %slice.82), channel_id=1, source_target_pairs={{0,8},{8,0},{16,24},{24,16},{1,9},{9,1},{17,25},{25,17},{2,10},{10... | collective-permute-start | bytes 3145736 | tf_op jit(solution)/shard_map/ppermute | solution.py:47
  256.7 23.6 %collective-permute-start.20 = (bf16[256,2048]{1,0:T(8,128)(2,1)}, bf16[256,2048]{1,0:T(8,128)(2,1)}, u32[]{:S(2)}, u32[]{:S(2)}) collective-permute-start(bf16[256,2048]{1,0:T(8,128)(2,1)} %copy-done.7), channel_id=1, source_target_pairs={{0,1},{1,0},{2,3},{3,2},{4,5},{5,4},{6,7},{7,6},{8,9},{9,8},{10,11... | collective-permute-start | bytes 3145736 | tf_op jit(solution)/shard_map/ppermute | solution.py:52
  256.7 23.6 %collective-permute-start.21 = (bf16[256,2048]{1,0:T(8,128)(2,1)}, bf16[256,2048]{1,0:T(8,128)(2,1)}, u32[]{:S(2)}, u32[]{:S(2)}) collective-permute-start(bf16[256,2048]{1,0:T(8,128)(2,1)} %copy-done.6), channel_id=1, source_target_pairs={{0,1},{1,0},{2,3},{3,2},{4,5},{5,4},{6,7},{7,6},{8,9},{9,8},{10,11... | collective-permute-start | bytes 3145736 | tf_op jit(solution)/shard_map/ppermute | solution.py:52
  287.1 92.3 %reduce-scatter.12.cloned.1.call-start = ((), (), s32[]{:S(2)}) async-start(), calls=%async_computation.12 | async-start | bytes 4718592 | tf_op jit(solution)/shard_map/reduce_scatter | solution.py:38
  298.9 31.2 %collective-permute-start.33 = (bf16[512,1024]{1,0:T(8,128)(2,1)S(1)}, bf16[512,1024]{1,0:T(8,128)(2,1)}, u32[]{:S(2)}, u32[]{:S(2)}) collective-permute-start(bf16[512,1024]{1,0:T(8,128)(2,1)S(1)} %copy-done.2), channel_id=1, source_target_pairs={{0,16},{8,24},{16,0},{24,8},{1,17},{9,25},{17,1},{25,9},{2,18},{10... | collective-permute-start | bytes 3145736 | tf_op jit(solution)/shard_map/ppermute | solution.py:47
  300.4 29.8 %collective-permute-start.32 = (bf16[512,1024]{1,0:T(8,128)(2,1)S(1)}, bf16[512,1024]{1,0:T(8,128)(2,1)}, u32[]{:S(2)}, u32[]{:S(2)}) collective-permute-start(bf16[512,1024]{1,0:T(8,128)(2,1)S(1)} %copy-done.2), channel_id=1, source_target_pairs={{0,8},{8,0},{16,24},{24,16},{1,9},{9,1},{17,25},{25,17},{2,10},{10... | collective-permute-start | bytes 3145736 | tf_op jit(solution)/shard_map/ppermute | solution.py:47
  330.2 80.4 %all-gather.14.cloned.1.call-start = ((), (), s32[]{:S(2)}) async-start(), calls=%async_computation.13 | async-start | bytes 2359296 | tf_op jit(solution)/shard_map/all_gather | solution.py:34
  341.7 28.4 %collective-permute-start.37 = (bf16[128,2048]{1,0:T(8,128)(2,1)}, bf16[128,2048]{1,0:T(8,128)(2,1)}, u32[]{:S(2)}, u32[]{:S(2)}) collective-permute-start(bf16[128,2048]{1,0:T(8,128)(2,1)} %get-tuple-element.218), channel_id=1, source_target_pairs={{0,16},{8,24},{16,0},{24,8},{1,17},{9,25},{17,1},{25,9},{2,18},{10... | collective-permute-start | bytes 1572872 | tf_op jit(solution)/shard_map/ppermute | solution.py:47
  342.5 27.5 %collective-permute-start.38 = (bf16[128,2048]{1,0:T(8,128)(2,1)}, bf16[128,2048]{1,0:T(8,128)(2,1)}, u32[]{:S(2)}, u32[]{:S(2)}) collective-permute-start(bf16[128,2048]{1,0:T(8,128)(2,1)} %get-tuple-element.219), channel_id=1, source_target_pairs={{0,24},{8,16},{16,8},{24,0},{1,25},{9,17},{17,9},{25,1},{2,26},{10... | collective-permute-start | bytes 1572872 | tf_op jit(solution)/shard_map/ppermute | solution.py:47
  381.1 126.9 %reduce-scatter.14.cloned.1.call-start = ((), (), s32[]{:S(2)}) async-start(), calls=%async_computation.14 | async-start | bytes 4866048 | tf_op jit(solution)/shard_map/reduce_scatter | solution.py:38
  413.4 38.3 %collective-permute-start.45 = (bf16[256,512]{1,0:T(8,128)(2,1)S(1)}, bf16[256,512]{1,0:T(8,128)(2,1)S(1)}, u32[]{:S(2)}, u32[]{:S(2)}) collective-permute-start(bf16[256,512]{1,0:T(8,128)(2,1)S(1)} %copy-done.16), channel_id=1, source_target_pairs={{0,24},{8,16},{16,8},{24,0},{1,25},{9,17},{17,9},{25,1},{2,26},{10... | collective-permute-start | bytes 786440 | tf_op jit(solution)/shard_map/ppermute | solution.py:47
  414.3 37.5 %collective-permute-start.44 = (bf16[256,512]{1,0:T(8,128)(2,1)S(1)}, bf16[256,512]{1,0:T(8,128)(2,1)S(1)}, u32[]{:S(2)}, u32[]{:S(2)}) collective-permute-start(bf16[256,512]{1,0:T(8,128)(2,1)S(1)} %copy-done.16), channel_id=1, source_target_pairs={{0,16},{8,24},{16,0},{24,8},{1,17},{9,25},{17,1},{25,9},{2,18},{10... | collective-permute-start | bytes 786440 | tf_op jit(solution)/shard_map/ppermute | solution.py:47
  415.5 36.3 %collective-permute-start.43 = (bf16[256,512]{1,0:T(8,128)(2,1)S(1)}, bf16[256,512]{1,0:T(8,128)(2,1)S(1)}, u32[]{:S(2)}, u32[]{:S(2)}) collective-permute-start(bf16[256,512]{1,0:T(8,128)(2,1)S(1)} %copy-done.16), channel_id=1, source_target_pairs={{0,8},{8,0},{16,24},{24,16},{1,9},{9,1},{17,25},{25,17},{2,10},{10... | collective-permute-start | bytes 786440 | tf_op jit(solution)/shard_map/ppermute | solution.py:47
  483.6 24.4 %collective-permute-start.51 = (bf16[64,2048]{1,0:T(8,128)(2,1)}, bf16[64,2048]{1,0:T(8,128)(2,1)S(1)}, u32[]{:S(2)}, u32[]{:S(2)}) collective-permute-start(bf16[64,2048]{1,0:T(8,128)(2,1)} %get-tuple-element.284), channel_id=1, source_target_pairs={{0,16},{8,24},{16,0},{24,8},{1,17},{9,25},{17,1},{25,9},{2,18},{10... | collective-permute-start | bytes 786440 | tf_op jit(solution)/shard_map/ppermute | solution.py:47
  484.2 23.9 %collective-permute-start.52 = (bf16[64,2048]{1,0:T(8,128)(2,1)}, bf16[64,2048]{1,0:T(8,128)(2,1)}, u32[]{:S(2)}, u32[]{:S(2)}) collective-permute-start(bf16[64,2048]{1,0:T(8,128)(2,1)} %get-tuple-element.285), channel_id=1, source_target_pairs={{0,24},{8,16},{16,8},{24,0},{1,25},{9,17},{17,9},{25,1},{2,26},{10... | collective-permute-start | bytes 786440 | tf_op jit(solution)/shard_map/ppermute | solution.py:47
  487.4 36.3 %collective-permute-start.61 = (bf16[128,2048]{1,0:T(8,128)(2,1)S(1)}, bf16[128,2048]{1,0:T(8,128)(2,1)S(1)}, u32[]{:S(2)}, u32[]{:S(2)}) collective-permute-start(bf16[128,2048]{1,0:T(8,128)(2,1)S(1)} %add_convert_fusion.refs_0_), channel_id=1, source_target_pairs={{0,24},{8,16},{16,8},{24,0},{1,25},{9,17},{17,9},{25,1},{2,26},{10... | collective-permute-start | bytes 1572872 | tf_op jit(solution)/shard_map/ppermute | solution.py:47
  488.9 38.3 %collective-permute-start.60 = (bf16[128,2048]{1,0:T(8,128)(2,1)S(1)}, bf16[128,2048]{1,0:T(8,128)(2,1)S(1)}, u32[]{:S(2)}, u32[]{:S(2)}) collective-permute-start(bf16[128,2048]{1,0:T(8,128)(2,1)S(1)} %add_convert_fusion.refs_0_), channel_id=1, source_target_pairs={{0,16},{8,24},{16,0},{24,8},{1,17},{9,25},{17,1},{25,9},{2,18},{10... | collective-permute-start | bytes 1572872 | tf_op jit(solution)/shard_map/ppermute | solution.py:47
  502.2 25.0 %collective-permute-start.59 = (bf16[128,2048]{1,0:T(8,128)(2,1)S(1)}, bf16[128,2048]{1,0:T(8,128)(2,1)S(1)}, u32[]{:S(2)}, u32[]{:S(2)}) collective-permute-start(bf16[128,2048]{1,0:T(8,128)(2,1)S(1)} %add_convert_fusion.refs_0_), channel_id=1, source_target_pairs={{0,8},{8,0},{16,24},{24,16},{1,9},{9,1},{17,25},{25,17},{2,10},{10... | collective-permute-start | bytes 1572872 | tf_op jit(solution)/shard_map/ppermute | solution.py:47
  (94 other events, 1282.1 us)
Sparse Core Ops, SparseCore 0:
  10.2 77.0 all-gather.5
  98.1 33.8 reduce-scatter.5
  133.5 29.6 all-gather.7
  173.3 34.7 reduce-scatter.7
  209.6 29.5 all-gather.9
  252.4 34.6 reduce-scatter.9
  288.7 29.5 all-gather.11
  330.3 49.0 reduce-scatter.11
  381.6 28.9 all-gather.13
  453.4 50.5 reduce-scatter.13

commit v2 on v1

--- a/solution.py
+++ b/solution.py
@@ -12,10 +12,33 @@
 BF16 = jnp.bfloat16
 INV_ROOT = float(HEAD_DIM) ** (-0.5)
 PAD = 16
-DIRECT = ()
-COST = {"self_forward": 17, "text_project": 25, "cross_forward": 0, "seed_product": 12, "feed_both": 6, "out_product": 15, "cross_backward": 20, "self_backward": 27, "self_end": 5, "text_back": 8, "down_grads": 17, "up_grads": 14, "text_grads": 15, "self_grads": 40, "cross_parts": 7, "self_parts": 7, "cross_finish": 0, "self_finish": 5}
-DONE_BY = {"T1": "scattered1", "KV": "scattered1", "T2": "scattered2", "X1": "partial2", "X2": "scattered2", "T3": "scattered2", "DA": "scattered2", "Y1": "partial3", "X3": "mixed2", "Y2": "partial3", "F1": "scattered3", "OUT": "mixed2", "Y3": "scattered3", "F2": "mixed3", "A1": "partial4", "A2": "scattered4", "F3": "mixed3", "C0": "scattered4", "TB": "scattered4", "U1": "mixed4", "C1": "scattered4", "GD": "mixed4", "U2": "partial5", "D": "partial5", "GU": "partial5", "GT": "scattered5", "Q1": "scattered5", "Q2": "small", "S0": "scattered5", "S1": "scattered5", "S2": "small"}
-AFTER = {"Y1": ("X2",), "A1": ("F2",), "U1": ("TB",), "D": ("C1", "U1",), "S1": ("Q2",), "GQ": ("S1",), "S2": ("GQ",), "GT": ("GU",)}
+BATCH, TENSOR = "batch", "tensor"
+(
+    T1, T2, T3, X1, X2, X3, Y1, Y2, Y3, KV, DA, F1, F2, F3, A1, A2, A3, U1, U2, U3, OUT, GD, GU,
+    C0, C1, CA, C2, C3, TB, D1, D2, D3, GT, S0, S1, SA, S2, S3, Q1, Q2, Q3, GQ, SM, CF, SF,
+) = range(45)
+(
+    SCATTERED1, MIXED1, PARTIAL2, SCATTERED2, MIXED2, PARTIAL3, SCATTERED3, MIXED3, PARTIAL4,
+    SCATTERED4, MIXED4, PARTIAL5, SCATTERED5, SMALL,
+) = range(14)
+DONE_BY = {
+    T1: SCATTERED1, KV: SCATTERED1, T2: PARTIAL2, X1: MIXED1, X2: SCATTERED2, T3: SCATTERED2,
+    DA: SCATTERED2, Y1: PARTIAL3, X3: SCATTERED2, Y2: PARTIAL3, F1: SCATTERED3, OUT: SCATTERED3,
+    Y3: SCATTERED3, F2: MIXED3, A1: PARTIAL4, A2: SCATTERED4, F3: MIXED3, C0: SCATTERED5,
+    TB: SCATTERED4, U1: MIXED4, C1: SCATTERED4, GD: MIXED4, U2: PARTIAL5, GU: SCATTERED5,
+    GT: SCATTERED5, Q1: SCATTERED5, Q2: SMALL, S0: SCATTERED5, C2: SCATTERED5, D2: SCATTERED5,
+    C3: SMALL,
+}
+AFTER = {
+    A1: (F2,), U1: (TB,), S1: (Q2,), GQ: (S1, SM,), F1: (Y3,), GT: (GU,), CF: (SM,), SF: (SM,),
+    D1: (C1, U1,), SA: (SM,), C3: (U2,),
+}
+DIRECT = (C2, D1, S2,)
+COST = dict(
+    self_forward=17, text_project=25, cross_forward=0, seed_product=3, feed_both=6, out_product=15,
+    cross_backward=20, self_backward=27, self_end=5, text_back=8, down_grads=0, up_grads=14,
+    text_grads=15, self_grads=40, cross_parts=0, self_parts=6, cross_finish=0, self_finish=25,
+)
 
 
 def contract(left, right, left_dim, right_dim):
@@ -31,30 +54,30 @@
 
 
 def gather_cols(array):
-    return lax.all_gather(array, "tensor", axis=1, tiled=True)
+    return lax.all_gather(array, TENSOR, axis=1, tiled=True)
 
 
 def scatter_cols(array):
-    return lax.psum_scatter(array, "tensor", scatter_dimension=1, tiled=True)
+    return lax.psum_scatter(array, TENSOR, scatter_dimension=1, tiled=True)
 
 
 def square_batch():
-    return lax.axis_size("batch") == 4
+    return lax.axis_size(BATCH) == 4
 
 
 def hop(array, flip):
-    pairs = [(i, i ^ flip) for i in range(lax.axis_size("batch"))]
-    return lax.ppermute(array, "batch", pairs)
+    pairs = [(i, i ^ flip) for i in range(lax.axis_size(BATCH))]
+    return lax.ppermute(array, BATCH, pairs)
 
 
 def swap_core(array):
-    pairs = [(i, i ^ 1) for i in range(lax.axis_size("tensor"))]
-    return lax.ppermute(array, "tensor", pairs)
+    pairs = [(i, i ^ 1) for i in range(lax.axis_size(TENSOR))]
+    return lax.ppermute(array, TENSOR, pairs)
 
 
 def ring_others(array):
-    size, own = lax.axis_size("batch"), lax.axis_index("batch")
-    whole = lax.all_gather(array, "batch", axis=0, tiled=False)
+    size, own = lax.axis_size(BATCH), lax.axis_index(BATCH)
+    whole = lax.all_gather(array, BATCH, axis=0, tiled=False)
     return [
         lax.dynamic_index_in_dim(whole, lax.rem(own + k, size), 0, keepdims=False)
         for k in range(1, size)
@@ -98,7 +121,7 @@
 
 def direct_sum(array):
     if not square_batch():
-        return lax.psum(array.astype(BF16), "batch").astype(F32)
+        return lax.psum(array.astype(BF16), BATCH).astype(F32)
     low = array.astype(BF16)
     moved = [hop(low, k) for k in (1, 2, 3)]
     return array + moved[0].astype(F32) + moved[1].astype(F32) + moved[2].astype(F32)
@@ -156,8 +179,7 @@
 class Packed:
     def __init__(self, rows, text_rows):
         self.rows = rows
-        self.pos = rows
-        self.text = rows + IMG_LEN
+        self.text = rows
         self.seed = self.text + text_rows
         self.vec = self.seed + rows
         self.total = self.vec + PAD
@@ -171,8 +193,6 @@
 
     def kernel(counts, order, tok, cap, cot, pos, *rest):
         out, block, mask = rest[-3:]
-        out[: at.pos, :] = tok[...]
-        out[at.pos : at.text, :] = pos[...]
         for k in range(text_blocks):
             low = at.text + k * text_rows
             out[low : low + text_rows, :] = cap[:, k * columns : (k + 1) * columns]
@@ -188,6 +208,8 @@
             column = jnp.max(hit.astype(F32), axis=1, keepdims=True)
             own = slice(i * IMG_LEN, (i + 1) * IMG_LEN)
             mask[own, :] = column
+            base = jnp.where(column > 0.0, vec[0:1, :].astype(F32), tok[own, :].astype(F32))
+            out[own, :] = (base + pos[...].astype(F32)).astype(BF16)
             out[at.seed + i * IMG_LEN : at.seed + (i + 1) * IMG_LEN, :] = jnp.where(
                 column > 0.0, cot[own, :].astype(F32), 0.0
             ).astype(BF16)
@@ -269,22 +291,17 @@
 
 
 def packed_specs(at, width):
-    return [
-        by_rows(IMG_LEN, 1),
-        by_rows(IMG_LEN, width),
-        fixed((IMG_LEN, width), at.pos // IMG_LEN),
-        fixed((PAD, width), at.vec // PAD),
-    ]
-
-
-def self_forward(place, at, mask, packed, query_w, key_w, value_w, out_w):
-    rows, width = mask.shape[0], packed.shape[1]
+    return [by_rows(IMG_LEN, width), fixed((PAD, width), at.vec // PAD)]
+
+
+def self_forward(place, at, packed, query_w, key_w, value_w, out_w):
+    rows, width = at.rows, packed.shape[1]
     columns = query_w.shape[1]
 
     def kernel(
-        place, mask, tok, pos, vec, wq, wk, wv, wo, normed, query, key, value, mixed, part, stats
+        place, zero, vec, wq, wk, wv, wo, normed, query, key, value, mixed, part, stats
     ):
-        normal, mean, inv_std = normalize(first_stream(mask, tok, pos, vec))
+        normal, mean, inv_std = normalize(zero[...].astype(F32))
         stats[:, 0:1] = mean
         stats[:, 1:2] = inv_std
         low = (normal * vec[1:2, :].astype(F32)).astype(BF16)
@@ -299,7 +316,7 @@
 
     outs = [struct((rows, width), BF16)] + [struct((rows, columns), BF16)] * 4
     outs += [struct((rows, width), BF16), struct((rows, 2), F32)]
-    args = (mask, packed, packed, packed, query_w, key_w, value_w, out_w)
+    args = (packed, packed, query_w, key_w, value_w, out_w)
     return call(
         "self_forward",
         kernel,
@@ -361,16 +378,16 @@
     )
 
 
-def cross_forward(place, at, mask, packed, added, query_w, key, value, out_w):
-    rows, width = mask.shape[0], packed.shape[1]
+def cross_forward(place, at, packed, added, query_w, key, value, out_w):
+    rows, width = at.rows, packed.shape[1]
     columns = query_w.shape[1]
     text_rows = key.shape[0] // (rows // IMG_LEN)
 
     def kernel(
-        place, mask, tok, pos, vec, add, wq, k, v, wo, stream, normed, query, mixed, part, scale
+        place, zero, vec, add, wq, k, v, wo, stream, normed, query, mixed, part, scale
     ):
-        one = first_stream(mask, tok, pos, vec) + add[...].astype(F32)
-        stream[...] = one
+        one = zero[...].astype(F32) + add[...].astype(F32)
+        stream[...] = one.astype(BF16)
         normal, mean, inv_std = normalize(one)
         scale[...] = inv_std
         low = (normal * vec[2:3, :].astype(F32)).astype(BF16)
@@ -381,10 +398,10 @@
         mixed[...] = a
         part[...] = contract(a, wo[...], 1, 0).astype(BF16)
 
-    outs = [struct((rows, width), F32), struct((rows, width), BF16)]
+    outs = [struct((rows, width), BF16)] * 2
     outs += [struct((rows, columns), BF16)] * 2 + [struct((rows, width), BF16)]
     outs += [struct((rows, 1), F32)]
-    args = (mask, packed, packed, packed, added, query_w, key, value, out_w)
+    args = (packed, packed, added, query_w, key, value, out_w)
     return call(
         "cross_forward",
         kernel,
@@ -438,11 +455,11 @@
 
 def feed_both(place, at, stream, added, packed, act_grad, up_w):
     rows, width = stream.shape
-    hidden, columns = up_w.shape[1], width // lax.axis_size("tensor")
+    hidden, columns = up_w.shape[1], width // lax.axis_size(TENSOR)
     block = IMG_LEN
 
     def kernel(place, one, add, vec, dact, up, slim, scale, normed, act, grad, part, two):
-        stream = one[...] + add[...].astype(F32)
+        stream = one[...].astype(F32) + add[...].astype(F32)
         two[...] = stream
         slim[...] = two[:, pl.ds(pl.multiple_of(place[0] * columns, columns), columns)]
         normal, mean, inv_std = normalize(stream)
@@ -519,12 +536,11 @@
     columns = query.shape[1]
     text_rows = key.shape[0] // (rows // IMG_LEN)
 
-    def kernel(place, three, inv, dn, g3, vec, wo, q, k, v, wq, room, grad, low, dq, dkv, part, gain):
+    def kernel(place, three, inv, dn, g3, vec, wo, q, k, v, wq, room, low, dq, dkv, part, gain):
         step, gain_step = norm_back(
             dn[...].astype(F32), three[...].astype(F32), inv[...], vec[3:4, :].astype(F32)
         )
         total = g3[...].astype(F32) + step
-        grad[...] = total
         y = total.astype(BF16)
         low[...] = y
 
@@ -541,7 +557,6 @@
         part[...] = contract(query_grad, wq[...], 1, 1).astype(BF16)
 
     outs = [
-        struct((rows, width), F32),
         struct((rows, width), BF16),
         struct((rows, columns), BF16),
         struct((key.shape[0], 2 * columns), BF16),
@@ -569,7 +584,6 @@
         ],
         [
             by_rows(IMG_LEN, width),
-            by_rows(IMG_LEN, width),
             by_rows(IMG_LEN, columns),
             by_rows(text_rows, 2 * columns),
             by_rows(IMG_LEN, width),
@@ -577,7 +591,7 @@
         ],
         outs,
         args,
-        aliases={len(args): 4},
+        aliases={len(args): 3},
     )
 
 
@@ -589,22 +603,27 @@
     cut = (shards, blocks, columns, columns)
 
     def kernel(place, grads, wk, wv, out):
-        for k in range(blocks):
-            part = contract(grads[:, :columns], wk[0, k], 1, 1) + contract(
-                grads[:, columns:], wv[0, k], 1, 1
-            )
-            out[k * text_rows : (k + 1) * text_rows, :] = part.astype(BF16)
-        out[blocks * text_rows :, :] = jnp.zeros((rows - blocks * text_rows, columns), BF16)
-
-    weight = pl.BlockSpec((1, *cut[1:]), lambda i, *_: (i, 0, 0, 0))
+        for t in range(step):
+            cols = slice(t * columns, (t + 1) * columns)
+            for k in range(blocks):
+                part = contract(grads[:, :columns], wk[t, k], 1, 1) + contract(
+                    grads[:, columns:], wv[t, k], 1, 1
+                )
+                out[k * text_rows : (k + 1) * text_rows, cols] = part.astype(BF16)
+        out[blocks * text_rows :, :] = jnp.zeros(
+            (rows - blocks * text_rows, step * columns), BF16
+        )
+
+    step = min(4, shards)
+    weight = pl.BlockSpec((step, *cut[1:]), lambda i, *_: (i, 0, 0, 0))
     outs = [struct((2 * rows, width), BF16)]
     return call(
         "text_back",
         kernel,
         place,
-        (shards,),
+        (shards // step,),
         [fixed(pair.shape), weight, weight],
-        [pl.BlockSpec((rows, columns), lambda i, *_: (1, i))],
+        [pl.BlockSpec((rows, step * columns), lambda i, *_: (1, i))],
         outs,
         (pair, key_w.reshape(cut), value_w.reshape(cut)),
     )[0]
@@ -624,7 +643,7 @@
         step, gain_step = norm_back(
             dn[...].astype(F32), two[...].astype(F32), inv[...], vec[2:3, :].astype(F32)
         )
-        total = g2[...] + step
+        total = g2[...].astype(F32) + step
         held[...] = total
         mine[...] = held[:, pl.ds(pl.multiple_of(place[0] * columns, columns), columns)]
         y = total.astype(BF16)
@@ -831,10 +850,13 @@
     core_split = square_batch()
     pieces, rights, terms = [], [pair], []
     for text_group, pair_group in zip(text_groups, pair_groups):
-        rights.append(pair_group[0][0])
+        base = len(rights)
+        rights += [piece for piece, _ in pair_group]
         for piece, row in text_group:
             pieces.append(piece)
-            terms.append((row // text_rows, row % text_rows, len(rights) - 1))
+            for k, (right, low) in enumerate(pair_group):
+                if low <= row % text_rows < low + right.shape[0]:
+                    terms.append((row // text_rows, row % text_rows - low, base + k))
     if not core_split:
         pieces, terms = [], []
         for k, text_group in enumerate(text_groups):
@@ -967,35 +989,47 @@
     def step_one(self):
         if not square_batch():
             parts = [contract(left, right, 0, 0) for left, right, _ in self.products]
-            return [lax.psum(p.astype(BF16), "batch") for p in parts]
+            return [lax.psum(p.astype(BF16), BATCH) for p in parts]
         return [hop(self.sent[k - 1], k) for k in (1, 2, 3)]
 
-    def step_two(self, held):
+    def add(self, held):
         if not square_batch():
             return held
         total = self.quarters[0].astype(F32)
         for moved in held:
             total = total + moved.astype(F32)
-        low = total.astype(BF16)
-        return [low] + [hop(low, k) for k in (1, 2, 3)]
+        return [total.astype(BF16)]
+
+    def step_two(self, held):
+        if not square_batch():
+            return held
+        self.groups = self.move.step_two(held)
+        return [self.low] + [piece for group in self.groups for piece, _ in group]
 
     def finish(self, held):
         if not square_batch():
             return [h.astype(F32) for h in held]
         height, width, rows = self.height, self.width, self.rows
         folds = [fold for _, _, fold in self.products]
+        spots = [(0, 0)] + [
+            (k + 1, first) for k, group in enumerate(self.groups) for _, first in group
+        ]
 
         def kernel(place, *refs):
-            ins, outs = refs[:4], refs[4:]
-            for n, (out, fold) in enumerate(zip(outs, folds)):
-                for k, ref in enumerate(ins):
-                    at = pl.multiple_of((place[1] ^ k) * rows, rows)
-                    piece = ref[n * rows : (n + 1) * rows, :].astype(F32)
+            ins, outs = refs[: len(held)], refs[len(held) :]
+            for ref, (k, first) in zip(ins, spots):
+                for n, (out, fold) in enumerate(zip(outs, folds)):
+                    low, high = max(n * rows, first), min((n + 1) * rows, first + ref.shape[0])
+                    if low >= high:
+                        continue
+                    count = high - low
+                    at = pl.multiple_of((place[1] ^ k) * rows + low - n * rows, count)
+                    piece = ref[low - first : high - first, :].astype(F32)
                     if fold:
                         for col in range(0, width, height):
-                            out[pl.ds(col + at, rows), :] = piece[:, col : col + height]
+                            out[pl.ds(col + at, count), :] = piece[:, col : col + height]
                     else:
-                        out[pl.ds(at, rows), :] = piece
+                        out[pl.ds(at, count), :] = piece
 
         outs = [struct((width, height) if fold else (height, width), F32) for fold in folds]
         return call(
@@ -1036,7 +1070,7 @@
     width, hidden = query_self.shape[0], up_weight.shape[1]
     text_rows, text_blocks = captions.shape[0], captions.shape[1] // columns
     at = Packed(rows, text_rows * text_blocks)
-    place = jnp.stack([lax.axis_index("tensor"), lax.axis_index("batch")]).astype(jnp.int32)
+    place = jnp.stack([lax.axis_index(TENSOR), lax.axis_index(BATCH)]).astype(jnp.int32)
     core = place[0] % 2
     shared = square_batch()
     packed, vectors, mask = pack_rows(
@@ -1065,52 +1099,53 @@
         )
     plan = Plan()
 
-    def spread(name, source, shared):
+    def spread(names, source, shared):
+        near, far, cores = names
         move = Spread(None, shared)
 
         def one():
-            move.array = plan.behind(name + "1", source())
-            return direct(move.array) if name in DIRECT else move.step_one()
+            move.array = plan.behind(near, source())
+            return direct(move.array) if near in DIRECT else move.step_one()
 
         def two():
-            held = plan.get(name + "1")
-            return held if name in DIRECT else move.step_two(held)
-
-        plan.job(name + "1", one)
-        plan.job(name + "2", two)
-        plan.job(name + "3", lambda: move.swap(plan.get(name + "2")))
+            held = plan.behind(far, plan.get(near))
+            return held if near in DIRECT else move.step_two(held)
+
+        plan.job(near, one)
+        plan.job(far, two)
+        plan.job(cores, lambda: move.swap(plan.get(far)))
 
     normed_self, query_one, key_one, value_one, mixed_self, partial, stats = self_forward(
-        place, at, mask, packed, query_self, key_self, value_self, out_self
-    )
-    spread("T", lambda: text_part, shared)
-    spread("X", lambda: normed_self[:IMG_LEN] if shared else normed_self, shared)
-    spread("Y", lambda: seed_part, shared)
-    plan.job("KV", lambda: text_project(place, at, packed, key_text, value_text))
-    plan.job("DA", lambda: seed_product(place, at, packed, down_weight))
-    scattered = plan.tie("scattered1", scatter_cols(partial))
-    mixed_out = plan.tie("mixed1", gather_cols(scattered))
-    key_two, value_two = plan.get("KV")
+        place, at, packed, query_self, key_self, value_self, out_self
+    )
+    spread((T1, T2, T3), lambda: text_part, shared)
+    spread((X1, X2, X3), lambda: normed_self[:IMG_LEN] if shared else normed_self, shared)
+    spread((Y1, Y2, Y3), lambda: seed_part, shared)
+    plan.job(KV, lambda: text_project(place, at, packed, key_text, value_text))
+    plan.job(DA, lambda: seed_product(place, at, packed, down_weight))
+    scattered = plan.tie(SCATTERED1, scatter_cols(partial))
+    mixed_out = plan.tie(MIXED1, gather_cols(scattered))
+    key_two, value_two = plan.get(KV)
 
     stream_one, normed_cross, query_two, mixed_cross, partial, scale_cross = cross_forward(
-        place, at, mask, packed, mixed_out, query_cross, key_two, value_two, out_cross
-    )
-    partial = plan.tie("partial2", partial)
-    scattered = plan.tie("scattered2", scatter_cols(partial))
-    mixed_out = plan.tie("mixed2", gather_cols(scattered))
+        place, at, packed, mixed_out, query_cross, key_two, value_two, out_cross
+    )
+    partial = plan.tie(PARTIAL2, partial)
+    scattered = plan.tie(SCATTERED2, scatter_cols(partial))
+    mixed_out = plan.tie(MIXED2, gather_cols(scattered))
 
     own_two, scale_feed, normed_feed, activation, hidden_grad, partial = feed_both(
-        place, at, stream_one, mixed_out, packed, plan.get("DA"), up_weight
-    )
-    spread("F", lambda: normed_feed[:IMG_LEN] if shared else normed_feed, shared)
-    spread("A", lambda: activation, False)
-    spread("U", lambda: hidden_grad, False)
-    plan.job("OUT", lambda: out_product(place, plan.behind("OUT", activation), down_weight))
-    partial = plan.tie("partial3", partial)
-    scattered = plan.tie("scattered3", scatter_cols(partial))
-    feed_back = plan.tie("mixed3", gather_cols(scattered))
-
-    grad_two, seed_cross, query_grad, pair, partial, feed_gain = cross_backward(
+        place, at, stream_one, mixed_out, packed, plan.get(DA), up_weight
+    )
+    spread((F1, F2, F3), lambda: normed_feed[:IMG_LEN] if shared else normed_feed, shared)
+    spread((A1, A2, A3), lambda: activation, False)
+    spread((U1, U2, U3), lambda: hidden_grad, False)
+    plan.job(OUT, lambda: out_product(place, plan.behind(OUT, activation), down_weight))
+    partial = plan.tie(PARTIAL3, partial)
+    scattered = plan.tie(SCATTERED3, scatter_cols(partial))
+    feed_back = plan.tie(MIXED3, gather_cols(scattered))
+
+    seed_cross, query_grad, pair, partial, feed_gain = cross_backward(
         place,
         at,
         normed_feed,
@@ -1123,31 +1158,29 @@
         key_two,
         value_two,
         query_cross,
-        plan.get("OUT"),
+        plan.get(OUT),
     )
     own_seed = [
         ((packed, IMG_LEN, lambda p: at.seed // IMG_LEN + p[0] % 2), 0),
         ((packed, IMG_LEN, lambda p: at.seed // IMG_LEN + 1 - p[0] % 2), IMG_LEN),
     ]
-    plan.job(
-        "GD",
+    plan.job(GD,
         lambda: grad_sum(
             "down_grads",
             place,
-            [[(plan.behind("GD", activation), 0)], *plan.get("A2")],
-            [own_seed, *plan.get("Y3")],
+            [[(plan.behind(GD, activation), 0)], *plan.get(A2)],
+            [own_seed, *plan.get(Y3)],
             (width,),
             256,
             ((0, hidden), (0, width)),
         ),
     )
-    plan.job(
-        "GU",
+    plan.job(GU,
         lambda: grad_sum(
             "up_grads",
             place,
-            [[(plan.behind("GU", normed_feed), 0)], *plan.get("F3")],
-            [[(hidden_grad, 0)], *plan.get("U2")],
+            [[(plan.behind(GU, normed_feed), 0)], *plan.get(F3)],
+            [[(hidden_grad, 0)], *plan.get(U2)],
             (hidden,),
             512,
             ((0, width), (0, hidden)),
@@ -1157,40 +1190,55 @@
         "cross", place, [(mixed_cross, seed_cross, False), (normed_cross, query_grad, True)]
     )
 
-    def batch_sum(name, total):
-        plan.job(name + "0", lambda: total.quarters)
+    def batch_sum(names, total):
+        make, out, add, near, far = names
+        plan.job(make, lambda: total.quarters)
 
         def one():
-            total.sent = plan.behind(name + "1", plan.get(name + "0")[1:])
+            total.sent = plan.behind(out, plan.get(make)[1:])
             return total.step_one()
 
-        plan.job(name + "1", one)
-        plan.job(name + "2", lambda: total.step_two(plan.behind(name + "2", plan.get(name + "1"))))
-
-    batch_sum("C", cross_sum)
-    plan.job(
-        "TB",
+        def back():
+            (total.low, *_) = held = plan.behind(near, plan.get(add))
+            if not shared:
+                return held
+            total.move = Spread(total.low, False)
+            return direct(total.low) if near in DIRECT else total.move.step_one()
+
+        def rest():
+            held = plan.behind(far, plan.get(near))
+            if near in DIRECT and shared:
+                total.groups = held
+                return [total.low] + [piece for group in held for piece, _ in group]
+            return total.step_two(held)
+
+        plan.job(out, one)
+        plan.job(add, lambda: total.add(plan.behind(add, plan.get(out))))
+        plan.job(near, back)
+        plan.job(far, rest)
+
+    batch_sum((C0, C1, CA, C2, C3), cross_sum)
+    plan.job(TB,
         lambda: text_back(
-            place, plan.behind("TB", pair), key_text, value_text, rows + PAD, width
+            place, plan.behind(TB, pair), key_text, value_text, rows + PAD, width
         ),
     )
-    plan.job("D", lambda: direct(plan.behind("D", pair)))
-    plan.job(
-        "GT",
+    spread((D1, D2, D3), lambda: pair, False)
+    plan.job(GT,
         lambda: text_grads(
             place,
             at,
             packed,
-            plan.behind("GT", pair),
-            plan.get("T3"),
-            plan.get("D"),
+            plan.behind(GT, pair),
+            plan.get(T3),
+            plan.get(D2),
             text_blocks,
         ),
     )
-    partial = plan.tie("partial4", partial)
-    scattered = plan.tie("scattered4", scatter_cols(partial))
+    partial = plan.tie(PARTIAL4, partial)
+    scattered = plan.tie(SCATTERED4, scatter_cols(partial))
     out_slice = scattered[rows:]
-    cross_back = plan.tie("mixed4", gather_cols(scattered[:rows]))
+    cross_back = plan.tie(MIXED4, gather_cols(scattered[:rows]))
 
     own_one, seed_self, triple, partial, cross_gain = self_backward(
         place,
@@ -1200,32 +1248,31 @@
         scale_cross,
         cross_back,
         packed,
-        grad_two,
+        seed_cross,
         out_self,
         query_one,
         key_one,
         value_one,
         (query_self, key_self, value_self),
-        plan.get("TB"),
+        plan.get(TB),
     )
     layer_out = (own_two + out_slice.astype(F32)).astype(BF16)
     self_sum = BatchSum("self", place, [(mixed_self, seed_self, False)])
-    batch_sum("S", self_sum)
-    spread("Q", lambda: triple, False)
-    plan.job(
-        "GQ",
+    batch_sum((S0, S1, SA, S2, S3), self_sum)
+    spread((Q1, Q2, Q3), lambda: triple, False)
+    plan.job(GQ,
         lambda: grad_sum(
             "self_grads",
             place,
-            [[(plan.behind("GQ", normed_self), 0)], *plan.get("X3")],
-            [[(triple, 0)], *plan.get("Q2")],
+            [[(plan.behind(GQ, normed_self), 0)], *plan.get(X3)],
+            [[(triple, 0)], *plan.get(Q2)],
             (columns,) * 3,
             512,
             ((0, width), (0, 3 * columns)),
         ),
     )
-    partial = plan.tie("partial5", partial)
-    scattered = plan.tie("scattered5", scatter_cols(partial))
+    partial = plan.tie(PARTIAL5, partial)
+    scattered = plan.tie(SCATTERED5, scatter_cols(partial))
     low = rows + PAD
     captions_grad = jnp.concatenate(
         [
@@ -1246,14 +1293,18 @@
         (cross_gain, feed_gain),
         width,
     )
-    small = plan.tie("small", small)
+    small = plan.tie(SMALL, small)
+    seen = small
+    plan.job(SM, lambda: seen)
+    plan.job(CF, lambda: cross_sum.finish(plan.behind(CF, plan.get(C3))))
+    plan.job(SF, lambda: self_sum.finish(plan.behind(SF, plan.get(S3))))
     small = direct_sum(small)
-    (down_grad,) = plan.get("GD")
-    (up_grad,) = plan.get("GU")
-    key_text_grad, value_text_grad = plan.get("GT")
-    query_self_grad, key_self_grad, value_self_grad = plan.get("GQ")
-    out_cross_grad, query_cross_grad = cross_sum.finish(plan.get("C2"))
-    (out_self_grad,) = self_sum.finish(plan.get("S2"))
+    (down_grad,) = plan.get(GD)
+    (up_grad,) = plan.get(GU)
+    key_text_grad, value_text_grad = plan.get(GT)
+    query_self_grad, key_self_grad, value_self_grad = plan.get(GQ)
+    out_cross_grad, query_cross_grad = plan.get(CF)
+    (out_self_grad,) = plan.get(SF)
     return (
         layer_out,
         tokens_grad,
@@ -1281,46 +1332,46 @@
         body,
         mesh=mesh,
         in_specs=(
-            P("batch", "tensor"),
-            P("batch", "tensor"),
-            P("batch"),
-            P("batch", None),
-            P("batch", "tensor"),
-            P("tensor"),
-            P(None, "tensor"),
-            P("tensor"),
-            P(None, "tensor"),
-            P(None, "tensor"),
-            P(None, "tensor"),
-            P("tensor", None),
-            P("tensor"),
-            P(None, "tensor"),
-            P(None, "tensor"),
-            P(None, "tensor"),
-            P("tensor", None),
-            P("tensor"),
-            P(None, "tensor"),
-            P("tensor", None),
+            P(BATCH, TENSOR),
+            P(BATCH, TENSOR),
+            P(BATCH),
+            P(BATCH, None),
+            P(BATCH, TENSOR),
+            P(TENSOR),
+            P(None, TENSOR),
+            P(TENSOR),
+            P(None, TENSOR),
+            P(None, TENSOR),
+            P(None, TENSOR),
+            P(TENSOR, None),
+            P(TENSOR),
+            P(None, TENSOR),
+            P(None, TENSOR),
+            P(None, TENSOR),
+            P(TENSOR, None),
+            P(TENSOR),
+            P(None, TENSOR),
+            P(TENSOR, None),
         ),
         out_specs=(
-            P("batch", "tensor"),
-            P("batch", "tensor"),
-            P("batch", "tensor"),
-            P("tensor"),
-            P(None, "tensor"),
-            P("tensor"),
-            P(None, "tensor"),
-            P(None, "tensor"),
-            P(None, "tensor"),
-            P("tensor", None),
-            P("tensor"),
-            P(None, "tensor"),
-            P(None, "tensor"),
-            P(None, "tensor"),
-            P("tensor", None),
-            P("tensor"),
-            P(None, "tensor"),
-            P("tensor", None),
+            P(BATCH, TENSOR),
+            P(BATCH, TENSOR),
+            P(BATCH, TENSOR),
+            P(TENSOR),
+            P(None, TENSOR),
+            P(TENSOR),
+            P(None, TENSOR),
+            P(None, TENSOR),
+            P(None, TENSOR),
+            P(TENSOR, None),
+            P(TENSOR),
+            P(None, TENSOR),
+            P(None, TENSOR),
+            P(None, TENSOR),
+            P(TENSOR, None),
+            P(TENSOR),
+            P(None, TENSOR),
+            P(TENSOR, None),
         ),
         check_vma=False,
     )

time: 563 us -> 540 us (0.959)
  waiting for transfers between devices: 274 us -> 259 us
  Pallas kernels: 172 us -> 166 us
    all_gather x5, waiting for transfers between devices: 119 us -> 91.3 us  [gather_cols(): return lax.all_gather(array, TENSOR, axis=1, tiled=True)]
    ppermute x62, waiting for transfers between devices: 132 us -> 147 us  [the longest x46 139 us: hop(): return lax.ppermute(array, BATCH, pairs)]
    pallas_call x18, Pallas kernels: 170 us -> 163 us  [call(): pl.pallas_call(kernel, grid_spec=pltpu.PrefetchScalarGridSpec(num_scalar_...]
    unnamed x108 -> x110, local copies, waits for them, and re-layouts: 12.5 us -> 11.5 us
  transfers between devices with their start and end apart: 72 -> 72, of which waited for: 28 -> 37; matrix products, arithmetic and copies ran while one was open for 3% -> 3% of each run, Pallas kernels for 29% -> 28%
where the time goes in v2:
time: 540 us; the launch traced here: 533 us
  waiting for transfers between devices  259 us (48%)
  Pallas kernels  166 us (31%)
  starting transfers between devices  61.3 us (11%)
  local copies, waits for them, and re-layouts  25.2 us (5%)
  between operations  15.3 us (3%)
  other arithmetic  5.92 us (1%)
    pallas_call x18, Pallas kernels, call(): pl.pallas_call(kernel, grid_spec=pltpu.PrefetchScalarGridSpec(num_scalar_...  163 us
    ppermute x46, waiting for transfers between devices, hop(): return lax.ppermute(array, BATCH, pairs)  139 us
    all_gather x5, waiting for transfers between devices, gather_cols(): return lax.all_gather(array, TENSOR, axis=1, tiled=True)  91.3 us
    ppermute x46, starting transfers between devices, hop(): return lax.ppermute(array, BATCH, pairs)  57.1 us
    reduce_scatter x5, waiting for transfers between devices, scatter_cols(): return lax.psum_scatter(array, TENSOR, scatter_dimension=1, tiled=True)  21.2 us
    unnamed x110, local copies, waits for them, and re-layouts  11.5 us
  transfers between devices with their start and end apart: 72, of which 37 were waited for; matrix products, arithmetic and copies ran while one was open for 3% of the time, Pallas kernels for 28%

profile of v2, /device:TPU:0, one launch (start us, length us, event | category | flops | bytes accessed | tf_op | source)
XLA Modules:
  0.0 533.1 jit_solution(14765359632115316197)
XLA Ops:
  10.3 68.3 %all-gather.6.cloned.1.call-done.zero.vec.refs_0_.refs_1_.seed.g3.refs_5_.refs_6_.own = bf16[1552,2048]{1,0:T(8,128)(2,1)} async-done(((bf16[1552,256]{1,0:T(8,128)(2,1)}), bf16[1552,2048]{1,0:T(8,128)(2,1)}) %all-gather.6.cloned.1.call-update) | async-done | bytes 6357008 | tf_op jit(solution)/shard_map/all_gather | solution.py:57
  78.6 9.6 %self_forward.1 = (bf16[512,2048]{1,0:T(8,128)(2,1)}, bf16[512,256]{1,0:T(8,128)(2,1)}, bf16[512,256]{1,0:T(8,128)(2,1)}, bf16[512,256]{1,0:T(8,128)(2,1)}, bf16...) custom-call(s32[2]{0:T(128)} %pad_add_fusion.place, ...), custom_call_target="tpu_custom_call" | custom-call | flops 1000 | bytes 17001000 | tf_op jit(solution)/shard_map/self_forward/pallas_call | solution.py:158
  94.0 5.1 text_project.1
  99.1 17.3 %collective-permute-done.refs_0_ = bf16[256,2048]{1,0:T(8,128)(2,1)S(1)} collective-permute-done((bf16[256,2048]{1,0:T(8,128)(2,1)S(1)}, bf16[256,2048]{1,0:T(8,128)(2,1)S(1)}, u32[]{:S(2)}, u32[]{:S(2)}) %collective-permute-start) | collective-permute-done | bytes 1048608 | tf_op jit(solution)/shard_map/ppermute | solution.py:70
  117.7 4.5 reduce-scatter.6.cloned.1.call-done
  129.3 19.3 %collective-permute-done.2.refs_1_ = bf16[256,2048]{1,0:T(8,128)(2,1)S(1)} collective-permute-done((bf16[256,2048]{1,0:T(8,128)(2,1)S(1)}, bf16[256,2048]{1,0:T(8,128)(2,1)S(1)}, u32[]{:S(2)}, u32[]{:S(2)}) %collective-permute-start.2) | collective-permute-done | bytes 1048608 | tf_op jit(solution)/shard_map/ppermute | solution.py:70
  153.5 9.1 %cross_forward.1 = (bf16[512,2048]{1,0:T(8,128)(2,1)}, bf16[512,2048]{1,0:T(8,128)(2,1)}, bf16[512,256]{1,0:T(8,128)(2,1)}, bf16[512,256]{1,0:T(8,128)(2,1)}, bf...) custom-call(s32[2]{0:T(128)} %pad_add_fusion.place, ...), custom_call_target="tpu_custom_call" | custom-call | flops 1000 | bytes 1000 | tf_op jit(solution)/shard_map/cross_forward/pallas_call | solution.py:158
  167.5 10.2 %collective-permute-done.10.refs_5_ = bf16[128,2048]{1,0:T(8,128)(2,1)S(1)} collective-permute-done((bf16[128,2048]{1,0:T(8,128)(2,1)S(1)}, bf16[128,2048]{1,0:T(8,128)(2,1)S(1)}, u32[]{:S(2)}, u32[]{:S(2)}) %collective-permute-start.10) | collective-permute-done | bytes 524320 | tf_op jit(solution)/shard_map/ppermute | solution.py:70
  179.3 6.8 %seed_product.1.dact = f32[512,1024]{1,0:T(8,128)} custom-call(s32[2]{0:T(128)} %pad_add_fusion.place, bf16[1552,2048]{1,0:T(8,128)(2,1)} %all-gather.6.cloned.1.call-done.zero.vec.refs_0_.refs_1_.seed.g3.refs_5_.refs_6_.own, bf16[1024,2048]{1,0:T(8,128)(2,1)} %down.3), custom_call_target="tpu_custom_call" | custom-call | flops 1000 | bytes 3001000 | tf_op jit(solution)/shard_map/seed_product/pallas_call | solution.py:158
  188.4 9.3 %reduce-scatter.8.cloned.1.call-done = bf16[512,256]{1,0:T(8,128)(2,1)} async-done(((bf16[512,2048]{1,0:T(8,128)(2,1)}), bf16[512,256]{1,0:T(8,128)(2,1)}) %reduce-scatter.8.cloned.1.call-update) | async-done | bytes 262160 | tf_op jit(solution)/shard_map/reduce_scatter | solution.py:61
  200.7 19.7 %collective-permute-done.16.refs_7_ = bf16[256,2048]{1,0:T(8,128)(2,1)S(1)} collective-permute-done((bf16[256,2048]{1,0:T(8,128)(2,1)}, bf16[256,2048]{1,0:T(8,128)(2,1)S(1)}, u32[]{:S(2)}, u32[]{:S(2)}) %collective-permute-start.16) | collective-permute-done | bytes 1048608 | tf_op jit(solution)/shard_map/ppermute | solution.py:70
  228.6 12.6 %feed_both.1 = (f32[512,256]{1,0:T(8,128)}, f32[512,1]{1,0:T(8,128)}, bf16[512,2048]{1,0:T(8,128)(2,1)}, bf16[512,1024]{1,0:T(8,128)(2,1)}, bf16[512,1024]{1,0:T(8,128)(2,1)}, /*index=5*/bf16[512,2048]{1,0:T(8,128)(2,1)}) custom-call(s32[2]{0:T(128)} %pad_add_fusion.place, bf16[512,2048]{1,0:T(8,128)(2,1)} %get-tuple-element.199.one, ...), custom_call_target="tpu_custom_call" | custom-call | flops 1000 | bytes 6001000 | tf_op jit(solution)/shard_map/feed_both/pallas_call | solution.py:158
  250.9 6.6 %out_product.1.room = bf16[1024,2048]{1,0:T(8,128)(2,1)} custom-call(s32[2]{0:T(128)} %pad_add_fusion.place, bf16[512,1024]{1,0:T(8,128)(2,1)} %get-tuple-element.222.act.refs_0_, bf16[1024,2048]{1,0:T(8,128)(2,1)} %down.3), custom_call_target="tpu_custom_call" | custom-call | flops 1000 | bytes 15001000 | tf_op jit(solution)/shard_map/out_product/pallas_call | solution.py:158
  257.5 16.0 %collective-permute-done.24.refs_1_ = bf16[256,2048]{1,0:T(8,128)(2,1)S(1)} collective-permute-done((bf16[256,2048]{1,0:T(8,128)(2,1)S(1)}, bf16[256,2048]{1,0:T(8,128)(2,1)S(1)}, u32[]{:S(2)}, u32[]{:S(2)}) %collective-permute-start.24) | collective-permute-done | bytes 1048608 | tf_op jit(solution)/shard_map/ppermute | solution.py:70
  279.4 8.5 %collective-permute-done.26.refs_5_ = bf16[128,2048]{1,0:T(8,128)(2,1)S(1)} collective-permute-done((bf16[128,2048]{1,0:T(8,128)(2,1)S(1)}, bf16[128,2048]{1,0:T(8,128)(2,1)S(1)}, u32[]{:S(2)}, u32[]{:S(2)}) %collective-permute-start.26) | collective-permute-done | bytes 524320 | tf_op jit(solution)/shard_map/ppermute | solution.py:70
  295.5 11.8 %all-gather.12.cloned.1.call-done.dn = bf16[512,2048]{1,0:T(8,128)(2,1)} async-done(((bf16[512,256]{1,0:T(8,128)(2,1)}), bf16[512,2048]{1,0:T(8,128)(2,1)}) %all-gather.12.cloned.1.call-update) | async-done | bytes 2097168 | tf_op jit(solution)/shard_map/all_gather | solution.py:57
  307.4 11.3 %cross_backward.1 = (bf16[512,2048]{1,0:T(8,128)(2,1)}, bf16[512,256]{1,0:T(8,128)(2,1)}, bf16[256,512]{1,0:T(8,128)(2,1)}, bf16[1024,2048]{1,0:T(8,128)(2,1)}, f32[1,2048]{1,0:T(1,128)}) custom-call(s32[2]{0:T(128)} %pad_add_fusion.place, bf16[512,2048]{1,0:T(8,128)(2,1)} %get-tuple-element.213.three.refs_0_, ...), custom_call_target="tpu_custom_call", output_to_operand_aliasing={{3}: (11, {})} | custom-call | flops 1000 | bytes 20001000 | tf_op jit(solution)/shard_map/cross_backward/pallas_call | solution.py:158
  318.8 5.6 %cross_parts.1 = (bf16[128,2048]{1,0:T(8,128)(2,1)}, bf16[128,2048]{1,0:T(8,128)(2,1)}, bf16[128,2048]{1,0:T(8,128)(2,1)}, bf16[128,2048]{1,0:T(8,128)(2,1)}) custom-call(s32[2]{0:T(128)} %pad_add_fusion.place, bf16[512,256]{1,0:T(8,128)(2,1)} %get-tuple-element.233.refs_0_, bf16[512,2048]{1,0:T(8,128)(2,1)} %get-tuple-element.234.refs_1_.g2, ...), custom_call_target="tpu_custom_call" | custom-call | flops 1000 | bytes 1000 | tf_op jit(solution)/shard_map/cross_parts/pallas_call | solution.py:158
  332.8 5.0 text_back.1.room
  339.4 12.5 %collective-permute-done.37 = bf16[128,2048]{1,0:T(8,128)(2,1)} collective-permute-done((bf16[128,2048]{1,0:T(8,128)(2,1)}, bf16[128,2048]{1,0:T(8,128)(2,1)}, u32[]{:S(2)}, u32[]{:S(2)}) %collective-permute-start.37) | collective-permute-done | bytes 524320 | tf_op jit(solution)/shard_map/ppermute | solution.py:70
  351.9 10.2 %collective-permute-done.34.refs_3_ = bf16[256,1024]{1,0:T(8,128)(2,1)} collective-permute-done((bf16[256,1024]{1,0:T(8,128)(2,1)S(1)}, bf16[256,1024]{1,0:T(8,128)(2,1)}, u32[]{:S(2)}, u32[]{:S(2)}) %collective-permute-start.34) | collective-permute-done | bytes 524320 | tf_op jit(solution)/shard_map/ppermute | solution.py:70
  362.1 5.8 %reduce-scatter.12.cloned.1.call-done = bf16[1024,256]{1,0:T(8,128)(2,1)} async-done(((bf16[1024,2048]{1,0:T(8,128)(2,1)}), bf16[1024,256]{1,0:T(8,128)(2,1)}) %reduce-scatter.12.cloned.1.call-update) | async-done | bytes 524304 | tf_op jit(solution)/shard_map/reduce_scatter | solution.py:61
  372.9 17.8 %down_grads.1 = f32[1024,2048]{1,0:T(8,128)} custom-call(s32[2]{0:T(128)} %pad_add_fusion.place, bf16[512,1024]{1,0:T(8,128)(2,1)} %get-tuple-element.222.act.refs_0_, bf16[512,1024]{1,0:T(8,128)(2,1)} %collective-permute-done.32.refs_1_, bf16[512,1024]{1,0:T(8,128)(2,1)} %collective-permute-done.33.refs_2_, ...), custom_call_target="tpu_custom_call" | custom-call | flops 1000 | bytes 1000 | tf_op jit(solution)/shard_map/down_grads/pallas_call | solution.py:158
  393.9 4.9 all-gather.14.cloned.1.call-done.dn
  401.7 16.2 %self_backward.1 = (f32[512,256]{1,0:T(8,128)}, bf16[512,2048]{1,0:T(8,128)(2,1)}, bf16[512,768]{1,0:T(8,128)(2,1)}, bf16[1056,2048]{1,0:T(8,128)(2,1)}, f32[1,2048]{1,0:T(1,128)}) custom-call(s32[2]{0:T(128)} %pad_add_fusion.place, bf16[512,2048]{1,0:T(8,128)(2,1)} %get-tuple-element.329.one.refs_0_, ...), custom_call_target="tpu_custom_call", output_to_operand_aliasing={{3}: (14, {})} | custom-call | flops 1000 | bytes 27001000 | tf_op jit(solution)/shard_map/self_backward/pallas_call | solution.py:158
  430.2 5.6 %collective-permute-done.47.refs_10_ = bf16[256,512]{1,0:T(8,128)(2,1)S(1)} collective-permute-done((bf16[256,512]{1,0:T(8,128)(2,1)S(1)}, bf16[256,512]{1,0:T(8,128)(2,1)S(1)}, u32[]{:S(2)}, u32[]{:S(2)}) %collective-permute-start.47) | collective-permute-done | bytes 262176 | tf_op jit(solution)/shard_map/ppermute | solution.py:70
  438.8 4.1 self_parts.1
  442.9 16.9 %up_grads.1 = f32[2048,1024]{1,0:T(8,128)} custom-call(s32[2]{0:T(128)} %pad_add_fusion.place, bf16[512,2048]{1,0:T(8,128)(2,1)} %get-tuple-element.213.three.refs_0_, bf16[256,2048]{1,0:T(8,128)(2,1)} %copy-done.5, bf16[256,2048]{1,0:T(8,128)(2,1)} %copy-done.18, bf16[256,2048]{1,0:T(8,128)(2,1)} %copy-done.6, ...), custom_call_target="tpu_custom_call" | custom-call | flops 1000 | bytes 14001000 | tf_op jit(solution)/shard_map/up_grads/pallas_call | solution.py:158
  459.8 11.9 %text_grads.1 = (f32[8,2,256,256]{3,2,1,0:T(8,128)}, f32[8,2,256,256]{3,2,1,0:T(8,128)}) custom-call(s32[2]{0:T(128)} %pad_add_fusion.place, bf16[1552,2048]{1,0:T(8,128)(2,1)} %all-gather.6.cloned.1.call-done.zero.vec.refs_0_.refs_1_.seed.g3.refs_5_.refs_6_.own, bf16[256,2048]{1,0:T(8,128)(2,1)} %copy-done.11, bf16[256,2048]{1,0:T(8,128)(2,1)} %copy-done.23, ...), custom_call_target="tpu_custom_call" | custom-call | flops 1000 | bytes 15001000 | tf_op jit(solution)/shard_map/text_grads/pallas_call | solution.py:158
  478.5 3.7 self_end.1
  493.4 4.5 cross_finish.1
  507.4 13.6 %self_grads.1 = (f32[2048,256]{1,0:T(8,128)}, f32[2048,256]{1,0:T(8,128)}, f32[2048,256]{1,0:T(8,128)}) custom-call(s32[2]{0:T(128)} %pad_add_fusion.place, bf16[512,2048]{1,0:T(8,128)(2,1)} %get-tuple-element.329.one.refs_0_, bf16[256,2048]{1,0:T(8,128)(2,1)} %copy-done.3, bf16[256,2048]{1,0:T(8,128)(2,1)} %copy-done.16, bf16[256,2048]{1,0:T(8,128)(2,1)} %copy-done.4, ...), custom_call_target="tpu_custom_call" | custom-call | flops 1000 | bytes 40001000 | tf_op jit(solution)/shard_map/self_grads/pallas_call | solution.py:158
  (279 shorter events, 133.6 us)
Async XLA Ops:
  7.2 71.4 %all-gather.6.cloned.1.call-start = ((), (), s32[]{:S(2)}) async-start(), calls=%async_computation.5 | async-start | bytes 7151616 | tf_op jit(solution)/shard_map/all_gather | solution.py:57
  9.7 112.6 %reduce-scatter.6.cloned.1.call-start = ((), (), s32[]{:S(2)}) async-start(), calls=%async_computation.6 | async-start | bytes 2359296 | tf_op jit(solution)/shard_map/reduce_scatter | solution.py:61
  88.3 65.3 %all-gather.8.cloned.1.call-start = ((), (), s32[]{:S(2)}) async-start(), calls=%async_computation.7 | async-start | bytes 2359296 | tf_op jit(solution)/shard_map/all_gather | solution.py:57
  91.1 25.3 %collective-permute-start = (bf16[256,2048]{1,0:T(8,128)(2,1)S(1)}, bf16[256,2048]{1,0:T(8,128)(2,1)S(1)}, u32[]{:S(2)}, u32[]{:S(2)}) collective-permute-start(bf16[256,2048]{1,0:T(8,128)(2,1)S(1)} %get-tuple-element.363), channel_id=1, source_target_pairs={{0,8},{8,0},{16,24},{24,16},{1,9},{9,1},{17,25},{25,17},{2,10},{10... | collective-permute-start | bytes 3145736 | tf_op jit(solution)/shard_map/ppermute | solution.py:70
  92.6 25.1 %collective-permute-start.1 = (bf16[256,2048]{1,0:T(8,128)(2,1)S(1)}, bf16[256,2048]{1,0:T(8,128)(2,1)}, u32[]{:S(2)}, u32[]{:S(2)}) collective-permute-start(bf16[256,2048]{1,0:T(8,128)(2,1)S(1)} %get-tuple-element.363), channel_id=1, source_target_pairs={{0,16},{8,24},{16,0},{24,8},{1,17},{9,25},{17,1},{25,9},{2,18},{10... | collective-permute-start | bytes 3145736 | tf_op jit(solution)/shard_map/ppermute | solution.py:70
  122.3 75.4 %reduce-scatter.8.cloned.1.call-start = ((), (), s32[]{:S(2)}) async-start(), calls=%async_computation.8 | async-start | bytes 2359296 | tf_op jit(solution)/shard_map/reduce_scatter | solution.py:61
  122.4 26.2 %collective-permute-start.2 = (bf16[256,2048]{1,0:T(8,128)(2,1)S(1)}, bf16[256,2048]{1,0:T(8,128)(2,1)S(1)}, u32[]{:S(2)}, u32[]{:S(2)}) collective-permute-start(bf16[256,2048]{1,0:T(8,128)(2,1)S(1)} %slice.75), channel_id=1, source_target_pairs={{0,8},{8,0},{16,24},{24,16},{1,9},{9,1},{17,25},{25,17},{2,10},{10... | collective-permute-start | bytes 3145736 | tf_op jit(solution)/shard_map/ppermute | solution.py:70
  123.9 26.1 %collective-permute-start.3 = (bf16[256,2048]{1,0:T(8,128)(2,1)S(1)}, bf16[256,2048]{1,0:T(8,128)(2,1)S(1)}, u32[]{:S(2)}, u32[]{:S(2)}) collective-permute-start(bf16[256,2048]{1,0:T(8,128)(2,1)S(1)} %slice.75), channel_id=1, source_target_pairs={{0,16},{8,24},{16,0},{24,8},{1,17},{9,25},{17,1},{25,9},{2,18},{10... | collective-permute-start | bytes 3145736 | tf_op jit(solution)/shard_map/ppermute | solution.py:70
  126.2 36.4 %collective-permute-start.4 = (bf16[128,2048]{1,0:T(8,128)(2,1)}, bf16[128,2048]{1,0:T(8,128)(2,1)}, u32[]{:S(2)}, u32[]{:S(2)}) collective-permute-start(bf16[128,2048]{1,0:T(8,128)(2,1)} %slice.76), channel_id=1, source_target_pairs={{0,16},{8,24},{16,0},{24,8},{1,17},{9,25},{17,1},{25,9},{2,18},{10... | collective-permute-start | bytes 1572872 | tf_op jit(solution)/shard_map/ppermute | solution.py:70
  128.7 33.9 %collective-permute-start.5 = (bf16[128,2048]{1,0:T(8,128)(2,1)}, bf16[128,2048]{1,0:T(8,128)(2,1)}, u32[]{:S(2)}, u32[]{:S(2)}) collective-permute-start(bf16[128,2048]{1,0:T(8,128)(2,1)} %slice.77), channel_id=1, source_target_pairs={{0,8},{8,0},{16,24},{24,16},{1,9},{9,1},{17,25},{25,17},{2,10},{10... | collective-permute-start | bytes 1572872 | tf_op jit(solution)/shard_map/ppermute | solution.py:70
  162.6 66.0 %all-gather.10.cloned.1.call-start = ((), (), s32[]{:S(2)}) async-start(), calls=%async_computation.9 | async-start | bytes 2359296 | tf_op jit(solution)/shard_map/all_gather | solution.py:57
  197.7 78.5 %reduce-scatter.10.cloned.1.call-start = ((), (), s32[]{:S(2)}) async-start(), calls=%async_computation.10 | async-start | bytes 2359296 | tf_op jit(solution)/shard_map/reduce_scatter | solution.py:61
  199.3 23.3 %collective-permute-start.17 = (bf16[256,2048]{1,0:T(8,128)(2,1)}, bf16[256,2048]{1,0:T(8,128)(2,1)S(1)}, u32[]{:S(2)}, u32[]{:S(2)}) collective-permute-start(bf16[256,2048]{1,0:T(8,128)(2,1)} %get-tuple-element.362), channel_id=1, source_target_pairs={{0,16},{8,24},{16,0},{24,8},{1,17},{9,25},{17,1},{25,9},{2,18},{10... | collective-permute-start | bytes 3145736 | tf_op jit(solution)/shard_map/ppermute | solution.py:70
  241.2 66.1 %all-gather.12.cloned.1.call-start = ((), (), s32[]{:S(2)}) async-start(), calls=%async_computation.11 | async-start | bytes 2359296 | tf_op jit(solution)/shard_map/all_gather | solution.py:57
  248.2 25.3 %collective-permute-start.24 = (bf16[256,2048]{1,0:T(8,128)(2,1)S(1)}, bf16[256,2048]{1,0:T(8,128)(2,1)S(1)}, u32[]{:S(2)}, u32[]{:S(2)}) collective-permute-start(bf16[256,2048]{1,0:T(8,128)(2,1)S(1)} %slice.82), channel_id=1, source_target_pairs={{0,8},{8,0},{16,24},{24,16},{1,9},{9,1},{17,25},{25,17},{2,10},{10... | collective-permute-start | bytes 3145736 | tf_op jit(solution)/shard_map/ppermute | solution.py:70
  249.4 25.1 %collective-permute-start.25 = (bf16[256,2048]{1,0:T(8,128)(2,1)S(1)}, bf16[256,2048]{1,0:T(8,128)(2,1)S(1)}, u32[]{:S(2)}, u32[]{:S(2)}) collective-permute-start(bf16[256,2048]{1,0:T(8,128)(2,1)S(1)} %slice.82), channel_id=1, source_target_pairs={{0,16},{8,24},{16,0},{24,8},{1,17},{9,25},{17,1},{25,9},{2,18},{10... | collective-permute-start | bytes 3145736 | tf_op jit(solution)/shard_map/ppermute | solution.py:70
  276.2 91.7 %reduce-scatter.12.cloned.1.call-start = ((), (), s32[]{:S(2)}) async-start(), calls=%async_computation.12 | async-start | bytes 4718592 | tf_op jit(solution)/shard_map/reduce_scatter | solution.py:61
  288.4 30.2 %collective-permute-start.32 = (bf16[512,1024]{1,0:T(8,128)(2,1)S(1)}, bf16[512,1024]{1,0:T(8,128)(2,1)}, u32[]{:S(2)}, u32[]{:S(2)}) collective-permute-start(bf16[512,1024]{1,0:T(8,128)(2,1)S(1)} %copy-done.2), channel_id=1, source_target_pairs={{0,8},{8,0},{16,24},{24,16},{1,9},{9,1},{17,25},{25,17},{2,10},{10... | collective-permute-start | bytes 3145736 | tf_op jit(solution)/shard_map/ppermute | solution.py:70
  289.8 28.8 %collective-permute-start.33 = (bf16[512,1024]{1,0:T(8,128)(2,1)S(1)}, bf16[512,1024]{1,0:T(8,128)(2,1)}, u32[]{:S(2)}, u32[]{:S(2)}) collective-permute-start(bf16[512,1024]{1,0:T(8,128)(2,1)S(1)} %copy-done.2), channel_id=1, source_target_pairs={{0,16},{8,24},{16,0},{24,8},{1,17},{9,25},{17,1},{25,9},{2,18},{10... | collective-permute-start | bytes 3145736 | tf_op jit(solution)/shard_map/ppermute | solution.py:70
  318.7 80.1 %all-gather.14.cloned.1.call-start = ((), (), s32[]{:S(2)}) async-start(), calls=%async_computation.13 | async-start | bytes 2359296 | tf_op jit(solution)/shard_map/all_gather | solution.py:57
  325.6 26.3 %collective-permute-start.37 = (bf16[128,2048]{1,0:T(8,128)(2,1)}, bf16[128,2048]{1,0:T(8,128)(2,1)}, u32[]{:S(2)}, u32[]{:S(2)}) collective-permute-start(bf16[128,2048]{1,0:T(8,128)(2,1)} %get-tuple-element.238), channel_id=1, source_target_pairs={{0,16},{8,24},{16,0},{24,8},{1,17},{9,25},{17,1},{25,9},{2,18},{10... | collective-permute-start | bytes 1572872 | tf_op jit(solution)/shard_map/ppermute | solution.py:70
  327.0 24.9 %collective-permute-start.38 = (bf16[128,2048]{1,0:T(8,128)(2,1)}, bf16[128,2048]{1,0:T(8,128)(2,1)}, u32[]{:S(2)}, u32[]{:S(2)}) collective-permute-start(bf16[128,2048]{1,0:T(8,128)(2,1)} %get-tuple-element.239), channel_id=1, source_target_pairs={{0,24},{8,16},{16,8},{24,0},{1,25},{9,17},{17,9},{25,1},{2,26},{10... | collective-permute-start | bytes 1572872 | tf_op jit(solution)/shard_map/ppermute | solution.py:70
  328.9 33.2 %collective-permute-start.34 = (bf16[256,1024]{1,0:T(8,128)(2,1)S(1)}, bf16[256,1024]{1,0:T(8,128)(2,1)}, u32[]{:S(2)}, u32[]{:S(2)}) collective-permute-start(bf16[256,1024]{1,0:T(8,128)(2,1)S(1)} %slice.85), channel_id=1, source_target_pairs={{0,16},{8,24},{16,0},{24,8},{1,17},{9,25},{17,1},{25,9},{2,18},{10... | collective-permute-start | bytes 1572872 | tf_op jit(solution)/shard_map/ppermute | solution.py:70
  331.3 30.9 %collective-permute-start.35 = (bf16[256,1024]{1,0:T(8,128)(2,1)S(1)}, bf16[256,1024]{1,0:T(8,128)(2,1)}, u32[]{:S(2)}, u32[]{:S(2)}) collective-permute-start(bf16[256,1024]{1,0:T(8,128)(2,1)S(1)} %slice.86), channel_id=1, source_target_pairs={{0,8},{8,0},{16,24},{24,16},{1,9},{9,1},{17,25},{25,17},{2,10},{10... | collective-permute-start | bytes 1572872 | tf_op jit(solution)/shard_map/ppermute | solution.py:70
  369.6 105.0 %reduce-scatter.14.cloned.1.call-start = ((), (), s32[]{:S(2)}) async-start(), calls=%async_computation.14 | async-start | bytes 4866048 | tf_op jit(solution)/shard_map/reduce_scatter | solution.py:61
  369.9 22.8 %collective-permute-start.39 = (bf16[512,1024]{1,0:T(8,128)(2,1)S(1)}, bf16[512,1024]{1,0:T(8,128)(2,1)S(1)}, u32[]{:S(2)}, u32[]{:S(2)}) collective-permute-start(bf16[512,1024]{1,0:T(8,128)(2,1)S(1)} %copy-done.17), channel_id=1, source_target_pairs={{0,8},{8,0},{16,24},{24,16},{1,9},{9,1},{17,25},{25,17},{2,10},{10... | collective-permute-start | bytes 3145736 | tf_op jit(solution)/shard_map/ppermute | solution.py:70
  371.4 22.5 %collective-permute-start.40 = (bf16[512,1024]{1,0:T(8,128)(2,1)S(1)}, bf16[512,1024]{1,0:T(8,128)(2,1)S(1)}, u32[]{:S(2)}, u32[]{:S(2)}) collective-permute-start(bf16[512,1024]{1,0:T(8,128)(2,1)S(1)} %copy-done.17), channel_id=1, source_target_pairs={{0,16},{8,24},{16,0},{24,8},{1,17},{9,25},{17,1},{25,9},{2,18},{10... | collective-permute-start | bytes 3145736 | tf_op jit(solution)/shard_map/ppermute | solution.py:70
  423.9 49.7 %collective-permute-start.49 = (bf16[512,768]{1,0:T(8,128)(2,1)S(1)}, bf16[512,768]{1,0:T(8,128)(2,1)S(1)}, u32[]{:S(2)}, u32[]{:S(2)}) collective-permute-start(bf16[512,768]{1,0:T(8,128)(2,1)S(1)} %copy-done.25), channel_id=1, source_target_pairs={{0,8},{8,0},{16,24},{24,16},{1,9},{9,1},{17,25},{25,17},{2,10},{10... | collective-permute-start | bytes 2359304 | tf_op jit(solution)/shard_map/ppermute | solution.py:70
  424.5 50.1 %collective-permute-start.50 = (bf16[512,768]{1,0:T(8,128)(2,1)S(1)}, bf16[512,768]{1,0:T(8,128)(2,1)S(1)}, u32[]{:S(2)}, u32[]{:S(2)}) collective-permute-start(bf16[512,768]{1,0:T(8,128)(2,1)S(1)} %copy-done.25), channel_id=1, source_target_pairs={{0,16},{8,24},{16,0},{24,8},{1,17},{9,25},{17,1},{25,9},{2,18},{10... | collective-permute-start | bytes 2359304 | tf_op jit(solution)/shard_map/ppermute | solution.py:70
  429.7 42.1 %collective-permute-start.43 = (bf16[128,2048]{1,0:T(8,128)(2,1)S(1)}, bf16[128,2048]{1,0:T(8,128)(2,1)S(1)}, u32[]{:S(2)}, u32[]{:S(2)}) collective-permute-start(bf16[128,2048]{1,0:T(8,128)(2,1)S(1)} %add_convert_fusion.refs_0_), channel_id=1, source_target_pairs={{0,8},{8,0},{16,24},{24,16},{1,9},{9,1},{17,25},{25,17},{2,10},{10... | collective-permute-start | bytes 1572872 | tf_op jit(solution)/shard_map/ppermute | solution.py:70
  435.9 37.7 %collective-permute-start.44 = (bf16[128,2048]{1,0:T(8,128)(2,1)S(1)}, bf16[128,2048]{1,0:T(8,128)(2,1)S(1)}, u32[]{:S(2)}, u32[]{:S(2)}) collective-permute-start(bf16[128,2048]{1,0:T(8,128)(2,1)S(1)} %add_convert_fusion.refs_0_), channel_id=1, source_target_pairs={{0,16},{8,24},{16,0},{24,8},{1,17},{9,25},{17,1},{25,9},{2,18},{10... | collective-permute-start | bytes 1572872 | tf_op jit(solution)/shard_map/ppermute | solution.py:70
  436.6 37.0 %collective-permute-start.45 = (bf16[128,2048]{1,0:T(8,128)(2,1)S(1)}, bf16[128,2048]{1,0:T(8,128)(2,1)S(1)}, u32[]{:S(2)}, u32[]{:S(2)}) collective-permute-start(bf16[128,2048]{1,0:T(8,128)(2,1)S(1)} %add_convert_fusion.refs_0_), channel_id=1, source_target_pairs={{0,24},{8,16},{16,8},{24,0},{1,25},{9,17},{17,9},{25,1},{2,26},{10... | collective-permute-start | bytes 1572872 | tf_op jit(solution)/shard_map/ppermute | solution.py:70
  (95 other events, 1214.5 us)
Sparse Core Ops, SparseCore 0:
  10.2 68.4 all-gather.5
  88.4 33.8 reduce-scatter.5
  123.8 29.6 all-gather.7
  162.8 34.8 reduce-scatter.7
  199.1 29.4 all-gather.9
  241.4 34.8 reduce-scatter.9
  277.8 29.5 all-gather.11
  318.8 49.0 reduce-scatter.11
  369.7 28.9 all-gather.13
  419.7 50.5 reduce-scatter.13

commit v3 on v2

--- a/solution.py
+++ b/solution.py
@@ -23,21 +23,19 @@
 ) = range(14)
 DONE_BY = {
     T1: SCATTERED1, KV: SCATTERED1, T2: PARTIAL2, X1: MIXED1, X2: SCATTERED2, T3: SCATTERED2,
-    DA: SCATTERED2, Y1: PARTIAL3, X3: SCATTERED2, Y2: PARTIAL3, F1: SCATTERED3, OUT: SCATTERED3,
-    Y3: SCATTERED3, F2: MIXED3, A1: PARTIAL4, A2: SCATTERED4, F3: MIXED3, C0: SCATTERED5,
-    TB: SCATTERED4, U1: MIXED4, C1: SCATTERED4, GD: MIXED4, U2: PARTIAL5, GU: SCATTERED5,
-    GT: SCATTERED5, Q1: SCATTERED5, Q2: SMALL, S0: SCATTERED5, C2: SCATTERED5, D2: SCATTERED5,
-    C3: SMALL,
+    DA: SCATTERED2, Y1: PARTIAL3, X3: SCATTERED2, Y2: PARTIAL3, F1: SCATTERED3, OUT: MIXED3,
+    Y3: SCATTERED3, F2: MIXED3, A1: PARTIAL4, A2: MIXED4, F3: MIXED3, C0: SCATTERED4,
+    TB: SCATTERED4, U1: SCATTERED4, C1: PARTIAL5, GD: SCATTERED4, U2: MIXED4, GU: SCATTERED5,
+    GT: MIXED4, Q1: SMALL, Q2: SCATTERED5, S0: SCATTERED5, D2: PARTIAL5, GQ: SCATTERED5, C2: SMALL,
 }
 AFTER = {
-    A1: (F2,), U1: (TB,), S1: (Q2,), GQ: (S1, SM,), F1: (Y3,), GT: (GU,), CF: (SM,), SF: (SM,),
-    D1: (C1, U1,), SA: (SM,), C3: (U2,),
+    A1: (F2,), U1: (A2,), S1: (Q2,), F1: (Y3,), CF: (SM,), SF: (SM,), D1: (U1,), SA: (SM,),
 }
-DIRECT = (C2, D1, S2,)
+DIRECT = (C2, D1, Q1,)
 COST = dict(
     self_forward=17, text_project=25, cross_forward=0, seed_product=3, feed_both=6, out_product=15,
-    cross_backward=20, self_backward=27, self_end=5, text_back=8, down_grads=0, up_grads=14,
-    text_grads=15, self_grads=40, cross_parts=0, self_parts=6, cross_finish=0, self_finish=25,
+    cross_backward=20, self_backward=27, self_end=10, text_back=8, down_grads=0, up_grads=14,
+    text_grads=15, self_grads=40, cross_parts=0, self_parts=10, cross_finish=0, self_finish=0,
 )
 
 

time: 540 us -> 532 us (0.985)
  waiting for transfers between devices: 259 us -> 244 us
  Pallas kernels: 166 us -> 175 us
    pallas_call x18, Pallas kernels: 163 us -> 173 us  [call(): pl.pallas_call(kernel, grid_spec=pltpu.PrefetchScalarGridSpec(num_scalar_...]
    all_gather x5, waiting for transfers between devices: 91.3 us -> 82.9 us  [gather_cols(): return lax.all_gather(array, TENSOR, axis=1, tiled=True)]
    unnamed x110 -> x102, local copies, waits for them, and re-layouts: 11.5 us -> 8.11 us
  transfers between devices with their start and end apart: 72 -> 72, of which waited for: 37 -> 29; matrix products, arithmetic and copies ran while one was open for 3% -> 4% of each run, Pallas kernels for 28% -> 30%
where the time goes in v3:
time: 532 us; the launch traced here: 525 us
  waiting for transfers between devices  244 us (46%)
  Pallas kernels  175 us (33%)
  starting transfers between devices  62.8 us (12%)
  local copies, waits for them, and re-layouts  22.4 us (4%)
  between operations  15.1 us (3%)
  other arithmetic  6.07 us (1%)
    pallas_call x18, Pallas kernels, call(): pl.pallas_call(kernel, grid_spec=pltpu.PrefetchScalarGridSpec(num_scalar_...  173 us
    ppermute x46, waiting for transfers between devices, hop(): return lax.ppermute(array, BATCH, pairs)  138 us
    all_gather x5, waiting for transfers between devices, gather_cols(): return lax.all_gather(array, TENSOR, axis=1, tiled=True)  82.9 us
    ppermute x46, starting transfers between devices, hop(): return lax.ppermute(array, BATCH, pairs)  58.8 us
    reduce_scatter x5, waiting for transfers between devices, scatter_cols(): return lax.psum_scatter(array, TENSOR, scatter_dimension=1, tiled=True)  17.8 us
  transfers between devices with their start and end apart: 72, of which 29 were waited for; matrix products, arithmetic and copies ran while one was open for 4% of the time, Pallas kernels for 30%

profile of v3, /device:TPU:0, one launch (start us, length us, event | category | flops | bytes accessed | tf_op | source)
XLA Modules:
  0.0 525.0 jit_solution(17337163471393931513)
XLA Ops:
  10.4 68.3 %all-gather.6.cloned.1.call-done.zero.vec.refs_0_.refs_1_.seed.g3.refs_5_.refs_6_.own = bf16[1552,2048]{1,0:T(8,128)(2,1)} async-done(((bf16[1552,256]{1,0:T(8,128)(2,1)}), bf16[1552,2048]{1,0:T(8,128)(2,1)}) %all-gather.6.cloned.1.call-update) | async-done | bytes 6357008 | tf_op jit(solution)/shard_map/all_gather | solution.py:55
  78.6 9.6 %self_forward.1 = (bf16[512,2048]{1,0:T(8,128)(2,1)}, bf16[512,256]{1,0:T(8,128)(2,1)}, bf16[512,256]{1,0:T(8,128)(2,1)}, bf16[512,256]{1,0:T(8,128)(2,1)}, bf16...) custom-call(s32[2]{0:T(128)} %pad_add_fusion.place, ...), custom_call_target="tpu_custom_call" | custom-call | flops 1000 | bytes 17001000 | tf_op jit(solution)/shard_map/self_forward/pallas_call | solution.py:156
  94.0 5.1 text_project.1
  99.1 17.3 %collective-permute-done.refs_0_ = bf16[256,2048]{1,0:T(8,128)(2,1)S(1)} collective-permute-done((bf16[256,2048]{1,0:T(8,128)(2,1)S(1)}, bf16[256,2048]{1,0:T(8,128)(2,1)S(1)}, u32[]{:S(2)}, u32[]{:S(2)}) %collective-permute-start) | collective-permute-done | bytes 1048608 | tf_op jit(solution)/shard_map/ppermute | solution.py:68
  117.7 4.6 reduce-scatter.6.cloned.1.call-done
  129.3 19.3 %collective-permute-done.2.refs_1_ = bf16[256,2048]{1,0:T(8,128)(2,1)S(1)} collective-permute-done((bf16[256,2048]{1,0:T(8,128)(2,1)S(1)}, bf16[256,2048]{1,0:T(8,128)(2,1)S(1)}, u32[]{:S(2)}, u32[]{:S(2)}) %collective-permute-start.2) | collective-permute-done | bytes 1048608 | tf_op jit(solution)/shard_map/ppermute | solution.py:68
  150.0 3.5 all-gather.8.cloned.1.call-done.add
  153.5 9.1 %cross_forward.1 = (bf16[512,2048]{1,0:T(8,128)(2,1)}, bf16[512,2048]{1,0:T(8,128)(2,1)}, bf16[512,256]{1,0:T(8,128)(2,1)}, bf16[512,256]{1,0:T(8,128)(2,1)}, bf...) custom-call(s32[2]{0:T(128)} %pad_add_fusion.place, ...), custom_call_target="tpu_custom_call" | custom-call | flops 1000 | bytes 1000 | tf_op jit(solution)/shard_map/cross_forward/pallas_call | solution.py:156
  167.5 10.2 %collective-permute-done.10.refs_5_ = bf16[128,2048]{1,0:T(8,128)(2,1)S(1)} collective-permute-done((bf16[128,2048]{1,0:T(8,128)(2,1)S(1)}, bf16[128,2048]{1,0:T(8,128)(2,1)S(1)}, u32[]{:S(2)}, u32[]{:S(2)}) %collective-permute-start.10) | collective-permute-done | bytes 524320 | tf_op jit(solution)/shard_map/ppermute | solution.py:68
  179.3 6.8 %seed_product.1.dact = f32[512,1024]{1,0:T(8,128)} custom-call(s32[2]{0:T(128)} %pad_add_fusion.place, bf16[1552,2048]{1,0:T(8,128)(2,1)} %all-gather.6.cloned.1.call-done.zero.vec.refs_0_.refs_1_.seed.g3.refs_5_.refs_6_.own, bf16[1024,2048]{1,0:T(8,128)(2,1)} %down.3), custom_call_target="tpu_custom_call" | custom-call | flops 1000 | bytes 3001000 | tf_op jit(solution)/shard_map/seed_product/pallas_call | solution.py:156
  188.5 9.2 %reduce-scatter.8.cloned.1.call-done = bf16[512,256]{1,0:T(8,128)(2,1)} async-done(((bf16[512,2048]{1,0:T(8,128)(2,1)}), bf16[512,256]{1,0:T(8,128)(2,1)}) %reduce-scatter.8.cloned.1.call-update) | async-done | bytes 262160 | tf_op jit(solution)/shard_map/reduce_scatter | solution.py:59
  200.8 19.7 %collective-permute-done.16.refs_7_ = bf16[256,2048]{1,0:T(8,128)(2,1)} collective-permute-done((bf16[256,2048]{1,0:T(8,128)(2,1)}, bf16[256,2048]{1,0:T(8,128)(2,1)}, u32[]{:S(2)}, u32[]{:S(2)}) %collective-permute-start.16) | collective-permute-done | bytes 1048608 | tf_op jit(solution)/shard_map/ppermute | solution.py:68
  228.6 12.6 %feed_both.1 = (f32[512,256]{1,0:T(8,128)}, f32[512,1]{1,0:T(8,128)}, bf16[512,2048]{1,0:T(8,128)(2,1)}, bf16[512,1024]{1,0:T(8,128)(2,1)}, bf16[512,1024]{1,0:T(8,128)(2,1)}, /*index=5*/bf16[512,2048]{1,0:T(8,128)(2,1)}) custom-call(s32[2]{0:T(128)} %pad_add_fusion.place, bf16[512,2048]{1,0:T(8,128)(2,1)} %get-tuple-element.187.one, ...), custom_call_target="tpu_custom_call" | custom-call | flops 1000 | bytes 6001000 | tf_op jit(solution)/shard_map/feed_both/pallas_call | solution.py:156
  242.9 3.6 collective-permute-done.22.refs_13_
  250.0 22.6 %collective-permute-done.24.refs_1_ = bf16[256,2048]{1,0:T(8,128)(2,1)S(1)} collective-permute-done((bf16[256,2048]{1,0:T(8,128)(2,1)S(1)}, bf16[256,2048]{1,0:T(8,128)(2,1)S(1)}, u32[]{:S(2)}, u32[]{:S(2)}) %collective-permute-start.24) | collective-permute-done | bytes 1048608 | tf_op jit(solution)/shard_map/ppermute | solution.py:68
  279.4 8.0 %collective-permute-done.26.refs_5_ = bf16[128,2048]{1,0:T(8,128)(2,1)S(1)} collective-permute-done((bf16[128,2048]{1,0:T(8,128)(2,1)S(1)}, bf16[128,2048]{1,0:T(8,128)(2,1)S(1)}, u32[]{:S(2)}, u32[]{:S(2)}) %collective-permute-start.26) | collective-permute-done | bytes 524320 | tf_op jit(solution)/shard_map/ppermute | solution.py:68
  290.8 6.6 %out_product.1.room = bf16[1024,2048]{1,0:T(8,128)(2,1)} custom-call(s32[2]{0:T(128)} %pad_add_fusion.place, bf16[512,1024]{1,0:T(8,128)(2,1)} %get-tuple-element.213.act.refs_0_, bf16[1024,2048]{1,0:T(8,128)(2,1)} %down.3), custom_call_target="tpu_custom_call" | custom-call | flops 1000 | bytes 15001000 | tf_op jit(solution)/shard_map/out_product/pallas_call | solution.py:156
  299.2 8.2 %all-gather.12.cloned.1.call-done.dn = bf16[512,2048]{1,0:T(8,128)(2,1)} async-done(((bf16[512,256]{1,0:T(8,128)(2,1)}), bf16[512,2048]{1,0:T(8,128)(2,1)}) %all-gather.12.cloned.1.call-update) | async-done | bytes 2097168 | tf_op jit(solution)/shard_map/all_gather | solution.py:55
  307.3 11.3 %cross_backward.1 = (bf16[512,2048]{1,0:T(8,128)(2,1)}, bf16[512,256]{1,0:T(8,128)(2,1)}, bf16[256,512]{1,0:T(8,128)(2,1)}, bf16[1024,2048]{1,0:T(8,128)(2,1)}, f32[1,2048]{1,0:T(1,128)}) custom-call(s32[2]{0:T(128)} %pad_add_fusion.place, bf16[512,2048]{1,0:T(8,128)(2,1)} %get-tuple-element.201.three.refs_0_, ...), custom_call_target="tpu_custom_call", output_to_operand_aliasing={{3}: (11, {})} | custom-call | flops 1000 | bytes 20001000 | tf_op jit(solution)/shard_map/cross_backward/pallas_call | solution.py:156
  323.8 10.3 %collective-permute-done.34.refs_3_ = bf16[256,1024]{1,0:T(8,128)(2,1)S(1)} collective-permute-done((bf16[256,1024]{1,0:T(8,128)(2,1)S(1)}, bf16[256,1024]{1,0:T(8,128)(2,1)S(1)}, u32[]{:S(2)}, u32[]{:S(2)}) %collective-permute-start.34) | collective-permute-done | bytes 524320 | tf_op jit(solution)/shard_map/ppermute | solution.py:68
  338.1 4.8 text_back.1.room
  343.0 5.7 %cross_parts.1 = (bf16[128,2048]{1,0:T(8,128)(2,1)}, bf16[128,2048]{1,0:T(8,128)(2,1)}, bf16[128,2048]{1,0:T(8,128)(2,1)}, bf16[128,2048]{1,0:T(8,128)(2,1)}) custom-call(s32[2]{0:T(128)} %pad_add_fusion.place, bf16[512,256]{1,0:T(8,128)(2,1)} %get-tuple-element.231.refs_0_, bf16[512,2048]{1,0:T(8,128)(2,1)} %get-tuple-element.232.refs_1_.g2, ...), custom_call_target="tpu_custom_call" | custom-call | flops 1000 | bytes 1000 | tf_op jit(solution)/shard_map/cross_parts/pallas_call | solution.py:156
  348.7 17.7 %down_grads.1 = f32[1024,2048]{1,0:T(8,128)} custom-call(s32[2]{0:T(128)} %pad_add_fusion.place, bf16[512,1024]{1,0:T(8,128)(2,1)} %get-tuple-element.213.act.refs_0_, bf16[512,1024]{1,0:T(8,128)(2,1)} %collective-permute-done.32.refs_1_, bf16[512,1024]{1,0:T(8,128)(2,1)} %collective-permute-done.33.refs_2_, bf16[256,1024]{1,0:T(8,128)(2,1)} %copy-done.29, ...), custom_call_target="tpu_custom_call" | custom-call | flops 1000 | bytes 1000 | tf_op jit(solution)/shard_map/down_grads/pallas_call | solution.py:156
  380.4 5.0 collective-permute-done.41.refs_10_
  387.7 21.2 %text_grads.1 = (f32[8,2,256,256]{3,2,1,0:T(8,128)}, f32[8,2,256,256]{3,2,1,0:T(8,128)}) custom-call(s32[2]{0:T(128)} %pad_add_fusion.place, bf16[1552,2048]{1,0:T(8,128)(2,1)} %all-gather.6.cloned.1.call-done.zero.vec.refs_0_.refs_1_.seed.g3.refs_5_.refs_6_.own, bf16[256,2048]{1,0:T(8,128)(2,1)} %copy-done.9, bf16[256,2048]{1,0:T(8,128)(2,1)} %copy-done.19, ...), custom_call_target="tpu_custom_call" | custom-call | flops 1000 | bytes 15001000 | tf_op jit(solution)/shard_map/text_grads/pallas_call | solution.py:156
  409.0 16.2 %self_backward.1 = (f32[512,256]{1,0:T(8,128)}, bf16[512,2048]{1,0:T(8,128)(2,1)}, bf16[512,768]{1,0:T(8,128)(2,1)}, bf16[1056,2048]{1,0:T(8,128)(2,1)}, f32[1,2048]{1,0:T(1,128)}) custom-call(s32[2]{0:T(128)} %pad_add_fusion.place, bf16[512,2048]{1,0:T(8,128)(2,1)} %get-tuple-element.183.one.refs_0_, ...), custom_call_target="tpu_custom_call", output_to_operand_aliasing={{3}: (14, {})} | custom-call | flops 1000 | bytes 27001000 | tf_op jit(solution)/shard_map/self_backward/pallas_call | solution.py:156
  434.0 12.8 %collective-permute-done.46.refs_10_ = bf16[512,768]{1,0:T(8,128)(2,1)S(1)} collective-permute-done((bf16[512,768]{1,0:T(8,128)(2,1)S(1)}, bf16[512,768]{1,0:T(8,128)(2,1)S(1)}, u32[]{:S(2)}, u32[]{:S(2)}) %collective-permute-start.46) | collective-permute-done | bytes 786464 | tf_op jit(solution)/shard_map/ppermute | solution.py:68
  448.6 4.1 self_parts.1
  452.7 16.8 %up_grads.1 = f32[2048,1024]{1,0:T(8,128)} custom-call(s32[2]{0:T(128)} %pad_add_fusion.place, bf16[512,2048]{1,0:T(8,128)(2,1)} %get-tuple-element.201.three.refs_0_, bf16[256,2048]{1,0:T(8,128)(2,1)} %copy-done.5, bf16[256,2048]{1,0:T(8,128)(2,1)} %copy-done.14, bf16[256,2048]{1,0:T(8,128)(2,1)} %copy-done.6, ...), custom_call_target="tpu_custom_call" | custom-call | flops 1000 | bytes 14001000 | tf_op jit(solution)/shard_map/up_grads/pallas_call | solution.py:156
  471.3 13.7 %self_grads.1 = (f32[2048,256]{1,0:T(8,128)}, f32[2048,256]{1,0:T(8,128)}, f32[2048,256]{1,0:T(8,128)}) custom-call(s32[2]{0:T(128)} %pad_add_fusion.place, bf16[512,2048]{1,0:T(8,128)(2,1)} %get-tuple-element.183.one.refs_0_, bf16[256,2048]{1,0:T(8,128)(2,1)} %copy-done.3, bf16[256,2048]{1,0:T(8,128)(2,1)} %copy-done.12, bf16[256,2048]{1,0:T(8,128)(2,1)} %copy-done.4, ...), custom_call_target="tpu_custom_call" | custom-call | flops 1000 | bytes 40001000 | tf_op jit(solution)/shard_map/self_grads/pallas_call | solution.py:156
  490.3 3.7 self_end.1
  502.6 4.5 cross_finish.1
  (271 shorter events, 118.0 us)
Async XLA Ops:
  7.2 71.4 %all-gather.6.cloned.1.call-start = ((), (), s32[]{:S(2)}) async-start(), calls=%async_computation.5 | async-start | bytes 7151616 | tf_op jit(solution)/shard_map/all_gather | solution.py:55
  9.7 112.6 %reduce-scatter.6.cloned.1.call-start = ((), (), s32[]{:S(2)}) async-start(), calls=%async_computation.6 | async-start | bytes 2359296 | tf_op jit(solution)/shard_map/reduce_scatter | solution.py:59
  88.3 65.3 %all-gather.8.cloned.1.call-start = ((), (), s32[]{:S(2)}) async-start(), calls=%async_computation.7 | async-start | bytes 2359296 | tf_op jit(solution)/shard_map/all_gather | solution.py:55
  91.1 25.3 %collective-permute-start = (bf16[256,2048]{1,0:T(8,128)(2,1)S(1)}, bf16[256,2048]{1,0:T(8,128)(2,1)S(1)}, u32[]{:S(2)}, u32[]{:S(2)}) collective-permute-start(bf16[256,2048]{1,0:T(8,128)(2,1)S(1)} %get-tuple-element.339), channel_id=1, source_target_pairs={{0,8},{8,0},{16,24},{24,16},{1,9},{9,1},{17,25},{25,17},{2,10},{10... | collective-permute-start | bytes 3145736 | tf_op jit(solution)/shard_map/ppermute | solution.py:68
  92.6 25.1 %collective-permute-start.1 = (bf16[256,2048]{1,0:T(8,128)(2,1)S(1)}, bf16[256,2048]{1,0:T(8,128)(2,1)}, u32[]{:S(2)}, u32[]{:S(2)}) collective-permute-start(bf16[256,2048]{1,0:T(8,128)(2,1)S(1)} %get-tuple-element.339), channel_id=1, source_target_pairs={{0,16},{8,24},{16,0},{24,8},{1,17},{9,25},{17,1},{25,9},{2,18},{10... | collective-permute-start | bytes 3145736 | tf_op jit(solution)/shard_map/ppermute | solution.py:68
  122.3 75.3 %reduce-scatter.8.cloned.1.call-start = ((), (), s32[]{:S(2)}) async-start(), calls=%async_computation.8 | async-start | bytes 2359296 | tf_op jit(solution)/shard_map/reduce_scatter | solution.py:59
  122.5 26.2 %collective-permute-start.2 = (bf16[256,2048]{1,0:T(8,128)(2,1)S(1)}, bf16[256,2048]{1,0:T(8,128)(2,1)S(1)}, u32[]{:S(2)}, u32[]{:S(2)}) collective-permute-start(bf16[256,2048]{1,0:T(8,128)(2,1)S(1)} %slice.75), channel_id=1, source_target_pairs={{0,8},{8,0},{16,24},{24,16},{1,9},{9,1},{17,25},{25,17},{2,10},{10... | collective-permute-start | bytes 3145736 | tf_op jit(solution)/shard_map/ppermute | solution.py:68
  123.9 26.1 %collective-permute-start.3 = (bf16[256,2048]{1,0:T(8,128)(2,1)S(1)}, bf16[256,2048]{1,0:T(8,128)(2,1)S(1)}, u32[]{:S(2)}, u32[]{:S(2)}) collective-permute-start(bf16[256,2048]{1,0:T(8,128)(2,1)S(1)} %slice.75), channel_id=1, source_target_pairs={{0,16},{8,24},{16,0},{24,8},{1,17},{9,25},{17,1},{25,9},{2,18},{10... | collective-permute-start | bytes 3145736 | tf_op jit(solution)/shard_map/ppermute | solution.py:68
  126.2 36.4 %collective-permute-start.4 = (bf16[128,2048]{1,0:T(8,128)(2,1)}, bf16[128,2048]{1,0:T(8,128)(2,1)}, u32[]{:S(2)}, u32[]{:S(2)}) collective-permute-start(bf16[128,2048]{1,0:T(8,128)(2,1)} %slice.76), channel_id=1, source_target_pairs={{0,16},{8,24},{16,0},{24,8},{1,17},{9,25},{17,1},{25,9},{2,18},{10... | collective-permute-start | bytes 1572872 | tf_op jit(solution)/shard_map/ppermute | solution.py:68
  128.7 33.9 %collective-permute-start.5 = (bf16[128,2048]{1,0:T(8,128)(2,1)}, bf16[128,2048]{1,0:T(8,128)(2,1)}, u32[]{:S(2)}, u32[]{:S(2)}) collective-permute-start(bf16[128,2048]{1,0:T(8,128)(2,1)} %slice.77), channel_id=1, source_target_pairs={{0,8},{8,0},{16,24},{24,16},{1,9},{9,1},{17,25},{25,17},{2,10},{10... | collective-permute-start | bytes 1572872 | tf_op jit(solution)/shard_map/ppermute | solution.py:68
  162.6 66.0 %all-gather.10.cloned.1.call-start = ((), (), s32[]{:S(2)}) async-start(), calls=%async_computation.9 | async-start | bytes 2359296 | tf_op jit(solution)/shard_map/all_gather | solution.py:55
  197.6 78.4 %reduce-scatter.10.cloned.1.call-start = ((), (), s32[]{:S(2)}) async-start(), calls=%async_computation.10 | async-start | bytes 2359296 | tf_op jit(solution)/shard_map/reduce_scatter | solution.py:59
  241.2 66.1 %all-gather.12.cloned.1.call-start = ((), (), s32[]{:S(2)}) async-start(), calls=%async_computation.11 | async-start | bytes 2359296 | tf_op jit(solution)/shard_map/all_gather | solution.py:55
  247.2 25.4 %collective-permute-start.24 = (bf16[256,2048]{1,0:T(8,128)(2,1)S(1)}, bf16[256,2048]{1,0:T(8,128)(2,1)S(1)}, u32[]{:S(2)}, u32[]{:S(2)}) collective-permute-start(bf16[256,2048]{1,0:T(8,128)(2,1)S(1)} %slice.82), channel_id=1, source_target_pairs={{0,8},{8,0},{16,24},{24,16},{1,9},{9,1},{17,25},{25,17},{2,10},{10... | collective-permute-start | bytes 3145736 | tf_op jit(solution)/shard_map/ppermute | solution.py:68
  248.5 25.0 %collective-permute-start.25 = (bf16[256,2048]{1,0:T(8,128)(2,1)S(1)}, bf16[256,2048]{1,0:T(8,128)(2,1)S(1)}, u32[]{:S(2)}, u32[]{:S(2)}) collective-permute-start(bf16[256,2048]{1,0:T(8,128)(2,1)S(1)} %slice.82), channel_id=1, source_target_pairs={{0,16},{8,24},{16,0},{24,8},{1,17},{9,25},{17,1},{25,9},{2,18},{10... | collective-permute-start | bytes 3145736 | tf_op jit(solution)/shard_map/ppermute | solution.py:68
  276.1 91.8 %reduce-scatter.12.cloned.1.call-start = ((), (), s32[]{:S(2)}) async-start(), calls=%async_computation.12 | async-start | bytes 4718592 | tf_op jit(solution)/shard_map/reduce_scatter | solution.py:59
  288.0 30.7 %collective-permute-start.32 = (bf16[512,1024]{1,0:T(8,128)(2,1)S(1)}, bf16[512,1024]{1,0:T(8,128)(2,1)}, u32[]{:S(2)}, u32[]{:S(2)}) collective-permute-start(bf16[512,1024]{1,0:T(8,128)(2,1)S(1)} %copy-done.2), channel_id=1, source_target_pairs={{0,8},{8,0},{16,24},{24,16},{1,9},{9,1},{17,25},{25,17},{2,10},{10... | collective-permute-start | bytes 3145736 | tf_op jit(solution)/shard_map/ppermute | solution.py:68
  289.2 29.5 %collective-permute-start.33 = (bf16[512,1024]{1,0:T(8,128)(2,1)S(1)}, bf16[512,1024]{1,0:T(8,128)(2,1)}, u32[]{:S(2)}, u32[]{:S(2)}) collective-permute-start(bf16[512,1024]{1,0:T(8,128)(2,1)S(1)} %copy-done.2), channel_id=1, source_target_pairs={{0,16},{8,24},{16,0},{24,8},{1,17},{9,25},{17,1},{25,9},{2,18},{10... | collective-permute-start | bytes 3145736 | tf_op jit(solution)/shard_map/ppermute | solution.py:68
  318.7 90.3 %all-gather.14.cloned.1.call-start = ((), (), s32[]{:S(2)}) async-start(), calls=%async_computation.13 | async-start | bytes 2359296 | tf_op jit(solution)/shard_map/all_gather | solution.py:55
  336.1 30.3 %collective-permute-start.36 = (bf16[512,1024]{1,0:T(8,128)(2,1)S(1)}, bf16[512,1024]{1,0:T(8,128)(2,1)S(1)}, u32[]{:S(2)}, u32[]{:S(2)}) collective-permute-start(bf16[512,1024]{1,0:T(8,128)(2,1)S(1)} %copy-done.13), channel_id=1, source_target_pairs={{0,8},{8,0},{16,24},{24,16},{1,9},{9,1},{17,25},{25,17},{2,10},{10... | collective-permute-start | bytes 3145736 | tf_op jit(solution)/shard_map/ppermute | solution.py:68
  337.6 28.8 %collective-permute-start.37 = (bf16[512,1024]{1,0:T(8,128)(2,1)S(1)}, bf16[512,1024]{1,0:T(8,128)(2,1)S(1)}, u32[]{:S(2)}, u32[]{:S(2)}) collective-permute-start(bf16[512,1024]{1,0:T(8,128)(2,1)S(1)} %copy-done.13), channel_id=1, source_target_pairs={{0,16},{8,24},{16,0},{24,8},{1,17},{9,25},{17,1},{25,9},{2,18},{10... | collective-permute-start | bytes 3145736 | tf_op jit(solution)/shard_map/ppermute | solution.py:68
  369.6 115.4 %reduce-scatter.14.cloned.1.call-start = ((), (), s32[]{:S(2)}) async-start(), calls=%async_computation.14 | async-start | bytes 4866048 | tf_op jit(solution)/shard_map/reduce_scatter | solution.py:59
  373.3 35.6 %collective-permute-start.38 = (bf16[256,1024]{1,0:T(8,128)(2,1)S(1)}, bf16[256,1024]{1,0:T(8,128)(2,1)S(1)}, u32[]{:S(2)}, u32[]{:S(2)}) collective-permute-start(bf16[256,1024]{1,0:T(8,128)(2,1)S(1)} %slice.89), channel_id=1, source_target_pairs={{0,16},{8,24},{16,0},{24,8},{1,17},{9,25},{17,1},{25,9},{2,18},{10... | collective-permute-start | bytes 1572872 | tf_op jit(solution)/shard_map/ppermute | solution.py:68
  374.8 34.1 %collective-permute-start.39 = (bf16[256,1024]{1,0:T(8,128)(2,1)S(1)}, bf16[256,1024]{1,0:T(8,128)(2,1)}, u32[]{:S(2)}, u32[]{:S(2)}) collective-permute-start(bf16[256,1024]{1,0:T(8,128)(2,1)S(1)} %slice.90), channel_id=1, source_target_pairs={{0,8},{8,0},{16,24},{24,16},{1,9},{9,1},{17,25},{25,17},{2,10},{10... | collective-permute-start | bytes 1572872 | tf_op jit(solution)/shard_map/ppermute | solution.py:68
  379.0 46.2 %collective-permute-start.43 = (bf16[128,2048]{1,0:T(8,128)(2,1)}, bf16[128,2048]{1,0:T(8,128)(2,1)}, u32[]{:S(2)}, u32[]{:S(2)}) collective-permute-start(bf16[128,2048]{1,0:T(8,128)(2,1)} %get-tuple-element.264), channel_id=1, source_target_pairs={{0,8},{8,0},{16,24},{24,16},{1,9},{9,1},{17,25},{25,17},{2,10},{10... | collective-permute-start | bytes 1572872 | tf_op jit(solution)/shard_map/ppermute | solution.py:68
  385.4 39.8 %collective-permute-start.44 = (bf16[128,2048]{1,0:T(8,128)(2,1)}, bf16[128,2048]{1,0:T(8,128)(2,1)}, u32[]{:S(2)}, u32[]{:S(2)}) collective-permute-start(bf16[128,2048]{1,0:T(8,128)(2,1)} %get-tuple-element.265), channel_id=1, source_target_pairs={{0,16},{8,24},{16,0},{24,8},{1,17},{9,25},{17,1},{25,9},{2,18},{10... | collective-permute-start | bytes 1572872 | tf_op jit(solution)/shard_map/ppermute | solution.py:68
  386.5 38.8 %collective-permute-start.45 = (bf16[128,2048]{1,0:T(8,128)(2,1)}, bf16[128,2048]{1,0:T(8,128)(2,1)S(1)}, u32[]{:S(2)}, u32[]{:S(2)}) collective-permute-start(bf16[128,2048]{1,0:T(8,128)(2,1)} %get-tuple-element.266), channel_id=1, source_target_pairs={{0,24},{8,16},{16,8},{24,0},{1,25},{9,17},{17,9},{25,1},{2,26},{10... | collective-permute-start | bytes 1572872 | tf_op jit(solution)/shard_map/ppermute | solution.py:68
  427.6 41.9 %collective-permute-start.47 = (bf16[512,768]{1,0:T(8,128)(2,1)S(1)}, bf16[512,768]{1,0:T(8,128)(2,1)S(1)}, u32[]{:S(2)}, u32[]{:S(2)}) collective-permute-start(bf16[512,768]{1,0:T(8,128)(2,1)S(1)} %copy-done.21), channel_id=1, source_target_pairs={{0,16},{8,24},{16,0},{24,8},{1,17},{9,25},{17,1},{25,9},{2,18},{10... | collective-permute-start | bytes 2359304 | tf_op jit(solution)/shard_map/ppermute | solution.py:68
  428.7 40.9 %collective-permute-start.48 = (bf16[512,768]{1,0:T(8,128)(2,1)S(1)}, bf16[512,768]{1,0:T(8,128)(2,1)S(1)}, u32[]{:S(2)}, u32[]{:S(2)}) collective-permute-start(bf16[512,768]{1,0:T(8,128)(2,1)S(1)} %copy-done.21), channel_id=1, source_target_pairs={{0,24},{8,16},{16,8},{24,0},{1,25},{9,17},{17,9},{25,1},{2,26},{10... | collective-permute-start | bytes 2359304 | tf_op jit(solution)/shard_map/ppermute | solution.py:68
  431.4 55.4 %collective-permute-start.49 = (bf16[128,2048]{1,0:T(8,128)(2,1)S(1)}, bf16[128,2048]{1,0:T(8,128)(2,1)S(1)}, u32[]{:S(2)}, u32[]{:S(2)}) collective-permute-start(bf16[128,2048]{1,0:T(8,128)(2,1)S(1)} %add_convert_fusion.refs_0_), channel_id=1, source_target_pairs={{0,8},{8,0},{16,24},{24,16},{1,9},{9,1},{17,25},{25,17},{2,10},{10... | collective-permute-start | bytes 1572872 | tf_op jit(solution)/shard_map/ppermute | solution.py:68
  432.8 61.2 %collective-permute-start.50 = (bf16[128,2048]{1,0:T(8,128)(2,1)S(1)}, bf16[128,2048]{1,0:T(8,128)(2,1)S(1)}, u32[]{:S(2)}, u32[]{:S(2)}) collective-permute-start(bf16[128,2048]{1,0:T(8,128)(2,1)S(1)} %add_convert_fusion.refs_0_), channel_id=1, source_target_pairs={{0,16},{8,24},{16,0},{24,8},{1,17},{9,25},{17,1},{25,9},{2,18},{10... | collective-permute-start | bytes 1572872 | tf_op jit(solution)/shard_map/ppermute | solution.py:68
  446.9 47.1 %collective-permute-start.51 = (bf16[128,2048]{1,0:T(8,128)(2,1)S(1)}, bf16[128,2048]{1,0:T(8,128)(2,1)S(1)}, u32[]{:S(2)}, u32[]{:S(2)}) collective-permute-start(bf16[128,2048]{1,0:T(8,128)(2,1)S(1)} %add_convert_fusion.refs_0_), channel_id=1, source_target_pairs={{0,24},{8,16},{16,8},{24,0},{1,25},{9,17},{17,9},{25,1},{2,26},{10... | collective-permute-start | bytes 1572872 | tf_op jit(solution)/shard_map/ppermute | solution.py:68
  (91 other events, 1154.4 us)
Sparse Core Ops, SparseCore 0:
  10.2 68.4 all-gather.5
  88.4 33.8 reduce-scatter.5
  123.9 29.6 all-gather.7
  162.8 34.8 reduce-scatter.7
  199.1 29.5 all-gather.9
  241.4 34.6 reduce-scatter.9
  277.7 29.6 all-gather.11
  318.8 49.0 reduce-scatter.11
  370.1 28.9 all-gather.13
  425.4 49.7 reduce-scatter.13

commit v4 on v3

--- a/solution.py
+++ b/solution.py
@@ -25,13 +25,14 @@
     T1: SCATTERED1, KV: SCATTERED1, T2: PARTIAL2, X1: MIXED1, X2: SCATTERED2, T3: SCATTERED2,
     DA: SCATTERED2, Y1: PARTIAL3, X3: SCATTERED2, Y2: PARTIAL3, F1: SCATTERED3, OUT: MIXED3,
     Y3: SCATTERED3, F2: MIXED3, A1: PARTIAL4, A2: MIXED4, F3: MIXED3, C0: SCATTERED4,
-    TB: SCATTERED4, U1: SCATTERED4, C1: PARTIAL5, GD: SCATTERED4, U2: MIXED4, GU: SCATTERED5,
+    TB: SCATTERED4, U1: SCATTERED4, C1: PARTIAL5, GD: SCATTERED4, U2: PARTIAL5, GU: SCATTERED5,
     GT: MIXED4, Q1: SMALL, Q2: SCATTERED5, S0: SCATTERED5, D2: PARTIAL5, GQ: SCATTERED5, C2: SMALL,
 }
 AFTER = {
     A1: (F2,), U1: (A2,), S1: (Q2,), F1: (Y3,), CF: (SM,), SF: (SM,), D1: (U1,), SA: (SM,),
+    CA: (GD,),
 }
-DIRECT = (C2, D1, Q1,)
+DIRECT = (D1, Q1,)
 COST = dict(
     self_forward=17, text_project=25, cross_forward=0, seed_product=3, feed_both=6, out_product=15,
     cross_backward=20, self_backward=27, self_end=10, text_back=8, down_grads=0, up_grads=14,

time: 532 us -> 533 us (level)
    ppermute x46 -> x47, waiting for transfers between devices: 138 us -> 133 us  [hop(): return lax.ppermute(array, BATCH, pairs)]
    ppermute x46 -> x47, starting transfers between devices: 58.8 us -> 59.8 us  [hop(): return lax.ppermute(array, BATCH, pairs)]
  transfers between devices with their start and end apart: 72 -> 73, of which waited for: 29 -> 30; matrix products, arithmetic and copies ran while one was open for 4% -> 4% of each run, Pallas kernels for 30% -> 31%
where the time goes in v4:
time: 533 us; the launch traced here: 524 us
  waiting for transfers between devices  239 us (45%)
  Pallas kernels  175 us (33%)
  starting transfers between devices  64 us (12%)
  local copies, waits for them, and re-layouts  25.4 us (5%)
  between operations  15.1 us (3%)
    pallas_call x18, Pallas kernels, call(): pl.pallas_call(kernel, grid_spec=pltpu.PrefetchScalarGridSpec(num_scalar_...  173 us
    ppermute x47, waiting for transfers between devices, hop(): return lax.ppermute(array, BATCH, pairs)  133 us
    all_gather x5, waiting for transfers between devices, gather_cols(): return lax.all_gather(array, TENSOR, axis=1, tiled=True)  83 us
    ppermute x47, starting transfers between devices, hop(): return lax.ppermute(array, BATCH, pairs)  59.8 us
    reduce_scatter x5, waiting for transfers between devices, scatter_cols(): return lax.psum_scatter(array, TENSOR, scatter_dimension=1, tiled=True)  17.8 us
  transfers between devices with their start and end apart: 73, of which 30 were waited for; matrix products, arithmetic and copies ran while one was open for 4% of the time, Pallas kernels for 31%

profile of v4, /device:TPU:0, one launch (start us, length us, event | category | flops | bytes accessed | tf_op | source)
XLA Modules:
  0.0 523.9 jit_solution(3891953919639200977)
XLA Ops:
  10.3 68.4 %all-gather.6.cloned.1.call-done.zero.vec.refs_0_.refs_1_.seed.g3.refs_5_.refs_6_.own = bf16[1552,2048]{1,0:T(8,128)(2,1)} async-done(((bf16[1552,256]{1,0:T(8,128)(2,1)}), bf16[1552,2048]{1,0:T(8,128)(2,1)}) %all-gather.6.cloned.1.call-update) | async-done | bytes 6357008 | tf_op jit(solution)/shard_map/all_gather | solution.py:56
  78.6 9.6 %self_forward.1 = (bf16[512,2048]{1,0:T(8,128)(2,1)}, bf16[512,256]{1,0:T(8,128)(2,1)}, bf16[512,256]{1,0:T(8,128)(2,1)}, bf16[512,256]{1,0:T(8,128)(2,1)}, bf16...) custom-call(s32[2]{0:T(128)} %pad_add_fusion.place, ...), custom_call_target="tpu_custom_call" | custom-call | flops 1000 | bytes 17001000 | tf_op jit(solution)/shard_map/self_forward/pallas_call | solution.py:157
  94.0 5.0 text_project.1
  99.1 17.3 %collective-permute-done.refs_0_ = bf16[256,2048]{1,0:T(8,128)(2,1)S(1)} collective-permute-done((bf16[256,2048]{1,0:T(8,128)(2,1)S(1)}, bf16[256,2048]{1,0:T(8,128)(2,1)S(1)}, u32[]{:S(2)}, u32[]{:S(2)}) %collective-permute-start) | collective-permute-done | bytes 1048608 | tf_op jit(solution)/shard_map/ppermute | solution.py:69
  117.7 4.6 reduce-scatter.6.cloned.1.call-done
  129.3 19.3 %collective-permute-done.2.refs_1_ = bf16[256,2048]{1,0:T(8,128)(2,1)S(1)} collective-permute-done((bf16[256,2048]{1,0:T(8,128)(2,1)S(1)}, bf16[256,2048]{1,0:T(8,128)(2,1)S(1)}, u32[]{:S(2)}, u32[]{:S(2)}) %collective-permute-start.2) | collective-permute-done | bytes 1048608 | tf_op jit(solution)/shard_map/ppermute | solution.py:69
  150.0 3.5 all-gather.8.cloned.1.call-done.add
  153.5 9.1 %cross_forward.1 = (bf16[512,2048]{1,0:T(8,128)(2,1)}, bf16[512,2048]{1,0:T(8,128)(2,1)}, bf16[512,256]{1,0:T(8,128)(2,1)}, bf16[512,256]{1,0:T(8,128)(2,1)}, bf...) custom-call(s32[2]{0:T(128)} %pad_add_fusion.place, ...), custom_call_target="tpu_custom_call" | custom-call | flops 1000 | bytes 1000 | tf_op jit(solution)/shard_map/cross_forward/pallas_call | solution.py:157
  167.9 9.9 %collective-permute-done.10.refs_5_ = bf16[128,2048]{1,0:T(8,128)(2,1)S(1)} collective-permute-done((bf16[128,2048]{1,0:T(8,128)(2,1)S(1)}, bf16[128,2048]{1,0:T(8,128)(2,1)S(1)}, u32[]{:S(2)}, u32[]{:S(2)}) %collective-permute-start.10) | collective-permute-done | bytes 524320 | tf_op jit(solution)/shard_map/ppermute | solution.py:69
  179.3 6.8 %seed_product.1.dact = f32[512,1024]{1,0:T(8,128)} custom-call(s32[2]{0:T(128)} %pad_add_fusion.place, bf16[1552,2048]{1,0:T(8,128)(2,1)} %all-gather.6.cloned.1.call-done.zero.vec.refs_0_.refs_1_.seed.g3.refs_5_.refs_6_.own, bf16[1024,2048]{1,0:T(8,128)(2,1)} %down.3), custom_call_target="tpu_custom_call" | custom-call | flops 1000 | bytes 3001000 | tf_op jit(solution)/shard_map/seed_product/pallas_call | solution.py:157
  188.5 9.1 %reduce-scatter.8.cloned.1.call-done = bf16[512,256]{1,0:T(8,128)(2,1)} async-done(((bf16[512,2048]{1,0:T(8,128)(2,1)}), bf16[512,256]{1,0:T(8,128)(2,1)}) %reduce-scatter.8.cloned.1.call-update) | async-done | bytes 262160 | tf_op jit(solution)/shard_map/reduce_scatter | solution.py:60
  200.8 19.8 %collective-permute-done.16.refs_7_ = bf16[256,2048]{1,0:T(8,128)(2,1)} collective-permute-done((bf16[256,2048]{1,0:T(8,128)(2,1)}, bf16[256,2048]{1,0:T(8,128)(2,1)}, u32[]{:S(2)}, u32[]{:S(2)}) %collective-permute-start.16) | collective-permute-done | bytes 1048608 | tf_op jit(solution)/shard_map/ppermute | solution.py:69
  228.5 12.6 %feed_both.1 = (f32[512,256]{1,0:T(8,128)}, f32[512,1]{1,0:T(8,128)}, bf16[512,2048]{1,0:T(8,128)(2,1)}, bf16[512,1024]{1,0:T(8,128)(2,1)}, bf16[512,1024]{1,0:T(8,128)(2,1)}, /*index=5*/bf16[512,2048]{1,0:T(8,128)(2,1)}) custom-call(s32[2]{0:T(128)} %pad_add_fusion.place, bf16[512,2048]{1,0:T(8,128)(2,1)} %get-tuple-element.190.one, ...), custom_call_target="tpu_custom_call" | custom-call | flops 1000 | bytes 6001000 | tf_op jit(solution)/shard_map/feed_both/pallas_call | solution.py:157
  242.8 3.6 collective-permute-done.22.refs_13_
  249.9 22.6 %collective-permute-done.24.refs_1_ = bf16[256,2048]{1,0:T(8,128)(2,1)S(1)} collective-permute-done((bf16[256,2048]{1,0:T(8,128)(2,1)S(1)}, bf16[256,2048]{1,0:T(8,128)(2,1)S(1)}, u32[]{:S(2)}, u32[]{:S(2)}) %collective-permute-start.24) | collective-permute-done | bytes 1048608 | tf_op jit(solution)/shard_map/ppermute | solution.py:69
  279.2 8.1 %collective-permute-done.26.refs_5_ = bf16[128,2048]{1,0:T(8,128)(2,1)S(1)} collective-permute-done((bf16[128,2048]{1,0:T(8,128)(2,1)S(1)}, bf16[128,2048]{1,0:T(8,128)(2,1)S(1)}, u32[]{:S(2)}, u32[]{:S(2)}) %collective-permute-start.26) | collective-permute-done | bytes 524320 | tf_op jit(solution)/shard_map/ppermute | solution.py:69
  290.7 6.6 %out_product.1.room = bf16[1024,2048]{1,0:T(8,128)(2,1)} custom-call(s32[2]{0:T(128)} %pad_add_fusion.place, bf16[512,1024]{1,0:T(8,128)(2,1)} %get-tuple-element.216.act.refs_0_, bf16[1024,2048]{1,0:T(8,128)(2,1)} %down.3), custom_call_target="tpu_custom_call" | custom-call | flops 1000 | bytes 15001000 | tf_op jit(solution)/shard_map/out_product/pallas_call | solution.py:157
  299.1 8.2 %all-gather.12.cloned.1.call-done.dn = bf16[512,2048]{1,0:T(8,128)(2,1)} async-done(((bf16[512,256]{1,0:T(8,128)(2,1)}), bf16[512,2048]{1,0:T(8,128)(2,1)}) %all-gather.12.cloned.1.call-update) | async-done | bytes 2097168 | tf_op jit(solution)/shard_map/all_gather | solution.py:56
  307.2 11.3 %cross_backward.1 = (bf16[512,2048]{1,0:T(8,128)(2,1)}, bf16[512,256]{1,0:T(8,128)(2,1)}, bf16[256,512]{1,0:T(8,128)(2,1)}, bf16[1024,2048]{1,0:T(8,128)(2,1)}, f32[1,2048]{1,0:T(1,128)}) custom-call(s32[2]{0:T(128)} %pad_add_fusion.place, bf16[512,2048]{1,0:T(8,128)(2,1)} %get-tuple-element.204.three.refs_0_, ...), custom_call_target="tpu_custom_call", output_to_operand_aliasing={{3}: (11, {})} | custom-call | flops 1000 | bytes 20001000 | tf_op jit(solution)/shard_map/cross_backward/pallas_call | solution.py:157
  323.7 10.3 %collective-permute-done.34.refs_3_ = bf16[256,1024]{1,0:T(8,128)(2,1)S(1)} collective-permute-done((bf16[256,1024]{1,0:T(8,128)(2,1)S(1)}, bf16[256,1024]{1,0:T(8,128)(2,1)S(1)}, u32[]{:S(2)}, u32[]{:S(2)}) %collective-permute-start.34) | collective-permute-done | bytes 524320 | tf_op jit(solution)/shard_map/ppermute | solution.py:69
  338.0 4.8 text_back.1.room
  342.9 5.7 %cross_parts.1 = (bf16[128,2048]{1,0:T(8,128)(2,1)}, bf16[128,2048]{1,0:T(8,128)(2,1)}, bf16[128,2048]{1,0:T(8,128)(2,1)}, bf16[128,2048]{1,0:T(8,128)(2,1)}) custom-call(s32[2]{0:T(128)} %pad_add_fusion.place, bf16[512,256]{1,0:T(8,128)(2,1)} %get-tuple-element.234.refs_0_, bf16[512,2048]{1,0:T(8,128)(2,1)} %get-tuple-element.235.refs_1_.g2, ...), custom_call_target="tpu_custom_call" | custom-call | flops 1000 | bytes 1000 | tf_op jit(solution)/shard_map/cross_parts/pallas_call | solution.py:157
  348.6 17.7 %down_grads.1 = f32[1024,2048]{1,0:T(8,128)} custom-call(s32[2]{0:T(128)} %pad_add_fusion.place, bf16[512,1024]{1,0:T(8,128)(2,1)} %get-tuple-element.216.act.refs_0_, bf16[512,1024]{1,0:T(8,128)(2,1)} %collective-permute-done.32.refs_1_, bf16[512,1024]{1,0:T(8,128)(2,1)} %collective-permute-done.33.refs_2_, bf16[256,1024]{1,0:T(8,128)(2,1)} %copy-done.31, ...), custom_call_target="tpu_custom_call" | custom-call | flops 1000 | bytes 1000 | tf_op jit(solution)/shard_map/down_grads/pallas_call | solution.py:157
  380.3 4.9 collective-permute-done.39.refs_10_
  387.1 21.3 %text_grads.1 = (f32[8,2,256,256]{3,2,1,0:T(8,128)}, f32[8,2,256,256]{3,2,1,0:T(8,128)}) custom-call(s32[2]{0:T(128)} %pad_add_fusion.place, bf16[1552,2048]{1,0:T(8,128)(2,1)} %all-gather.6.cloned.1.call-done.zero.vec.refs_0_.refs_1_.seed.g3.refs_5_.refs_6_.own, bf16[256,2048]{1,0:T(8,128)(2,1)} %copy-done.9, bf16[256,2048]{1,0:T(8,128)(2,1)} %copy-done.21, ...), custom_call_target="tpu_custom_call" | custom-call | flops 1000 | bytes 15001000 | tf_op jit(solution)/shard_map/text_grads/pallas_call | solution.py:157
  408.5 16.3 %self_backward.1 = (f32[512,256]{1,0:T(8,128)}, bf16[512,2048]{1,0:T(8,128)(2,1)}, bf16[512,768]{1,0:T(8,128)(2,1)}, bf16[1056,2048]{1,0:T(8,128)(2,1)}, f32[1,2048]{1,0:T(1,128)}) custom-call(s32[2]{0:T(128)} %pad_add_fusion.place, bf16[512,2048]{1,0:T(8,128)(2,1)} %get-tuple-element.186.one.refs_0_, ...), custom_call_target="tpu_custom_call", output_to_operand_aliasing={{3}: (14, {})} | custom-call | flops 1000 | bytes 27001000 | tf_op jit(solution)/shard_map/self_backward/pallas_call | solution.py:157
  434.1 4.1 self_parts.1
  438.2 16.8 %up_grads.1 = f32[2048,1024]{1,0:T(8,128)} custom-call(s32[2]{0:T(128)} %pad_add_fusion.place, bf16[512,2048]{1,0:T(8,128)(2,1)} %get-tuple-element.204.three.refs_0_, bf16[256,2048]{1,0:T(8,128)(2,1)} %copy-done.5, bf16[256,2048]{1,0:T(8,128)(2,1)} %copy-done.16, bf16[256,2048]{1,0:T(8,128)(2,1)} %copy-done.6, ...), custom_call_target="tpu_custom_call" | custom-call | flops 1000 | bytes 14001000 | tf_op jit(solution)/shard_map/up_grads/pallas_call | solution.py:157
  455.1 5.2 collective-permute-done.47.refs_11_
  462.4 13.7 %self_grads.1 = (f32[2048,256]{1,0:T(8,128)}, f32[2048,256]{1,0:T(8,128)}, f32[2048,256]{1,0:T(8,128)}) custom-call(s32[2]{0:T(128)} %pad_add_fusion.place, bf16[512,2048]{1,0:T(8,128)(2,1)} %get-tuple-element.186.one.refs_0_, bf16[256,2048]{1,0:T(8,128)(2,1)} %copy-done.3, bf16[256,2048]{1,0:T(8,128)(2,1)} %copy-done.14, bf16[256,2048]{1,0:T(8,128)(2,1)} %copy-done.4, ...), custom_call_target="tpu_custom_call" | custom-call | flops 1000 | bytes 40001000 | tf_op jit(solution)/shard_map/self_grads/pallas_call | solution.py:157
  480.4 3.7 self_end.1
  507.8 4.4 cross_finish.1
  (281 shorter events, 124.7 us)
Async XLA Ops:
  7.2 71.4 %all-gather.6.cloned.1.call-start = ((), (), s32[]{:S(2)}) async-start(), calls=%async_computation.5 | async-start | bytes 7151616 | tf_op jit(solution)/shard_map/all_gather | solution.py:56
  9.7 112.6 %reduce-scatter.6.cloned.1.call-start = ((), (), s32[]{:S(2)}) async-start(), calls=%async_computation.6 | async-start | bytes 2359296 | tf_op jit(solution)/shard_map/reduce_scatter | solution.py:60
  88.3 65.3 %all-gather.8.cloned.1.call-start = ((), (), s32[]{:S(2)}) async-start(), calls=%async_computation.7 | async-start | bytes 2359296 | tf_op jit(solution)/shard_map/all_gather | solution.py:56
  91.1 25.3 %collective-permute-start = (bf16[256,2048]{1,0:T(8,128)(2,1)S(1)}, bf16[256,2048]{1,0:T(8,128)(2,1)S(1)}, u32[]{:S(2)}, u32[]{:S(2)}) collective-permute-start(bf16[256,2048]{1,0:T(8,128)(2,1)S(1)} %get-tuple-element.345), channel_id=1, source_target_pairs={{0,8},{8,0},{16,24},{24,16},{1,9},{9,1},{17,25},{25,17},{2,10},{10... | collective-permute-start | bytes 3145736 | tf_op jit(solution)/shard_map/ppermute | solution.py:69
  92.6 25.1 %collective-permute-start.1 = (bf16[256,2048]{1,0:T(8,128)(2,1)S(1)}, bf16[256,2048]{1,0:T(8,128)(2,1)}, u32[]{:S(2)}, u32[]{:S(2)}) collective-permute-start(bf16[256,2048]{1,0:T(8,128)(2,1)S(1)} %get-tuple-element.345), channel_id=1, source_target_pairs={{0,16},{8,24},{16,0},{24,8},{1,17},{9,25},{17,1},{25,9},{2,18},{10... | collective-permute-start | bytes 3145736 | tf_op jit(solution)/shard_map/ppermute | solution.py:69
  122.3 75.3 %reduce-scatter.8.cloned.1.call-start = ((), (), s32[]{:S(2)}) async-start(), calls=%async_computation.8 | async-start | bytes 2359296 | tf_op jit(solution)/shard_map/reduce_scatter | solution.py:60
  122.5 26.2 %collective-permute-start.2 = (bf16[256,2048]{1,0:T(8,128)(2,1)S(1)}, bf16[256,2048]{1,0:T(8,128)(2,1)S(1)}, u32[]{:S(2)}, u32[]{:S(2)}) collective-permute-start(bf16[256,2048]{1,0:T(8,128)(2,1)S(1)} %slice.81), channel_id=1, source_target_pairs={{0,8},{8,0},{16,24},{24,16},{1,9},{9,1},{17,25},{25,17},{2,10},{10... | collective-permute-start | bytes 3145736 | tf_op jit(solution)/shard_map/ppermute | solution.py:69
  123.9 26.1 %collective-permute-start.3 = (bf16[256,2048]{1,0:T(8,128)(2,1)S(1)}, bf16[256,2048]{1,0:T(8,128)(2,1)S(1)}, u32[]{:S(2)}, u32[]{:S(2)}) collective-permute-start(bf16[256,2048]{1,0:T(8,128)(2,1)S(1)} %slice.81), channel_id=1, source_target_pairs={{0,16},{8,24},{16,0},{24,8},{1,17},{9,25},{17,1},{25,9},{2,18},{10... | collective-permute-start | bytes 3145736 | tf_op jit(solution)/shard_map/ppermute | solution.py:69
  126.2 36.4 %collective-permute-start.4 = (bf16[128,2048]{1,0:T(8,128)(2,1)}, bf16[128,2048]{1,0:T(8,128)(2,1)}, u32[]{:S(2)}, u32[]{:S(2)}) collective-permute-start(bf16[128,2048]{1,0:T(8,128)(2,1)} %slice.82), channel_id=1, source_target_pairs={{0,16},{8,24},{16,0},{24,8},{1,17},{9,25},{17,1},{25,9},{2,18},{10... | collective-permute-start | bytes 1572872 | tf_op jit(solution)/shard_map/ppermute | solution.py:69
  128.7 33.9 %collective-permute-start.5 = (bf16[128,2048]{1,0:T(8,128)(2,1)}, bf16[128,2048]{1,0:T(8,128)(2,1)}, u32[]{:S(2)}, u32[]{:S(2)}) collective-permute-start(bf16[128,2048]{1,0:T(8,128)(2,1)} %slice.83), channel_id=1, source_target_pairs={{0,8},{8,0},{16,24},{24,16},{1,9},{9,1},{17,25},{25,17},{2,10},{10... | collective-permute-start | bytes 1572872 | tf_op jit(solution)/shard_map/ppermute | solution.py:69
  162.6 65.8 %all-gather.10.cloned.1.call-start = ((), (), s32[]{:S(2)}) async-start(), calls=%async_computation.9 | async-start | bytes 2359296 | tf_op jit(solution)/shard_map/all_gather | solution.py:56
  197.6 78.5 %reduce-scatter.10.cloned.1.call-start = ((), (), s32[]{:S(2)}) async-start(), calls=%async_computation.10 | async-start | bytes 2359296 | tf_op jit(solution)/shard_map/reduce_scatter | solution.py:60
  241.1 66.1 %all-gather.12.cloned.1.call-start = ((), (), s32[]{:S(2)}) async-start(), calls=%async_computation.11 | async-start | bytes 2359296 | tf_op jit(solution)/shard_map/all_gather | solution.py:56
  247.1 25.4 %collective-permute-start.24 = (bf16[256,2048]{1,0:T(8,128)(2,1)S(1)}, bf16[256,2048]{1,0:T(8,128)(2,1)S(1)}, u32[]{:S(2)}, u32[]{:S(2)}) collective-permute-start(bf16[256,2048]{1,0:T(8,128)(2,1)S(1)} %slice.88), channel_id=1, source_target_pairs={{0,8},{8,0},{16,24},{24,16},{1,9},{9,1},{17,25},{25,17},{2,10},{10... | collective-permute-start | bytes 3145736 | tf_op jit(solution)/shard_map/ppermute | solution.py:69
  248.4 25.0 %collective-permute-start.25 = (bf16[256,2048]{1,0:T(8,128)(2,1)S(1)}, bf16[256,2048]{1,0:T(8,128)(2,1)S(1)}, u32[]{:S(2)}, u32[]{:S(2)}) collective-permute-start(bf16[256,2048]{1,0:T(8,128)(2,1)S(1)} %slice.88), channel_id=1, source_target_pairs={{0,16},{8,24},{16,0},{24,8},{1,17},{9,25},{17,1},{25,9},{2,18},{10... | collective-permute-start | bytes 3145736 | tf_op jit(solution)/shard_map/ppermute | solution.py:69
  276.1 91.7 %reduce-scatter.12.cloned.1.call-start = ((), (), s32[]{:S(2)}) async-start(), calls=%async_computation.12 | async-start | bytes 4718592 | tf_op jit(solution)/shard_map/reduce_scatter | solution.py:60
  287.8 30.7 %collective-permute-start.32 = (bf16[512,1024]{1,0:T(8,128)(2,1)S(1)}, bf16[512,1024]{1,0:T(8,128)(2,1)}, u32[]{:S(2)}, u32[]{:S(2)}) collective-permute-start(bf16[512,1024]{1,0:T(8,128)(2,1)S(1)} %copy-done.2), channel_id=1, source_target_pairs={{0,8},{8,0},{16,24},{24,16},{1,9},{9,1},{17,25},{25,17},{2,10},{10... | collective-permute-start | bytes 3145736 | tf_op jit(solution)/shard_map/ppermute | solution.py:69
  289.1 29.4 %collective-permute-start.33 = (bf16[512,1024]{1,0:T(8,128)(2,1)S(1)}, bf16[512,1024]{1,0:T(8,128)(2,1)}, u32[]{:S(2)}, u32[]{:S(2)}) collective-permute-start(bf16[512,1024]{1,0:T(8,128)(2,1)S(1)} %copy-done.2), channel_id=1, source_target_pairs={{0,16},{8,24},{16,0},{24,8},{1,17},{9,25},{17,1},{25,9},{2,18},{10... | collective-permute-start | bytes 3145736 | tf_op jit(solution)/shard_map/ppermute | solution.py:69
  318.6 89.9 %all-gather.14.cloned.1.call-start = ((), (), s32[]{:S(2)}) async-start(), calls=%async_computation.13 | async-start | bytes 2359296 | tf_op jit(solution)/shard_map/all_gather | solution.py:56
  336.0 30.3 %collective-permute-start.36 = (bf16[512,1024]{1,0:T(8,128)(2,1)S(1)}, bf16[512,1024]{1,0:T(8,128)(2,1)S(1)}, u32[]{:S(2)}, u32[]{:S(2)}) collective-permute-start(bf16[512,1024]{1,0:T(8,128)(2,1)S(1)} %copy-done.15), channel_id=1, source_target_pairs={{0,8},{8,0},{16,24},{24,16},{1,9},{9,1},{17,25},{25,17},{2,10},{10... | collective-permute-start | bytes 3145736 | tf_op jit(solution)/shard_map/ppermute | solution.py:69
  337.5 28.8 %collective-permute-start.37 = (bf16[512,1024]{1,0:T(8,128)(2,1)S(1)}, bf16[512,1024]{1,0:T(8,128)(2,1)S(1)}, u32[]{:S(2)}, u32[]{:S(2)}) collective-permute-start(bf16[512,1024]{1,0:T(8,128)(2,1)S(1)} %copy-done.15), channel_id=1, source_target_pairs={{0,16},{8,24},{16,0},{24,8},{1,17},{9,25},{17,1},{25,9},{2,18},{10... | collective-permute-start | bytes 3145736 | tf_op jit(solution)/shard_map/ppermute | solution.py:69
  369.5 106.6 %reduce-scatter.14.cloned.1.call-start = ((), (), s32[]{:S(2)}) async-start(), calls=%async_computation.14 | async-start | bytes 4866048 | tf_op jit(solution)/shard_map/reduce_scatter | solution.py:60
  374.8 49.9 %collective-permute-start.41 = (bf16[256,1024]{1,0:T(8,128)(2,1)}, bf16[256,1024]{1,0:T(8,128)(2,1)S(1)}, u32[]{:S(2)}, u32[]{:S(2)}) collective-permute-start(bf16[256,1024]{1,0:T(8,128)(2,1)} %slice.95), channel_id=1, source_target_pairs={{0,16},{8,24},{16,0},{24,8},{1,17},{9,25},{17,1},{25,9},{2,18},{10... | collective-permute-start | bytes 1572872 | tf_op jit(solution)/shard_map/ppermute | solution.py:69
  376.3 48.5 %collective-permute-start.42 = (bf16[256,1024]{1,0:T(8,128)(2,1)}, bf16[256,1024]{1,0:T(8,128)(2,1)}, u32[]{:S(2)}, u32[]{:S(2)}) collective-permute-start(bf16[256,1024]{1,0:T(8,128)(2,1)} %slice.96), channel_id=1, source_target_pairs={{0,8},{8,0},{16,24},{24,16},{1,9},{9,1},{17,25},{25,17},{2,10},{10... | collective-permute-start | bytes 1572872 | tf_op jit(solution)/shard_map/ppermute | solution.py:69
  378.9 45.9 %collective-permute-start.43 = (bf16[128,2048]{1,0:T(8,128)(2,1)}, bf16[128,2048]{1,0:T(8,128)(2,1)}, u32[]{:S(2)}, u32[]{:S(2)}) collective-permute-start(bf16[128,2048]{1,0:T(8,128)(2,1)} %get-tuple-element.267), channel_id=1, source_target_pairs={{0,8},{8,0},{16,24},{24,16},{1,9},{9,1},{17,25},{25,17},{2,10},{10... | collective-permute-start | bytes 1572872 | tf_op jit(solution)/shard_map/ppermute | solution.py:69
  385.2 39.5 %collective-permute-start.44 = (bf16[128,2048]{1,0:T(8,128)(2,1)}, bf16[128,2048]{1,0:T(8,128)(2,1)}, u32[]{:S(2)}, u32[]{:S(2)}) collective-permute-start(bf16[128,2048]{1,0:T(8,128)(2,1)} %get-tuple-element.268), channel_id=1, source_target_pairs={{0,16},{8,24},{16,0},{24,8},{1,17},{9,25},{17,1},{25,9},{2,18},{10... | collective-permute-start | bytes 1572872 | tf_op jit(solution)/shard_map/ppermute | solution.py:69
  386.4 38.4 %collective-permute-start.45 = (bf16[128,2048]{1,0:T(8,128)(2,1)}, bf16[128,2048]{1,0:T(8,128)(2,1)S(1)}, u32[]{:S(2)}, u32[]{:S(2)}) collective-permute-start(bf16[128,2048]{1,0:T(8,128)(2,1)} %get-tuple-element.269), channel_id=1, source_target_pairs={{0,24},{8,16},{16,8},{24,0},{1,25},{9,17},{17,9},{25,1},{2,26},{10... | collective-permute-start | bytes 1572872 | tf_op jit(solution)/shard_map/ppermute | solution.py:69
  426.1 29.0 %collective-permute-start.46 = (bf16[512,768]{1,0:T(8,128)(2,1)S(1)}, bf16[512,768]{1,0:T(8,128)(2,1)S(1)}, u32[]{:S(2)}, u32[]{:S(2)}) collective-permute-start(bf16[512,768]{1,0:T(8,128)(2,1)S(1)} %copy-done.23), channel_id=1, source_target_pairs={{0,8},{8,0},{16,24},{24,16},{1,9},{9,1},{17,25},{25,17},{2,10},{10... | collective-permute-start | bytes 2359304 | tf_op jit(solution)/shard_map/ppermute | solution.py:69
  427.6 32.6 %collective-permute-start.47 = (bf16[512,768]{1,0:T(8,128)(2,1)S(1)}, bf16[512,768]{1,0:T(8,128)(2,1)S(1)}, u32[]{:S(2)}, u32[]{:S(2)}) collective-permute-start(bf16[512,768]{1,0:T(8,128)(2,1)S(1)} %copy-done.23), channel_id=1, source_target_pairs={{0,16},{8,24},{16,0},{24,8},{1,17},{9,25},{17,1},{25,9},{2,18},{10... | collective-permute-start | bytes 2359304 | tf_op jit(solution)/shard_map/ppermute | solution.py:69
  428.9 32.7 %collective-permute-start.48 = (bf16[512,768]{1,0:T(8,128)(2,1)S(1)}, bf16[512,768]{1,0:T(8,128)(2,1)S(1)}, u32[]{:S(2)}, u32[]{:S(2)}) collective-permute-start(bf16[512,768]{1,0:T(8,128)(2,1)S(1)} %copy-done.23), channel_id=1, source_target_pairs={{0,24},{8,16},{16,8},{24,0},{1,25},{9,17},{17,9},{25,1},{2,26},{10... | collective-permute-start | bytes 2359304 | tf_op jit(solution)/shard_map/ppermute | solution.py:69
  431.1 53.0 %collective-permute-start.49 = (bf16[128,2048]{1,0:T(8,128)(2,1)S(1)}, bf16[128,2048]{1,0:T(8,128)(2,1)S(1)}, u32[]{:S(2)}, u32[]{:S(2)}) collective-permute-start(bf16[128,2048]{1,0:T(8,128)(2,1)S(1)} %add_convert_fusion.refs_0_), channel_id=1, source_target_pairs={{0,8},{8,0},{16,24},{24,16},{1,9},{9,1},{17,25},{25,17},{2,10},{10... | collective-permute-start | bytes 1572872 | tf_op jit(solution)/shard_map/ppermute | solution.py:69
  432.8 51.3 %collective-permute-start.50 = (bf16[128,2048]{1,0:T(8,128)(2,1)S(1)}, bf16[128,2048]{1,0:T(8,128)(2,1)S(1)}, u32[]{:S(2)}, u32[]{:S(2)}) collective-permute-start(bf16[128,2048]{1,0:T(8,128)(2,1)S(1)} %add_convert_fusion.refs_0_), channel_id=1, source_target_pairs={{0,16},{8,24},{16,0},{24,8},{1,17},{9,25},{17,1},{25,9},{2,18},{10... | collective-permute-start | bytes 1572872 | tf_op jit(solution)/shard_map/ppermute | solution.py:69
  (95 other events, 1182.5 us)
Sparse Core Ops, SparseCore 0:
  10.2 68.4 all-gather.5
  88.4 33.8 reduce-scatter.5
  123.9 29.6 all-gather.7
  162.8 34.7 reduce-scatter.7
  199.0 29.3 all-gather.9
  241.2 34.8 reduce-scatter.9
  277.7 29.5 all-gather.11
  318.7 49.0 reduce-scatter.11
  370.0 28.9 all-gather.13
  424.9 49.8 reduce-scatter.13
